TPU v7x, 32 devices: a whole 2x2x4 slice. The times are simulated.
32 devices in a mesh: ctx: 8 (over y, x, core), wsh: 4 (over z).
Axes of the slice: x: 2, y: 2, z: 4, core: 2. Of those that a mesh axis runs over, the one named last changes fastest.
Arguments:
- tokens: bfloat16 [4, 2048, 1280], P('wsh', 'ctx'), may hold values from -6 to 6
- cotangent: bfloat16 [4, 2048, 1280], P('wsh', 'ctx'), may hold values from -6 to 6
- block_lengths: int32 [4, 8], P('wsh'), may hold values from 1 to 512, 2048 in all within a row
- group_order: int32 [8], replicated, may hold values from 0 to 7, each once
- w_query: bfloat16 [1280, 1280], P('wsh'), may hold values from -0.15625 to 0.15625
- w_key: bfloat16 [1280, 1280], P('wsh'), may hold values from -0.15625 to 0.15625
- w_value: bfloat16 [1280, 1280], P('wsh'), may hold values from -0.15625 to 0.15625
- w_out: bfloat16 [1280, 1280], P('wsh'), may hold values from -1 to 1
- w_up: bfloat16 [1280, 1280], P('wsh'), may hold values from -0.15625 to 0.15625
- w_down: bfloat16 [1280, 1280], P('wsh'), may hold values from -0.15625 to 0.15625
- gain_attn: bfloat16 [1280], P('wsh'), may hold values from 0.099609375 to 1.8984375
- gain_mlp: bfloat16 [1280], P('wsh'), may hold values from 0.099609375 to 1.8984375
- query_scale: bfloat16 [80], P('wsh'), may hold values from -3 to 3
Outputs:
- output: bfloat16 [4, 2048, 1280], P('wsh', 'ctx')
- grad_tokens: bfloat16 [4, 2048, 1280], P('wsh', 'ctx')
- grad_w_query: float32 [1280, 1280], P('wsh')
- grad_w_key: float32 [1280, 1280], P('wsh')
- grad_w_value: float32 [1280, 1280], P('wsh')
- grad_w_out: float32 [1280, 1280], P('wsh')
- grad_w_up: float32 [1280, 1280], P('wsh')
- grad_w_down: float32 [1280, 1280], P('wsh')
- grad_gain_attn: float32 [1280], P('wsh')
- grad_gain_mlp: float32 [1280], P('wsh')
- grad_query_scale: float32 [80], P('wsh')
Inputs may be any that keep to these rules, and one draw needn't show every extreme that they name: `block_lengths`: each row sums to 2048; its largest entry is exactly 512. `group_order`: A permutation of the stored groups.
All inputs are finite; a program needn't handle non-finite values.
Results may differ from a plain program's by a relative error of at most 0.023.
Values may be sent and summed in bfloat16 or wider, within the bound.
A program may use at most 384 MiB of HBM per device.

v0:
```python
import math

import jax
import jax.numpy as jnp
from jax import lax
from jax.sharding import PartitionSpec as P

H = 16


EPS = 1e-06
LOG_BASE = 1.442695041


def row_step():
    return 512


def rows_at(array, block_no, step_rows):
    return lax.dynamic_slice_in_dim(array, block_no * step_rows, step_rows, 0)


def inverse_rms(values):
    return lax.rsqrt(jnp.mean(values * values, -1, keepdims=True) + EPS)


def norm_back(normed, inverse, grad):
    return inverse * (grad - normed * jnp.mean(grad * normed, -1, keepdims=True))


def split_heads(matrix):
    return matrix.reshape(matrix.shape[0], H, -1)


def outer_product(left, right):
    return lax.dot_general(
        left, right, (((0,), (0,)), ((), ())), preferred_element_type=jnp.float32
    )


def back_product(grad, weight):
    return lax.dot_general(
        grad, weight, (((1,), (1,)), ((), ())), preferred_element_type=jnp.float32
    )


def probabilities(query3, key3, query_marks, key_marks, log_totals):
    scores = jnp.einsum("qhd,khd->hqk", query3, key3, preferred_element_type=jnp.float32)
    allowed = key_marks[None, None, :] <= query_marks[None, :, None]
    return jnp.exp(jnp.where(allowed, scores - log_totals[:, :, None], -jnp.inf))


def score_grads(chances, grad_out3, value3, deltas):
    grad_chances = jnp.einsum("qhd,khd->hqk", grad_out3, value3, preferred_element_type=jnp.float32)
    return (chances * (grad_chances - deltas[:, :, None])).astype(jnp.bfloat16)


def per_device(
    tokens,
    cotangent,
    block_lengths,
    group_order,
    w_query,
    w_key,
    w_value,
    w_out,
    w_up,
    w_down,
    gain_attn,
    gain_mlp,
    query_scale,
):
    gathered = (
        lax.all_gather(w_query, "wsh", axis=0, tiled=True),
        lax.all_gather(w_key, "wsh", axis=0, tiled=True),
        lax.all_gather(w_value, "wsh", axis=0, tiled=True),
        lax.all_gather(w_out, "wsh", axis=0, tiled=True),
        lax.all_gather(w_up, "wsh", axis=0, tiled=True),
        lax.all_gather(w_down, "wsh", axis=0, tiled=True),
        lax.all_gather(gain_attn, "wsh", axis=0, tiled=True),
        lax.all_gather(gain_mlp, "wsh", axis=0, tiled=True),
        lax.all_gather(query_scale, "wsh", axis=0, tiled=True),
    )
    (
        full_query,
        full_key,
        full_value,
        full_out,
        full_up,
        full_down,
        norm_attn,
        norm_mlp,
        scale_param,
    ) = gathered
    tok_rows = tokens.shape[1]
    model_width = tokens.shape[2]
    length = tok_rows * lax.axis_size("ctx")
    device = lax.axis_index("ctx")
    head_size = scale_param.shape[0]
    f32 = jnp.float32
    bf16 = jnp.bfloat16
    inputs = tokens.reshape(tok_rows, model_width).astype(f32)
    positions = (
        group_order[:, None] * tok_rows + jnp.arange(tok_rows, dtype=jnp.int32)[None, :]
    ).reshape(length)
    bounds = jnp.cumsum(block_lengths[0])
    block_ids = jnp.sum((bounds[None, :] <= positions[:, None]).astype(jnp.int32), -1)
    query_ids = lax.dynamic_slice_in_dim(block_ids, device * tok_rows, tok_rows, 0)
    inverse_one = inverse_rms(inputs)
    normed_one = inputs * inverse_one
    hidden_one = (normed_one * norm_attn.astype(f32)).astype(bf16)
    query_raw = jnp.dot(hidden_one, full_query, preferred_element_type=f32).reshape(
        tok_rows, H, head_size
    )
    query_gain = LOG_BASE / math.sqrt(head_size) * jax.nn.softplus(scale_param.astype(f32))
    query3 = (query_raw * query_gain).astype(bf16)
    key_flat = jnp.dot(hidden_one, full_key, preferred_element_type=f32).astype(bf16)
    value_flat = jnp.dot(hidden_one, full_value, preferred_element_type=f32).astype(bf16)
    initial = (
        jnp.full((H, tok_rows), -1e30, f32),
        jnp.zeros((H, tok_rows), f32),
        jnp.zeros((tok_rows, H, head_size), f32),
    )
    key_rows = lax.all_gather(key_flat, "ctx", axis=0, tiled=True)
    value_rows = lax.all_gather(value_flat, "ctx", axis=0, tiled=True)
    row_count = key_rows.shape[0]
    step_rows = row_step()

    def one_block(block_no, looped):
        key_part = split_heads(rows_at(key_rows, block_no, step_rows))
        value_part = split_heads(rows_at(value_rows, block_no, step_rows))
        block_marks = rows_at(block_ids, block_no, step_rows)
        maxima, totals, running = looped
        scores = jnp.einsum("qhd,khd->hqk", query3, key_part, preferred_element_type=f32)
        allowed = block_marks[None, None, :] <= query_ids[None, :, None]
        scores = jnp.where(allowed, scores, -jnp.inf)
        raised = jnp.maximum(maxima, jnp.max(scores, -1))
        rescale = jnp.exp(maxima - raised)
        weights = jnp.exp(scores - raised[:, :, None])
        totals = totals * rescale + jnp.sum(weights, -1)
        running = running * rescale.T[:, :, None] + jnp.einsum(
            "hqk,khd->qhd", weights.astype(bf16), value_part, preferred_element_type=f32
        )
        return (raised, totals, running)

    maxima, totals, running = lax.fori_loop(0, row_count // step_rows, one_block, initial)
    log_totals = maxima + jnp.log(totals)
    attended = running / totals.T[:, :, None]
    attended_bf = attended.reshape(tok_rows, model_width).astype(bf16)
    mixed = inputs + jnp.dot(attended_bf, full_out, preferred_element_type=f32)
    inverse_two = inverse_rms(mixed)
    normed_two = mixed * inverse_two
    hidden_two = (normed_two * norm_mlp.astype(f32)).astype(bf16)
    up_raw = jnp.dot(hidden_two, full_up, preferred_element_type=f32)
    active = jax.nn.silu(up_raw).astype(bf16)
    outputs = mixed + jnp.dot(active, full_down, preferred_element_type=f32)
    grad_output = cotangent.reshape(tok_rows, model_width).astype(f32)
    grad_mlp = grad_output.astype(bf16)
    grad_active = back_product(grad_mlp, full_down)
    sigmoid_up = jax.nn.sigmoid(up_raw)
    grad_up_raw = (grad_active * sigmoid_up * (1.0 + up_raw * (1.0 - sigmoid_up))).astype(bf16)
    grad_hidden_two = back_product(grad_up_raw, full_up)
    grad_gain_mlp = jnp.sum(grad_hidden_two * normed_two, 0)
    grad_mixed = grad_output + norm_back(
        normed_two, inverse_two, grad_hidden_two * norm_mlp.astype(f32)
    )
    grad_branch = grad_mixed.astype(bf16)
    grad_att = back_product(grad_branch, full_out).astype(bf16)
    grad_att3 = split_heads(grad_att)
    deltas = jnp.sum(grad_att3.astype(f32) * attended, -1).T
    key_whole, value_whole = (
        lax.all_gather(key_flat, "ctx", axis=0, tiled=True),
        lax.all_gather(value_flat, "ctx", axis=0, tiled=True),
    )
    step_rows = row_step()
    block_total = length // step_rows

    def key_block(grad_q, block_parts):
        key_rows, value_rows, block_marks = block_parts
        key_part = split_heads(key_rows)
        value_part = split_heads(value_rows)
        zero_part = jnp.zeros((key_rows.shape[0], H, head_size), f32)
        chances = probabilities(query3, key_part, query_ids, block_marks, log_totals)
        slopes = score_grads(chances, grad_att3, value_part, deltas)
        new_grad = (grad_q, zero_part, zero_part)[0] + jnp.einsum(
            "hqk,khd->qhd", slopes, key_part, preferred_element_type=f32
        )
        grad_key_part = jnp.einsum("hqk,qhd->khd", slopes, query3, preferred_element_type=f32)
        grad_value_part = jnp.einsum(
            "hqk,qhd->khd", chances.astype(bf16), grad_att3, preferred_element_type=f32
        )
        return (new_grad, (grad_key_part, grad_value_part))

    grad_qs, (key_terms, value_terms) = lax.scan(
        key_block,
        jnp.zeros((tok_rows, H, head_size), f32),
        (
            key_whole.reshape(block_total, step_rows, model_width),
            value_whole.reshape(block_total, step_rows, model_width),
            block_ids.reshape(block_total, step_rows),
        ),
    )
    grad_key, grad_value = (
        lax.psum_scatter(
            key_terms.reshape(length, model_width).astype(jnp.bfloat16),
            "ctx",
            scatter_dimension=0,
            tiled=True,
        ).astype(jnp.float32),
        lax.psum_scatter(
            value_terms.reshape(length, model_width).astype(jnp.bfloat16),
            "ctx",
            scatter_dimension=0,
            tiled=True,
        ).astype(jnp.float32),
    )
    grad_key_bf = grad_key.astype(bf16)
    grad_value_bf = grad_value.astype(bf16)
    grad_query_bf = (grad_qs * query_gain).reshape(tok_rows, model_width).astype(bf16)
    grad_scale_param = (
        jnp.sum(grad_qs * query_raw, (0, 1))
        * (LOG_BASE / math.sqrt(head_size))
        * jax.nn.sigmoid(scale_param.astype(f32))
    )
    grad_hidden_one = (
        back_product(grad_query_bf, full_query)
        + back_product(grad_key_bf, full_key)
        + back_product(grad_value_bf, full_value)
    )
    grad_gain_attn = jnp.sum(grad_hidden_one * normed_one, 0)
    grad_inputs = grad_mixed + norm_back(
        normed_one, inverse_one, grad_hidden_one * norm_attn.astype(f32)
    )
    grad_queryw = outer_product(hidden_one, grad_query_bf)
    grad_keyw = outer_product(hidden_one, grad_key_bf)
    grad_valuew = outer_product(hidden_one, grad_value_bf)
    grad_outw = outer_product(attended_bf, grad_branch)
    grad_upw = outer_product(hidden_two, grad_up_raw)
    grad_downw = outer_product(active, grad_mlp)
    owned = (
        lax.psum_scatter(
            grad_queryw.astype(jnp.bfloat16), "wsh", scatter_dimension=0, tiled=True
        ).astype(jnp.float32),
        lax.psum_scatter(
            grad_keyw.astype(jnp.bfloat16), "wsh", scatter_dimension=0, tiled=True
        ).astype(jnp.float32),
        lax.psum_scatter(
            grad_valuew.astype(jnp.bfloat16), "wsh", scatter_dimension=0, tiled=True
        ).astype(jnp.float32),
        lax.psum_scatter(
            grad_outw.astype(jnp.bfloat16), "wsh", scatter_dimension=0, tiled=True
        ).astype(jnp.float32),
        lax.psum_scatter(
            grad_upw.astype(jnp.bfloat16), "wsh", scatter_dimension=0, tiled=True
        ).astype(jnp.float32),
        lax.psum_scatter(
            grad_downw.astype(jnp.bfloat16), "wsh", scatter_dimension=0, tiled=True
        ).astype(jnp.float32),
        lax.psum_scatter(
            grad_gain_attn.astype(jnp.bfloat16), "wsh", scatter_dimension=0, tiled=True
        ).astype(jnp.float32),
        lax.psum_scatter(
            grad_gain_mlp.astype(jnp.bfloat16), "wsh", scatter_dimension=0, tiled=True
        ).astype(jnp.float32),
        lax.psum_scatter(
            grad_scale_param.astype(jnp.bfloat16), "wsh", scatter_dimension=0, tiled=True
        ).astype(jnp.float32),
    )
    summed = (
        lax.psum(owned[0].astype(jnp.bfloat16), "ctx").astype(jnp.float32),
        lax.psum(owned[1].astype(jnp.bfloat16), "ctx").astype(jnp.float32),
        lax.psum(owned[2].astype(jnp.bfloat16), "ctx").astype(jnp.float32),
        lax.psum(owned[3].astype(jnp.bfloat16), "ctx").astype(jnp.float32),
        lax.psum(owned[4].astype(jnp.bfloat16), "ctx").astype(jnp.float32),
        lax.psum(owned[5].astype(jnp.bfloat16), "ctx").astype(jnp.float32),
        lax.psum(owned[6].astype(jnp.bfloat16), "ctx").astype(jnp.float32),
        lax.psum(owned[7].astype(jnp.bfloat16), "ctx").astype(jnp.float32),
        lax.psum(owned[8].astype(jnp.bfloat16), "ctx").astype(jnp.float32),
    )
    return (
        outputs.reshape(tokens.shape).astype(bf16),
        grad_inputs.reshape(tokens.shape).astype(bf16),
        summed[0],
        summed[1],
        summed[2],
        summed[3],
        summed[4],
        summed[5],
        summed[6],
        summed[7],
        summed[8],
    )


def solution(mesh):
    in_specs = (
        P("wsh", "ctx", None),
        P("wsh", "ctx", None),
        P("wsh", None),
        P(),
        P("wsh", None),
        P("wsh", None),
        P("wsh", None),
        P("wsh", None),
        P("wsh", None),
        P("wsh", None),
        P("wsh"),
        P("wsh"),
        P("wsh"),
    )
    out_specs = (
        P("wsh", "ctx", None),
        P("wsh", "ctx", None),
        P("wsh", None),
        P("wsh", None),
        P("wsh", None),
        P("wsh", None),
        P("wsh", None),
        P("wsh", None),
        P("wsh"),
        P("wsh"),
        P("wsh"),
    )
    return jax.shard_map(
        per_device, mesh=mesh, in_specs=in_specs, out_specs=out_specs, check_vma=False
    )
```

profile of v0, /device:TPU:0, one launch (start us, length us, event | category | flops | bytes accessed | tf_op | source)
XLA Modules:
  0.0 1203.4 jit_solution(14284775622364229493)
XLA Ops:
  12.2 14.1 %all-reduce.9 = (bf16[1280]{0:T(1024)(128)(2,1)S(1)}, bf16[80]{0:T(256)(128)(2,1)S(1)}, bf16[1280]{0:T(1024)(128)(2,1)S(1)}) all-reduce(bf16[1280]{0:T(1024)(128)(2,1)S(1)} %dynamic-update-slice, bf16[80]{0:T(256)(128)(2,1)S(1)} %dynamic-update-slice.1, bf16[1280]{0:T(1024)(128)(2,1)S(1)} %dynamic-update-slice.2), channel_id=1, replica_groups=mesh['ctx'=8,'wsh'=4] {'wsh'}, use_global_device_ids=true, to_apply=%add | all-reduce | flops 2640 | bytes 10560
  26.6 51.6 %all-gather.15.cloned.1.call-done = bf16[1280,1280]{1,0:T(8,128)(2,1)} async-done(((bf16[320,1280]{1,0:T(8,128)(2,1)}), bf16[1280,1280]{1,0:T(8,128)(2,1)}) %all-gather.15.cloned.1.call-update) | async-done | bytes 3276816 | tf_op jit(solution)/shard_map/all_gather | solution.py:76
  82.1 62.0 %all-gather.9.cloned.1.call-done = bf16[1280,1280]{1,0:T(8,128)(2,1)} async-done(((bf16[320,1280]{1,0:T(8,128)(2,1)}), bf16[1280,1280]{1,0:T(8,128)(2,1)}) %all-gather.9.cloned.1.call-update) | async-done | bytes 3276816 | tf_op jit(solution)/shard_map/all_gather | solution.py:75
  150.7 59.4 %all-gather.13.cloned.1.call-done = bf16[1280,1280]{1,0:T(8,128)(2,1)} async-done(((bf16[320,1280]{1,0:T(8,128)(2,1)}), bf16[1280,1280]{1,0:T(8,128)(2,1)}) %all-gather.13.cloned.1.call-update) | async-done | bytes 3276816 | tf_op jit(solution)/shard_map/all_gather | solution.py:74
  219.8 32.3 %all-gather.17.cloned.1.call-done = bf16[2048,1280]{1,0:T(8,128)(2,1)} async-done(((bf16[256,1280]{1,0:T(8,128)(2,1)}), bf16[2048,1280]{1,0:T(8,128)(2,1)}) %all-gather.17.cloned.1.call-update) | async-done | bytes 5242896 | tf_op jit(solution)/shard_map/all_gather | solution.py:125
  252.1 43.5 %all-gather.11.cloned.1.call-done = bf16[2048,1280]{1,0:T(8,128)(2,1)} async-done(((bf16[256,1280]{1,0:T(8,128)(2,1)}), bf16[2048,1280]{1,0:T(8,128)(2,1)}) %all-gather.11.cloned.1.call-update) | async-done | bytes 5242896 | tf_op jit(solution)/shard_map/all_gather | solution.py:124
  295.6 42.3 %while.33 = (s32[]{:T(128)}, f32[16,256]{1,0:T(8,128)S(1)}, f32[16,256]{1,0:T(8,128)S(1)}, f32[256,16,80]{0,2,1:T(8,128)}, s32[2048]{0:T(1024)S(1)}, /*index=5*/...) while((s32[]{:T(128)}, f32[16,256]{1,0:T(8,128)S(1)}, ...), condition=%wide.region_6.7_spmd.clone, body=%wide.region_3.6_spmd.clone.sunk | while | flops 689004544 | bytes 52829436 | solution.py:146
  339.5 23.3 %all-gather.19.cloned.1.call-done = bf16[1280,1280]{1,0:T(8,128)(2,1)} async-done(((bf16[320,1280]{1,0:T(8,128)(2,1)}), bf16[1280,1280]{1,0:T(8,128)(2,1)}) %all-gather.19.cloned.1.call-update) | async-done | bytes 3276816 | tf_op jit(solution)/shard_map/all_gather | solution.py:77
  365.8 62.8 %all-gather.21.cloned.1.call-done = bf16[1280,1280]{1,0:T(8,128)(2,1)} async-done(((bf16[320,1280]{1,0:T(8,128)(2,1)}), bf16[1280,1280]{1,0:T(8,128)(2,1)}) %all-gather.21.cloned.1.call-update) | async-done | bytes 3276816 | tf_op jit(solution)/shard_map/all_gather | solution.py:78
  432.8 61.8 %all-gather.23.cloned.1.call-done = bf16[1280,1280]{1,0:T(8,128)(2,1)} async-done(((bf16[320,1280]{1,0:T(8,128)(2,1)}), bf16[1280,1280]{1,0:T(8,128)(2,1)}) %all-gather.23.cloned.1.call-update) | async-done | bytes 3276816 | tf_op jit(solution)/shard_map/all_gather | solution.py:79
  504.3 73.5 %while.34 = (s32[]{:T(128)}, f32[256,16,80]{0,2,1:T(8,128)}, bf16[4,512,16,80]{1,3,2,0:T(8,128)(2,1)}, bf16[4,512,16,80]{1,3,2,0:T(8,128)(2,1)}, bf16[4,512,1280...) while((s32[]{:T(128)}, f32[256,16,80]{0,2,1:T(8,128)}, ...), condition=%wide.region_11.12_spmd.clone, body=%wide.region_10.11_spmd.clone.sunk | while | flops 1695285248 | bytes 115531104 | solution.py:194
  577.9 6.9 copy.70
  589.7 6.9 copy.69
  622.0 22.7 %reduce-scatter.11.cloned.1.call-done = bf16[256,1280]{0,1:T(8,128)(2,1)} async-done(((bf16[2048,1280]{0,1:T(8,128)(2,1)}), bf16[256,1280]{0,1:T(8,128)(2,1)}) %reduce-scatter.11.cloned.1.call-update) | async-done | bytes 655376 | tf_op jit(solution)/shard_map/reduce_scatter | solution.py:210
  648.8 56.1 %reduce-scatter.9.cloned.1.call-done = bf16[256,1280]{0,1:T(8,128)(2,1)} async-done(((bf16[2048,1280]{0,1:T(8,128)(2,1)}), bf16[256,1280]{0,1:T(8,128)(2,1)}) %reduce-scatter.9.cloned.1.call-update) | async-done | bytes 655376 | tf_op jit(solution)/shard_map/reduce_scatter | solution.py:204
  710.2 59.4 %reduce-scatter.21.cloned.1.call-done = bf16[320,1280]{1,0:T(8,128)(2,1)} async-done(((bf16[1280,1280]{1,0:T(8,128)(2,1)}), bf16[320,1280]{1,0:T(8,128)(2,1)}) %reduce-scatter.21.cloned.1.call-update) | async-done | bytes 819216 | tf_op jit(solution)/shard_map/reduce_scatter | solution.py:253
  769.6 64.6 %reduce-scatter.23.cloned.1.call-done = bf16[320,1280]{1,0:T(8,128)(2,1)} async-done(((bf16[1280,1280]{1,0:T(8,128)(2,1)}), bf16[320,1280]{1,0:T(8,128)(2,1)}) %reduce-scatter.23.cloned.1.call-update) | async-done | bytes 819216 | tf_op jit(solution)/shard_map/reduce_scatter | solution.py:256
  834.2 64.7 %reduce-scatter.19.cloned.1.call-done = bf16[320,1280]{1,0:T(8,128)(2,1)} async-done(((bf16[1280,1280]{1,0:T(8,128)(2,1)}), bf16[320,1280]{1,0:T(8,128)(2,1)}) %reduce-scatter.19.cloned.1.call-update) | async-done | bytes 819216 | tf_op jit(solution)/shard_map/reduce_scatter | solution.py:250
  899.0 64.6 %reduce-scatter.13.cloned.1.call-done = bf16[320,1280]{1,0:T(8,128)(2,1)} async-done(((bf16[1280,1280]{1,0:T(8,128)(2,1)}), bf16[320,1280]{1,0:T(8,128)(2,1)}) %reduce-scatter.13.cloned.1.call-update) | async-done | bytes 819216 | tf_op jit(solution)/shard_map/reduce_scatter | solution.py:241
  963.6 64.6 %reduce-scatter.17.cloned.1.call-done = bf16[320,1280]{1,0:T(8,128)(2,1)} async-done(((bf16[1280,1280]{1,0:T(8,128)(2,1)}), bf16[320,1280]{1,0:T(8,128)(2,1)}) %reduce-scatter.17.cloned.1.call-update) | async-done | bytes 819216 | tf_op jit(solution)/shard_map/reduce_scatter | solution.py:247
  1028.2 64.6 %reduce-scatter.15.cloned.1.call-done = bf16[320,1280]{1,0:T(8,128)(2,1)} async-done(((bf16[1280,1280]{1,0:T(8,128)(2,1)}), bf16[320,1280]{1,0:T(8,128)(2,1)}) %reduce-scatter.15.cloned.1.call-update) | async-done | bytes 819216 | tf_op jit(solution)/shard_map/reduce_scatter | solution.py:244
  1105.6 10.0 all-reduce.8
  1115.8 12.4 %all-reduce.6 = (bf16[320]{0:T(512)(128)(2,1)S(1)}, bf16[320]{0:T(512)(128)(2,1)S(1)}, bf16[20]{0:T(256)(128)(2,1)S(1)}) all-reduce(bf16[320]{0:T(512)(128)(2,1)S(1)} %dynamic-slice.4, bf16[320]{0:T(512)(128)(2,1)S(1)} %dynamic-slice.6, bf16[20]{0:T(256)(128)(2,1)S(1)} %dynamic-slice.8), channel_id=1, replica_groups=mesh['ctx'=8,'wsh'=4] {'ctx'}, use_global_device_ids=true, to_apply=%region_29.30 | all-reduce | flops 660 | bytes 2640 | tf_op jit(solution)/shard_map/psum | solution.py:276
  1131.1 56.1 %all-reduce.12.cloned.1.call-done = (bf16[320,1280]{1,0:T(8,128)(2,1)}, bf16[320,1280]{1,0:T(8,128)(2,1)}, bf16[320,1280]{1,0:T(8,128)(2,1)}, bf16[320,1280]{1,0...) async-done(((bf16[320,1280]{1,0:T(8,128)(2,1)}, bf16[320,1280]{1,0:T(8,128)(2,1)}, bf16[320,1280]{1,0:T(8,128)(2,1)}, bf16[320,1280]{1,0:T(8,128)(2,1)}, ...) | async-done | bytes 4915216 | tf_op jit(solution)/shard_map/psum | solution.py:270
  (353 shorter events, 220.0 us)
Async XLA Ops:
  7.2 70.9 %all-gather.15.cloned.1.call-start = ((), (), s32[]{:S(2)}) async-start(), calls=%async_computation.11 | async-start | bytes 4096000 | tf_op jit(solution)/shard_map/all_gather | solution.py:76
  8.0 136.1 %all-gather.9.cloned.1.call-start = ((), (), s32[]{:S(2)}) async-start(), calls=%async_computation.8 | async-start | bytes 4096000 | tf_op jit(solution)/shard_map/all_gather | solution.py:75
  8.7 201.3 %all-gather.13.cloned.1.call-start = ((), (), s32[]{:S(2)}) async-start(), calls=%async_computation.10 | async-start | bytes 4096000 | tf_op jit(solution)/shard_map/all_gather | solution.py:74
  9.5 242.7 %all-gather.17.cloned.1.call-start = ((), (), s32[]{:S(2)}) async-start(), calls=%async_computation.12 | async-start | bytes 5898240 | tf_op jit(solution)/shard_map/all_gather | solution.py:125
  26.3 124.1 %copy-start.50 = (bf16[80]{0:T(256)(128)(2,1)}, bf16[80]{0:T(256)(128)(2,1)S(1)}, u32[]{:S(2)}) copy-start(bf16[80]{0:T(256)(128)(2,1)S(1)} %get-tuple-element.449) | copy-start | bytes 484
  26.3 189.3 %copy-start.36 = (f32[1280]{0:T(1024)}, f32[1280]{0:T(1024)S(1)}, u32[]{:S(2)}) copy-start(f32[1280]{0:T(1024)S(1)} %convert_element_type.194) | copy-start | bytes 15364
  26.6 189.1 %copy-start.38 = (f32[256]{0:T(256)}, f32[256]{0:T(256)S(1)}, u32[]{:S(2)}) copy-start(f32[256]{0:T(256)S(1)} %add_rsqrt_fusion.1) | copy-start | bytes 3076
  82.0 213.6 %all-gather.11.cloned.1.call-start = ((), (), s32[]{:S(2)}) async-start(), calls=%async_computation.9 | async-start | bytes 5898240 | tf_op jit(solution)/shard_map/all_gather | solution.py:124
  148.0 214.7 %all-gather.19.cloned.1.call-start = ((), (), s32[]{:S(2)}) async-start(), calls=%async_computation.13 | async-start | bytes 4096000 | tf_op jit(solution)/shard_map/all_gather | solution.py:77
  148.6 280.1 %all-gather.21.cloned.1.call-start = ((), (), s32[]{:S(2)}) async-start(), calls=%async_computation.14 | async-start | bytes 4096000 | tf_op jit(solution)/shard_map/all_gather | solution.py:78
  149.3 345.2 %all-gather.23.cloned.1.call-start = ((), (), s32[]{:S(2)}) async-start(), calls=%async_computation.15 | async-start | bytes 4096000 | tf_op jit(solution)/shard_map/all_gather | solution.py:79
  150.1 494.7 %reduce-scatter.11.cloned.1.call-start = ((), (), s32[]{:S(2)}) async-start(), calls=%async_computation.17 | async-start | bytes 5898240 | tf_op jit(solution)/shard_map/reduce_scatter | solution.py:210
  150.4 65.3 %copy-start.43 = (f32[80]{0:T(128)}, f32[80]{0:T(128)S(1)}, u32[]{:S(2)}) copy-start(f32[80]{0:T(128)S(1)} %fusion.60) | copy-start | bytes 964
  339.4 26.4 %copy-start.17 = (bf16[256,16,80]{0,2,1:T(8,128)(2,1)}, bf16[256,16,80]{0,2,1:T(8,128)(2,1)S(1)}, u32[]{:S(2)}) copy-start(bf16[256,16,80]{0,2,1:T(8,128)(2,1)S(1)} %fusion.55) | copy-start | bytes 1966084
  365.8 133.5 %copy-start.13 = (f32[256,1280]{1,0:T(8,128)}, f32[256,1280]{1,0:T(8,128)S(1)}, u32[]{:S(2)}) copy-start(f32[256,1280]{1,0:T(8,128)S(1)} %get-tuple-element.466) | copy-start | bytes 3932164
  428.6 65.9 %copy-start.32 = (bf16[1,256,1280]{2,1,0:T(8,128)(2,1)S(1)}, bf16[1,256,1280]{2,1,0:T(8,128)(2,1)}, u32[]{:S(2)}) copy-start(bf16[1,256,1280]{2,1,0:T(8,128)(2,1)} %param.18) | copy-start | bytes 1966084
  589.4 115.5 %reduce-scatter.9.cloned.1.call-start = ((), (), s32[]{:S(2)}) async-start(), calls=%async_computation.16 | async-start | bytes 5898240 | tf_op jit(solution)/shard_map/reduce_scatter | solution.py:204
  601.3 168.3 %reduce-scatter.21.cloned.1.call-start = ((), (), s32[]{:S(2)}) async-start(), calls=%async_computation.22 | async-start | bytes 4096000 | tf_op jit(solution)/shard_map/reduce_scatter | solution.py:253
  605.8 228.4 %reduce-scatter.23.cloned.1.call-start = ((), (), s32[]{:S(2)}) async-start(), calls=%async_computation.23 | async-start | bytes 4096000 | tf_op jit(solution)/shard_map/reduce_scatter | solution.py:256
  610.2 288.7 %reduce-scatter.19.cloned.1.call-start = ((), (), s32[]{:S(2)}) async-start(), calls=%async_computation.21 | async-start | bytes 4096000 | tf_op jit(solution)/shard_map/reduce_scatter | solution.py:250
  614.9 348.7 %reduce-scatter.13.cloned.1.call-start = ((), (), s32[]{:S(2)}) async-start(), calls=%async_computation.18 | async-start | bytes 4096000 | tf_op jit(solution)/shard_map/reduce_scatter | solution.py:241
  621.7 406.4 %reduce-scatter.17.cloned.1.call-start = ((), (), s32[]{:S(2)}) async-start(), calls=%async_computation.20 | async-start | bytes 4096000 | tf_op jit(solution)/shard_map/reduce_scatter | solution.py:247
  648.8 444.0 %reduce-scatter.15.cloned.1.call-start = ((), (), s32[]{:S(2)}) async-start(), calls=%async_computation.19 | async-start | bytes 4096000 | tf_op jit(solution)/shard_map/reduce_scatter | solution.py:244
  708.9 478.4 %all-reduce.12.cloned.1.call-start = ((), (), s32[]{:S(2)}) async-start(), calls=%async_computation.24 | async-start | bytes 9830400 | tf_op jit(solution)/shard_map/psum | solution.py:270
  (74 other events, 225.9 us)
Sparse Core Ops, SparseCore 0:
  9.6 68.4 all-gather.14
  79.7 64.3 all-gather.8
  145.7 64.3 all-gather.12
  212.4 39.7 all-gather.16
  254.4 41.1 all-gather.10
  297.0 65.6 all-gather.18
  364.3 64.3 all-gather.20
  430.2 64.2 all-gather.22
  589.5 55.1 reduce-scatter.10
  648.4 56.5 reduce-scatter.8
  707.3 62.2 reduce-scatter.20
  771.7 62.4 reduce-scatter.22
  836.5 62.3 reduce-scatter.18
  901.1 62.3 reduce-scatter.12
  965.7 62.3 reduce-scatter.16
  1030.3 62.3 reduce-scatter.14
  1096.7 90.4 all-reduce.11
where the time goes:
time: 1210 us; the launch traced here: 1200 us
  waiting for transfers between devices  918 us (76%)
  matrix products  113 us (9%)
  local copies, waits for them, and re-layouts  92 us (8%)
  blocking collectives  36.5 us (3%)
  other arithmetic  23.1 us (2%)
  between operations  17.5 us (1%)
    reduce_scatter x1, waiting for transfers between devices, per_device(): lax.psum_scatter(grad_outw.astype(jnp.bfloat16), 'wsh', scatter_dimension...  64.7 us
    reduce_scatter x1, waiting for transfers between devices, per_device(): lax.psum_scatter(grad_downw.astype(jnp.bfloat16), 'wsh', scatter_dimensio...  64.6 us
    reduce_scatter x1, waiting for transfers between devices, per_device(): lax.psum_scatter(grad_queryw.astype(jnp.bfloat16), 'wsh', scatter_dimensi...  64.6 us
    reduce_scatter x1, waiting for transfers between devices, per_device(): lax.psum_scatter(grad_keyw.astype(jnp.bfloat16), 'wsh', scatter_dimension...  64.6 us
    reduce_scatter x1, waiting for transfers between devices, per_device(): lax.psum_scatter(grad_valuew.astype(jnp.bfloat16), 'wsh', scatter_dimensi...  64.6 us
    all_gather x1, waiting for transfers between devices, per_device(): lax.all_gather(w_up, 'wsh', axis=0, tiled=True)  62.8 us
    all_gather x1, waiting for transfers between devices, per_device(): lax.all_gather(w_key, 'wsh', axis=0, tiled=True)  62 us
    all_gather x1, waiting for transfers between devices, per_device(): lax.all_gather(w_down, 'wsh', axis=0, tiled=True)  61.8 us
  transfers between devices with their start and end apart: 17, of which 17 were waited for; matrix products, arithmetic and copies ran while one was open for 10% of the time, Pallas kernels for 0%

commit v1 on v0

--- a/solution.py
+++ b/solution.py
@@ -1,8 +1,11 @@
+import functools
 import math
 
 import jax
 import jax.numpy as jnp
 from jax import lax
+from jax.experimental import pallas as pl
+from jax.experimental.pallas import tpu as pltpu
 from jax.sharding import PartitionSpec as P
 
 H = 16
@@ -292,6 +295,930 @@
     )
 
 
+MESH = pl.DeviceIdType.MESH
+NEG = -1e30
+VMEM_BYTES = 60 * 1024 * 1024
+
+
+def place():
+    c, z = lax.axis_index("ctx"), lax.axis_index("wsh")
+    core, x, y = lax.rem(c, 2), lax.rem(c // 2, 2), c // 4
+    sib = c + 1 - 2 * core
+    over_x, over_y = c + 2 - 4 * x, c + 4 - 8 * y
+    first = over_x * (1 - core) + over_y * core
+    second = over_y * (1 - core) + over_x * core
+    diag = over_x + over_y - c
+    return c, z, sib, first, second, diag
+
+
+def enter(c, z, n_ctx, n_wsh):
+    barrier = pltpu.get_barrier_semaphore()
+    for k in range(1, n_ctx):
+        pl.semaphore_signal(
+            barrier, inc=1, device_id=(lax.rem(c + k, n_ctx), z), device_id_type=MESH
+        )
+    for k in range(1, n_wsh):
+        pl.semaphore_signal(
+            barrier, inc=1, device_id=(c, lax.rem(z + k, n_wsh)), device_id_type=MESH
+        )
+    pl.semaphore_wait(barrier, n_ctx + n_wsh - 2)
+
+
+def send(src, dst, send_sem, recv_sem, c, z):
+    copy = pltpu.make_async_remote_copy(
+        src_ref=src, dst_ref=dst, send_sem=send_sem, recv_sem=recv_sem,
+        device_id=(c, z), device_id_type=MESH,
+    )
+    copy.start()
+    return copy
+
+
+def arrive(dst, send_sem, recv_sem, c, z):
+    pltpu.make_async_remote_copy(
+        src_ref=dst, dst_ref=dst, send_sem=send_sem, recv_sem=recv_sem,
+        device_id=(c, z), device_id_type=MESH,
+    ).wait_recv()
+
+
+def left(src, send_sem, recv_sem, c, z):
+    pltpu.make_async_remote_copy(
+        src_ref=src, dst_ref=src, send_sem=send_sem, recv_sem=recv_sem,
+        device_id=(c, z), device_id_type=MESH,
+    ).wait_send()
+
+
+class Line:
+    def __init__(self, at, c, z, n, send_sem, recv_sem):
+        self.at, self.c, self.z, self.n = at, c, z, n
+        self.send_sem, self.recv_sem = send_sem, recv_sem
+
+    def start(self, own):
+        c, z = self.c, self.z
+
+        @pl.when(z < self.n - 1)
+        def _():
+            send(own, self.at(z), self.send_sem.at[0], self.recv_sem.at[z], c, z + 1)
+
+        @pl.when(z > 0)
+        def _():
+            send(own, self.at(z), self.send_sem.at[1], self.recv_sem.at[z], c, z - 1)
+
+    def forward(self, distance, then=None):
+        c, z, n = self.c, self.z, self.n
+        below, above = z - distance, z + distance
+
+        @pl.when(below >= 0)
+        def _():
+            arrive(self.at(below), self.send_sem.at[0], self.recv_sem.at[below], c, z)
+
+            @pl.when(z < n - 1)
+            def _():
+                send(self.at(below), self.at(below), self.send_sem.at[2 * distance], self.recv_sem.at[below], c, z + 1)
+
+            if then is not None:
+                then(below)
+
+        @pl.when(above < n)
+        def _():
+            arrive(self.at(above), self.send_sem.at[0], self.recv_sem.at[above], c, z)
+
+            @pl.when(z > 0)
+            def _():
+                send(self.at(above), self.at(above), self.send_sem.at[2 * distance + 1], self.recv_sem.at[above], c, z - 1)
+
+            if then is not None:
+                then(above)
+
+    def finish(self, own):
+        c, z, n = self.c, self.z, self.n
+
+        @pl.when(z < n - 1)
+        def _():
+            left(own, self.send_sem.at[0], self.recv_sem.at[z], c, z)
+
+        @pl.when(z > 0)
+        def _():
+            left(own, self.send_sem.at[1], self.recv_sem.at[z], c, z)
+
+        for distance in range(1, n):
+            below, above = z - distance, z + distance
+
+            @pl.when((below >= 0) & (z < n - 1))
+            def _():
+                left(self.at(below), self.send_sem.at[2 * distance], self.recv_sem.at[below], c, z)
+
+            @pl.when((above < n) & (z > 0))
+            def _():
+                left(self.at(above), self.send_sem.at[2 * distance + 1], self.recv_sem.at[above], c, z)
+
+
+class Plane:
+    def __init__(self, at, c, z, around, send_sem, recv_sem):
+        self.at, self.c, self.z = at, c, z
+        self.sib, self.first, self.second, self.diag = around
+        self.send_sem, self.recv_sem = send_sem, recv_sem
+
+    def push(self, slot, block, target, src=None):
+        src = self.at(block) if src is None else src
+        send(src, self.at(block), self.send_sem.at[slot], self.recv_sem.at[block], target, self.z)
+
+    def wait(self, block):
+        arrive(self.at(block), self.send_sem.at[0], self.recv_sem.at[block], self.c, self.z)
+
+    def start(self, own=None):
+        self.push(0, self.c, self.first, own)
+        self.push(1, self.c, self.second, own)
+        self.push(2, self.c, self.sib, own)
+
+    def from_first(self):
+        self.wait(self.first)
+        self.push(3, self.first, self.second)
+        self.push(4, self.first, self.sib)
+
+    def from_second(self):
+        self.wait(self.second)
+        self.push(5, self.second, self.sib)
+
+    def from_diag(self):
+        self.wait(self.diag)
+        self.push(6, self.diag, self.sib)
+
+    def others(self):
+        shift = self.sib - self.c
+        return (self.sib, self.second + shift, self.first + shift, self.diag + shift)
+
+    def finish(self):
+        for slot in range(7):
+            left(self.at(self.c), self.send_sem.at[slot], self.recv_sem.at[self.c], self.c, self.z)
+
+
+def block_ids_of(block, order_ref, lengths_ref, rows):
+    n_blk = lengths_ref.shape[1]
+    position = order_ref[block] * rows + lax.broadcasted_iota(jnp.int32, (8, rows), 1)
+    ids = jnp.zeros((8, rows), jnp.int32)
+    bound = jnp.int32(0)
+    for b in range(n_blk):
+        bound = bound + lengths_ref[0, b]
+        ids = ids + jnp.where(position >= bound, 1, 0)
+    return ids, lax.broadcasted_iota(jnp.int32, (8, rows), 0)
+
+
+def three_rows(value, rows):
+    f32 = jnp.float32
+    high = value.astype(jnp.bfloat16).astype(f32)
+    rest = value - high
+    mid = rest.astype(jnp.bfloat16).astype(f32)
+    low = rest - mid
+    row = lax.broadcasted_iota(jnp.int32, (8, rows), 0)
+    return jnp.where(row == 0, high, 0.0) + jnp.where(row == 1, mid, 0.0) + jnp.where(row == 2, low, 0.0)
+
+
+def forward_kernel(
+    dims,
+    tok_ref, wqkv_ref, w3_ref, pack_ref, order_ref, lengths_ref,
+    h1_out, wc_out, kaug_out, vaug_out, kt_out, qaug_out, qraw_out, o_out, ob_out, full_out, gain_out,
+    tok_all, h1_all, w_c, packs, gains, kaug, vaug, kt, vt, qaug, qraw, qneg, o_all, ob_stage, ob_land, s_buf,
+    tok_send, tok_recv, wz_send, wz_recv, pk_send, pk_recv, ob_send, ob_recv,
+    w3z_send, w3z_recv, w3p_send, w3p_recv, local_sem,
+):
+    n_ctx, n_wsh, hd, heads = dims
+    f32, bf16 = jnp.float32, jnp.bfloat16
+    c, z, sib, first, second, diag = place()
+    around = (sib, first, second, diag)
+    rows, width = tok_ref.shape
+    span = hd * heads
+    shard = w_c.shape[0] // n_wsh
+    cut = shard // (n_ctx // 2)
+    half = width // 2
+    length = rows * n_ctx
+    enter(c, z, n_ctx, n_wsh)
+
+    tokens = Plane(lambda b: tok_all.at[b], c, z, around, tok_send, tok_recv)
+    tokens.start(tok_ref)
+    wline = Line(lambda s: w_c.at[pl.ds(pl.multiple_of(s * shard, 16), shard)], c, z, n_wsh, wz_send, wz_recv)
+    for k in range(1, n_wsh):
+        send(pack_ref, packs.at[z], pk_send.at[k], pk_recv.at[z], c, lax.rem(z + k, n_wsh))
+    wline.start(wqkv_ref)
+    own_tok = pltpu.make_async_copy(tok_ref, tok_all.at[c], local_sem.at[0])
+    own_w = pltpu.make_async_copy(wqkv_ref, wline.at(z), local_sem.at[1])
+    own_pack = pltpu.make_async_copy(pack_ref, packs.at[z], local_sem.at[2])
+    own_full = pltpu.make_async_copy(
+        w3_ref, full_out.at[:, pl.ds(pl.multiple_of(z * shard, 16), shard)], local_sem.at[3]
+    )
+    for copy in (own_tok, own_w, own_pack, own_full):
+        copy.start()
+    own_tok.wait()
+    own_pack.wait()
+    for k in range(1, n_wsh):
+        other = lax.rem(z + k, n_wsh)
+        arrive(packs.at[other], pk_send.at[0], pk_recv.at[other], c, z)
+
+    row8 = lax.broadcasted_iota(jnp.int32, (8, width), 0)
+    total = jnp.zeros((8, width), f32)
+    for s in range(n_wsh):
+        wide = jnp.concatenate([packs[s], jnp.zeros((8, width - packs.shape[2]), f32)], axis=1)
+        by_shard = pltpu.roll(wide, s * shard, 1) if s else wide
+        by_dim = pltpu.roll(wide, s * (hd // n_wsh), 1) if s else wide
+        total = total + jnp.where(row8 < 2, by_shard, by_dim)
+    gains[...] = total
+    scale = jnp.concatenate([total[2:3, 0:128], jnp.zeros((7, 128), f32)], axis=0)
+    soft = jnp.maximum(scale, 0.0) + jnp.log(1.0 + jnp.exp(-jnp.abs(scale)))
+    gain_col = (LOG_BASE / math.sqrt(hd) * soft).T[0:hd, 0:1]
+
+    def norm_block(b):
+        gain = gains[0:1, :]
+
+        def some_rows(i, _):
+            at = pl.ds(pl.multiple_of(i * 32, 32), 32)
+            t = tok_all[b, at, :].astype(f32)
+            inverse = lax.rsqrt(jnp.mean(t * t, -1, keepdims=True) + EPS)
+            h1_all[b, at, :] = (t * inverse * gain).astype(bf16)
+            return 0
+
+        lax.fori_loop(0, rows // 32, some_rows, 0)
+        pltpu.make_async_copy(h1_all.at[b], h1_out.at[b], local_sem.at[5]).start()
+
+    others = tokens.others()
+    norm_block(c)
+    tokens.wait(others[0])
+    norm_block(others[0])
+    wline.forward(1)
+    tokens.from_first()
+    norm_block(first)
+    wline.forward(2)
+    tokens.from_second()
+    norm_block(second)
+    tokens.wait(others[1])
+    norm_block(others[1])
+    tokens.wait(others[2])
+    norm_block(others[2])
+    wline.forward(3)
+    tokens.from_diag()
+    norm_block(diag)
+    own_w.wait()
+
+    def piece(s, b):
+        top = pl.multiple_of(s * shard + (b // 2) * cut, 16)
+        return full_out.at[:, pl.ds(top, cut), pl.ds(pl.multiple_of(lax.rem(b, 2) * half, 128), half)]
+
+    my_piece = w3_ref.at[
+        :, pl.ds(pl.multiple_of((c // 2) * cut, 16), cut), pl.ds(pl.multiple_of(lax.rem(c, 2) * half, 128), half)
+    ]
+    line3 = Line(lambda s: piece(s, c), c, z, n_wsh, w3z_send, w3z_recv)
+    line3.start(my_piece)
+
+    tokens.wait(others[3])
+    norm_block(others[3])
+
+    def project(b, _):
+        raw = jnp.dot(h1_all[b], w_c[...], preferred_element_type=f32).T
+        at = pl.ds(pl.multiple_of(b * rows, 128), rows)
+        ids, row = block_ids_of(b, order_ref, lengths_ref, rows)
+        hot = jnp.where(ids == row, 1.0, 0.0)
+        neg = jnp.where(row > ids, NEG, 0.0)
+        ones = jnp.ones((8, rows), f32)
+        qneg[b] = neg
+        qraw[b] = raw[0:span]
+        for h in range(heads):
+            q = raw[h * hd : (h + 1) * hd] * gain_col
+            qaug[b, h, 0:hd, :] = q.astype(bf16)
+            qaug[b, h, hd : hd + 16, :] = jnp.concatenate([neg, jnp.zeros((8, rows), f32)], axis=0).astype(bf16)
+            qaug[b, h, hd + 16 : 128, :] = jnp.zeros((112 - hd, rows), bf16)
+            k = raw[span + h * hd : span + (h + 1) * hd].astype(bf16)
+            v = raw[2 * span + h * hd : 2 * span + (h + 1) * hd].astype(bf16)
+            tail = jnp.zeros((112 - hd, rows), f32)
+            kt[h, :, at] = k
+            vt[h, 0:hd, at] = v
+            vt[h, hd : hd + 16, at] = jnp.ones((16, rows), bf16)
+            kaug[h, at, :] = jnp.concatenate([k.astype(f32), hot, ones, tail], axis=0).T.astype(bf16)
+            vaug[h, at, :] = jnp.concatenate([v.astype(f32), ones, ones, tail], axis=0).T.astype(bf16)
+        return 0
+
+    lax.fori_loop(0, n_ctx, project, 0)
+    saved = [
+        pltpu.make_async_copy(w_c, wc_out, local_sem.at[6]),
+        pltpu.make_async_copy(kaug, kaug_out, local_sem.at[7]),
+        pltpu.make_async_copy(vaug, vaug_out, local_sem.at[8]),
+        pltpu.make_async_copy(kt, kt_out, local_sem.at[9]),
+        pltpu.make_async_copy(qraw, qraw_out, local_sem.at[10]),
+        pltpu.make_async_copy(gains, gain_out, local_sem.at[11]),
+    ]
+    for copy in saved:
+        copy.start()
+
+    planes = [
+        Plane(lambda b, s=lax.rem(z + k, n_wsh): piece(s, b), c, z, around, w3p_send.at[k], w3p_recv.at[k])
+        for k in range(n_wsh)
+    ]
+
+    def plane_of(s):
+        k = lax.rem(s - z + n_wsh, n_wsh)
+        Plane(lambda b: piece(s, b), c, z, around, w3p_send.at[k], w3p_recv.at[k]).start()
+
+    keys = length // 4
+
+    def attend(i, _):
+        g = lax.rem(c + 1 + i, n_ctx)
+        for h in range(heads):
+            q = qaug[g, h]
+            top = jnp.full((1, rows), -jnp.inf, f32)
+            for j in range(4):
+                s = jnp.dot(kaug[h, j * keys : (j + 1) * keys, :], q, preferred_element_type=f32)
+                s_buf[j * keys : (j + 1) * keys, :] = s
+                top = jnp.maximum(top, jnp.max(s, axis=0, keepdims=True))
+            out = jnp.zeros((hd + 16, rows), f32)
+            for j in range(4):
+                p = jnp.exp(s_buf[j * keys : (j + 1) * keys, :] - top).astype(bf16)
+                out = out + jnp.dot(vt[h, :, j * keys : (j + 1) * keys], p, preferred_element_type=f32)
+            total = out[hd : hd + 1]
+            o = out[0:hd] / total
+            lse = top + jnp.log(total)
+            o_all[g, h * hd : (h + 1) * hd, :] = o
+            ob_stage[g, h * hd : (h + 1) * hd, :] = o.astype(bf16)
+            qaug[g, h, hd : hd + 16, :] = jnp.concatenate([qneg[g], three_rows(-lse, rows)], axis=0).astype(bf16)
+
+        @pl.when(i < n_ctx - 1)
+        def _():
+            send(ob_stage.at[g], ob_land.at[c], ob_send.at[g], ob_recv.at[c], g, z)
+
+        return 0
+
+    lax.fori_loop(0, n_ctx, attend, 0)
+    own_o = pltpu.make_async_copy(ob_stage.at[c], ob_land.at[c], local_sem.at[0])
+    own_o.start()
+    more = [
+        pltpu.make_async_copy(qaug, qaug_out, local_sem.at[12]),
+        pltpu.make_async_copy(o_all, o_out, local_sem.at[13]),
+    ]
+    for copy in more:
+        copy.start()
+
+    for distance in range(1, n_wsh):
+        line3.forward(distance, plane_of)
+    for k in range(1, n_wsh):
+        planes[k].from_first()
+    for k in range(1, n_wsh):
+        planes[k].from_second()
+    for k in range(1, n_wsh):
+        planes[k].from_diag()
+    for k in range(1, n_wsh):
+        for b in others:
+            planes[k].wait(b)
+    own_o.wait()
+    for k in range(1, n_ctx):
+        g = lax.rem(c + k, n_ctx)
+        arrive(ob_land.at[g], ob_send.at[0], ob_recv.at[g], c, z)
+        left(ob_stage.at[g], ob_send.at[g], ob_recv.at[g], c, z)
+    last = pltpu.make_async_copy(ob_land, ob_out, local_sem.at[4])
+    last.start()
+    tokens.finish()
+    wline.finish(wqkv_ref)
+    line3.finish(my_piece)
+    for k in range(1, n_wsh):
+        planes[k].finish()
+        left(pack_ref, pk_send.at[k], pk_recv.at[z], c, z)
+    for copy in saved + more:
+        copy.wait()
+    for k in range(n_ctx):
+        pltpu.make_async_copy(h1_all.at[k], h1_out.at[k], local_sem.at[5]).wait()
+    own_full.wait()
+    last.wait()
+
+
+def forward_call(dims, tok, wqkv, w3, pack, order, lengths):
+    n_ctx, n_wsh, hd, heads = dims
+    rows, width = tok.shape
+    span, length = hd * heads, rows * n_ctx
+    f32, bf16 = jnp.float32, jnp.bfloat16
+    hbm = pl.BlockSpec(memory_space=pl.ANY)
+    smem = pl.BlockSpec(memory_space=pltpu.SMEM)
+    shape = jax.ShapeDtypeStruct
+    dma = pltpu.SemaphoreType.DMA
+    outs = (
+        shape((n_ctx, rows, width), bf16),
+        shape((width, wqkv.shape[1]), bf16),
+        shape((heads, length, 128), bf16),
+        shape((heads, length, 128), bf16),
+        shape((heads, hd, length), bf16),
+        shape((n_ctx, heads, 128, rows), bf16),
+        shape((n_ctx, span, rows), f32),
+        shape((n_ctx, span, rows), f32),
+        shape((n_ctx, span, rows), bf16),
+        shape((3, width, width), bf16),
+        shape((8, width), f32),
+    )
+    scratch = [
+        pltpu.VMEM((n_ctx, rows, width), bf16),
+        pltpu.VMEM((n_ctx, rows, width), bf16),
+        pltpu.VMEM((width, wqkv.shape[1]), bf16),
+        pltpu.VMEM((n_wsh,) + pack.shape, f32),
+        pltpu.VMEM((8, width), f32),
+        pltpu.VMEM((heads, length, 128), bf16),
+        pltpu.VMEM((heads, length, 128), bf16),
+        pltpu.VMEM((heads, hd, length), bf16),
+        pltpu.VMEM((heads, hd + 16, length), bf16),
+        pltpu.VMEM((n_ctx, heads, 128, rows), bf16),
+        pltpu.VMEM((n_ctx, span, rows), f32),
+        pltpu.VMEM((n_ctx, 8, rows), f32),
+        pltpu.VMEM((n_ctx, span, rows), f32),
+        pltpu.VMEM((n_ctx, span, rows), bf16),
+        pltpu.VMEM((n_ctx, span, rows), bf16),
+        pltpu.VMEM((length, rows), f32),
+        dma((7,)), dma((n_ctx,)),
+        dma((2 * n_wsh,)), dma((n_wsh,)),
+        dma((n_wsh,)), dma((n_wsh,)),
+        dma((n_ctx,)), dma((n_ctx,)),
+        dma((2 * n_wsh,)), dma((n_wsh,)),
+        dma((n_wsh, 7)), dma((n_wsh, n_ctx)),
+        dma((14,)),
+    ]
+    return pl.pallas_call(
+        functools.partial(forward_kernel, dims),
+        out_shape=outs,
+        in_specs=[hbm] * 4 + [smem] * 2,
+        out_specs=[hbm] * len(outs),
+        scratch_shapes=scratch,
+        compiler_params=pltpu.CompilerParams(
+            collective_id=0, has_side_effects=True, vmem_limit_bytes=VMEM_BYTES
+        ),
+    )(tok, wqkv, w3, pack, order, lengths)
+
+
+def add_rows(target, index, at, other, other_index, other_at, rows, step=16):
+    f32 = jnp.float32
+
+    def some_rows(i, _):
+        here = pl.ds(pl.multiple_of(at + i * step, 16), step)
+        there = pl.ds(pl.multiple_of(other_at + i * step, 16), step)
+        left_part = target[index + (here, slice(None))].astype(f32)
+        right_part = other[other_index + (there, slice(None))].astype(f32)
+        target[index + (here, slice(None))] = (left_part + right_part).astype(target.dtype)
+        return 0
+
+    lax.fori_loop(0, rows // step, some_rows, 0)
+
+
+def windows(width, n):
+    part = width // n
+    tiles = -(-part // 128) + (0 if part % 128 == 0 else 0)
+    size = tiles * 128
+    return [min(s * part // 128 * 128, width - size) for s in range(n)], size
+
+
+def backward_kernel(
+    dims,
+    go_ref, dwo_ref, dwu_ref, dwd_ref, tok_ref, dx_ref, vec_ref, gain_ref,
+    h1_ref, wc_ref, kaug_ref, vaug_ref, kt_ref, qaug_ref, qraw_ref, o_ref,
+    gtok_out, dw3_out, dwqkv_out, vec_out,
+    go_land, h1_all, w_c, kaug, vaug, kt, qaug, qraw, o_all, goaug, go_tm, q_tm, dk, dv, dqkv, scale_acc,
+    win_out, win_land, fin_qkv, part, part_p, part_f, part_s,
+    acc, land_p, land_f, land_s, land_z, fin3, dh, dx, tok, gains, gtok, vec, vec_plane, vec_line, vec_mid, vec_sum,
+    go_send, go_recv, p_send, p_recv, f_send, f_recv, s_send, s_recv, z_send, z_recv, g_send, g_recv,
+    hp_send, hp_recv, hf_send, hf_recv, hs_send, hs_recv, w_send, w_recv, wg_send, wg_recv,
+    vp_send, vp_recv, vl_send, vl_recv, local_sem,
+):
+    n_ctx, n_wsh, hd, heads = dims
+    f32, bf16 = jnp.float32, jnp.bfloat16
+    c, z, sib, first, second, diag = place()
+    around = (sib, first, second, diag)
+    core, x, y = lax.rem(c, 2), lax.rem(c // 2, 2), c // 4
+    f_bit, s_bit = x * (1 - core) + y * core, y * (1 - core) + x * core
+    rows, width = tok_ref.shape
+    span = hd * heads
+    length = rows * n_ctx
+    shard = width // n_wsh
+    half = width // 2
+    two, one = shard // 2, shard // 4
+    weights = (dwo_ref, dwu_ref, dwd_ref)
+    enter(c, z, n_ctx, n_wsh)
+
+    for k in range(1, n_ctx):
+        g = lax.rem(c + k, n_ctx)
+        send(go_ref.at[g], go_land.at[c], go_send.at[k], go_recv.at[c], g, z)
+    mine = pl.ds(pl.multiple_of(core * half, 128), half)
+    theirs = pl.ds(pl.multiple_of((1 - core) * half, 128), half)
+    order3 = (2, 1, 0)
+    for w in order3:
+        send(weights[w].at[:, :, theirs], land_p.at[w], p_send.at[w], p_recv.at[w], sib, z)
+    loads = [
+        (go_ref.at[c], go_land.at[c]), (qaug_ref, qaug), (o_ref, o_all), (kaug_ref, kaug), (vaug_ref, vaug), (kt_ref, kt),
+        (qraw_ref, qraw), (gain_ref, gains),
+    ]
+    later = [
+        (dwd_ref.at[:, :, mine], acc.at[2]), (dwu_ref.at[:, :, mine], acc.at[1]), (dwo_ref.at[:, :, mine], acc.at[0]),
+        (h1_ref, h1_all), (wc_ref, w_c), (tok_ref, tok), (dx_ref, dx), (vec_ref, vec),
+    ]
+    loads = [pltpu.make_async_copy(a, b, local_sem.at[i]) for i, (a, b) in enumerate(loads)]
+    later = [pltpu.make_async_copy(a, b, local_sem.at[i + 8]) for i, (a, b) in enumerate(later)]
+    for copy in loads + later:
+        copy.start()
+    dk[...] = jnp.zeros_like(dk)
+    dv[...] = jnp.zeros_like(dv)
+    scale_acc[...] = jnp.zeros_like(scale_acc)
+    dqkv[3 * span :, :] = jnp.zeros((dqkv.shape[0] - 3 * span, length), bf16)
+    for copy in loads:
+        copy.wait()
+
+    scale = jnp.concatenate([gains[2:3, 0:128], jnp.zeros((7, 128), f32)], axis=0)
+    soft = jnp.maximum(scale, 0.0) + jnp.log(1.0 + jnp.exp(-jnp.abs(scale)))
+    gain_col = (LOG_BASE / math.sqrt(hd) * soft).T[0:hd, 0:1]
+
+    def prepare(g):
+        at = pl.ds(pl.multiple_of(g * rows, 16), rows)
+        for h in range(heads):
+            go = go_land[g, h * hd : (h + 1) * hd, :]
+            wide = go.astype(f32)
+            delta = jnp.sum(wide * o_all[g, h * hd : (h + 1) * hd, :], axis=0, keepdims=True)
+            tail = jnp.concatenate([three_rows(-delta, rows), jnp.zeros((120 - hd, rows), f32)], axis=0)
+            goaug[g, h, 0:hd, :] = go
+            goaug[g, h, hd:128, :] = tail.astype(bf16)
+            go_tm[h, at, :] = jnp.concatenate([wide, jnp.zeros((128 - hd, rows), f32)], axis=0).T.astype(bf16)
+            q = qaug[g, h, 0:hd, :].astype(f32)
+            q_tm[h, at, :] = jnp.concatenate([q, jnp.zeros((128 - hd, rows), f32)], axis=0).T.astype(bf16)
+
+    def reduce_pair(w):
+        arrive(land_p.at[w], p_send.at[w], p_recv.at[w], c, z)
+        for s in range(n_wsh):
+            add_rows(acc, (w, s), 0, land_p, (w, s), 0, shard)
+        at = pl.ds(pl.multiple_of((1 - f_bit) * two, 16), two)
+        send(acc.at[w, :, at], land_f.at[w], f_send.at[w], f_recv.at[w], first, z)
+
+    def reduce_first(w):
+        arrive(land_f.at[w], f_send.at[w], f_recv.at[w], c, z)
+        for s in range(n_wsh):
+            add_rows(acc, (w, s), f_bit * two, land_f, (w, s), 0, two)
+        at = pl.ds(pl.multiple_of(f_bit * two + (1 - s_bit) * one, 16), one)
+        send(acc.at[w, :, at], land_s.at[w], s_send.at[w], s_recv.at[w], second, z)
+
+    my_top = f_bit * two + s_bit * one
+
+    def reduce_second(w):
+        arrive(land_s.at[w], s_send.at[w], s_recv.at[w], c, z)
+        for s in range(n_wsh):
+            add_rows(acc, (w, s), my_top, land_s, (w, s), 0, one)
+        at = pl.ds(pl.multiple_of(my_top, 16), one)
+        for k in range(1, n_wsh):
+            s = lax.rem(z + k, n_wsh)
+            send(acc.at[w, s, at], land_z.at[w, z], z_send.at[w, k], z_recv.at[w, z], c, s)
+
+    def out_piece(w, b):
+        b_core, b_x, b_y = lax.rem(b, 2), lax.rem(b // 2, 2), b // 4
+        r = (1 - b_core) * (2 * b_x + b_y) + b_core * (2 * b_y + b_x)
+        return dw3_out.at[
+            w, pl.ds(pl.multiple_of(r * one, 16), one), pl.ds(pl.multiple_of(b_core * half, 128), half)
+        ]
+
+    planes = [
+        Plane(lambda b, w=w: out_piece(w, b), c, z, around, g_send.at[w], g_recv.at[w]) for w in range(3)
+    ]
+
+    def reduce_line(w):
+        for k in range(1, n_wsh):
+            s = lax.rem(z + k, n_wsh)
+            arrive(land_z.at[w, s], z_send.at[w, 0], z_recv.at[w, s], c, z)
+
+        def some_rows(i, _):
+            at = pl.ds(pl.multiple_of(i * 16, 16), 16)
+            total = acc[w, z, pl.ds(pl.multiple_of(my_top + i * 16, 16), 16), :].astype(f32)
+            for k in range(1, n_wsh):
+                total = total + land_z[w, lax.rem(z + k, n_wsh), at, :].astype(f32)
+            fin3[w, at, :] = total.astype(bf16)
+            return 0
+
+        lax.fori_loop(0, one // 16, some_rows, 0)
+        planes[w].start(fin3.at[w])
+        pltpu.make_async_copy(fin3.at[w], out_piece(w, c), local_sem.at[16]).start()
+
+    for k in range(n_ctx):
+        g = lax.rem(c + k, n_ctx)
+        if k:
+            arrive(go_land.at[g], go_send.at[0], go_recv.at[g], c, z)
+        prepare(g)
+    for copy in later:
+        copy.wait()
+    for w in order3:
+        reduce_pair(w)
+
+    chunk = length // 4
+
+    def attend(g, _):
+        at = pl.ds(pl.multiple_of(g * rows, 16), rows)
+        for h in range(heads):
+            dq = jnp.zeros((hd, rows), f32)
+            for j in range(4):
+                keys = slice(j * chunk, (j + 1) * chunk)
+                p = jnp.exp(jnp.dot(kaug[h, keys, :], qaug[g, h], preferred_element_type=f32))
+                ds = (p * jnp.dot(vaug[h, keys, :], goaug[g, h], preferred_element_type=f32)).astype(bf16)
+                dq = dq + jnp.dot(kt[h, :, keys], ds, preferred_element_type=f32)
+                dk[h, keys, :] += jnp.dot(ds, q_tm[h, at, :], preferred_element_type=f32)
+                dv[h, keys, :] += jnp.dot(p.astype(bf16), go_tm[h, at, :], preferred_element_type=f32)
+            scale_acc[...] += dq * qraw[g, h * hd : (h + 1) * hd, :]
+            lanes = pl.ds(pl.multiple_of(g * rows, 128), rows)
+            dqkv[h * hd : (h + 1) * hd, lanes] = (dq * gain_col).astype(bf16)
+
+        for step, w in ((3, 2), (6, 1)):
+
+            @pl.when(g == step)
+            def _():
+                reduce_first(w)
+
+        return 0
+
+    lax.fori_loop(0, n_ctx, attend, 0)
+
+    def settle(g, _):
+        at = pl.ds(pl.multiple_of(g * rows, 16), rows)
+        lanes = pl.ds(pl.multiple_of(g * rows, 128), rows)
+        for h in range(heads):
+            for source, top in ((dk, span), (dv, 2 * span)):
+                turned = source[h, at, :].T
+                dqkv[top + h * hd : top + (h + 1) * hd, lanes] = turned[0:hd].astype(bf16)
+        return 0
+
+    lax.fori_loop(0, n_ctx, settle, 0)
+
+    starts, size = windows(width, n_wsh)
+    for s in range(n_wsh):
+        total = jnp.zeros((3 * span, size), f32)
+        for b in range(n_ctx):
+            total = total + jnp.dot(
+                dqkv[0 : 3 * span, b * rows : (b + 1) * rows], h1_all[b, :, starts[s] : starts[s] + size],
+                preferred_element_type=f32,
+            )
+        win_out[s] = total.astype(bf16)
+
+        @pl.when(z != s)
+        def _():
+            send(win_out.at[s], win_land.at[z], w_send.at[s], w_recv.at[z], c, s)
+
+    def partial(b):
+        lanes = pl.ds(pl.multiple_of(b * rows, 128), rows)
+        part[b] = jnp.dot(w_c[...], dqkv[:, lanes], preferred_element_type=f32).astype(bf16)
+
+    shift = sib - c
+
+    def from_sib(i, _):
+        b = lax.rem(2 * i + (1 - core), n_ctx)
+        partial(b)
+        send(part.at[b], part_p.at[i], hp_send.at[i], hp_recv.at[i], sib, z)
+        return 0
+
+    lax.fori_loop(0, n_ctx // 2, from_sib, 0)
+
+    def own_core(i, _):
+        partial(2 * i + core)
+        return 0
+
+    lax.fori_loop(0, n_ctx // 2, own_core, 0)
+    reduce_first(0)
+    reduce_second(2)
+
+    for i, b in enumerate((first, diag, second, c)):
+        arrive(part_p.at[b // 2], hp_send.at[0], hp_recv.at[b // 2], c, z)
+        add_rows(part, (b,), 0, part_p, (b // 2,), 0, width)
+        if i < 2:
+            slot = s_bit if i == 0 else 1 - s_bit
+            send(part.at[b], part_f.at[slot], hf_send.at[i], hf_recv.at[slot], first, z)
+    reduce_second(1)
+    arrive(part_f.at[1 - s_bit], hf_send.at[0], hf_recv.at[1 - s_bit], c, z)
+    add_rows(part, (second,), 0, part_f, (1 - s_bit,), 0, width)
+    send(part.at[second], part_s, hs_send.at[0], hs_recv.at[0], second, z)
+    arrive(part_f.at[s_bit], hf_send.at[0], hf_recv.at[s_bit], c, z)
+    add_rows(part, (c,), 0, part_f, (s_bit,), 0, width)
+    reduce_second(0)
+    reduce_line(2)
+    reduce_line(1)
+
+    for k in range(1, n_wsh):
+        s = lax.rem(z + k, n_wsh)
+        arrive(win_land.at[s], w_send.at[0], w_recv.at[s], c, z)
+
+    def sum_windows(i, _):
+        at = pl.ds(pl.multiple_of(i * 16, 16), 16)
+        total = win_out[z, at, :].astype(f32)
+        for k in range(1, n_wsh):
+            total = total + win_land[lax.rem(z + k, n_wsh), at, :].astype(f32)
+        fin_qkv[at, :] = total.astype(bf16)
+        return 0
+
+    lax.fori_loop(0, 3 * span // 16, sum_windows, 0)
+    plane_w = Plane(lambda b: dwqkv_out.at[b], c, z, around, wg_send, wg_recv)
+    plane_w.start(fin_qkv)
+    own_fin = pltpu.make_async_copy(fin_qkv, dwqkv_out.at[c], local_sem.at[17])
+    own_fin.start()
+    reduce_line(0)
+
+    arrive(part_s, hs_send.at[0], hs_recv.at[0], c, z)
+
+    def turn(i, _):
+        at = pl.ds(pl.multiple_of(i * 128, 128), 128)
+        dh[:, at] = (part[c, at, :].astype(f32) + part_s[at, :].astype(f32)).T
+        return 0
+
+    lax.fori_loop(0, width // 128, turn, 0)
+
+    def last_rows(i, total):
+        at = pl.ds(pl.multiple_of(i * 16, 16), 16)
+        t = tok[at, :].astype(f32)
+        inverse = lax.rsqrt(jnp.mean(t * t, -1, keepdims=True) + EPS)
+        normed = t * inverse
+        grad = dh[at, :]
+        both = grad * normed
+        scaled = both * gains[0:1, :]
+        slope = jnp.mean(scaled, -1, keepdims=True)
+        gtok[at, :] = (dx[at, :] + inverse * (grad * gains[0:1, :] - normed * slope)).astype(bf16)
+        return total + both
+
+    gain_sum = lax.fori_loop(0, rows // 16, last_rows, jnp.zeros((16, width), f32))
+    scale_sum = jnp.sum(scale_acc[...], axis=1, keepdims=True)
+    scale_row = jnp.concatenate(
+        [jnp.broadcast_to(scale_sum, (hd, 128)), jnp.zeros((128 - hd, 128), f32)], axis=0
+    ).T[0:1, :]
+    vec[0:1, :] = jnp.sum(gain_sum, axis=0, keepdims=True)
+    vec[2:3, 0:128] = scale_row
+    own_tok = pltpu.make_async_copy(gtok, gtok_out, local_sem.at[18])
+    own_tok.start()
+    for k in range(1, n_ctx):
+        g = lax.rem(c + k, n_ctx)
+        send(vec, vec_plane.at[c], vp_send.at[k], vp_recv.at[c], g, z)
+    for w in order3:
+        planes[w].from_first()
+    plane_w.from_first()
+    for w in order3:
+        planes[w].from_second()
+    plane_w.from_second()
+    total = vec[...]
+    for k in range(1, n_ctx):
+        g = lax.rem(c + k, n_ctx)
+        arrive(vec_plane.at[g], vp_send.at[0], vp_recv.at[g], c, z)
+        total = total + vec_plane[g]
+    vec_mid[...] = total
+    for k in range(1, n_wsh):
+        send(vec_mid, vec_line.at[z], vl_send.at[k], vl_recv.at[z], c, lax.rem(z + k, n_wsh))
+    for w in order3:
+        planes[w].from_diag()
+    plane_w.from_diag()
+    for k in range(1, n_wsh):
+        s = lax.rem(z + k, n_wsh)
+        arrive(vec_line.at[s], vl_send.at[0], vl_recv.at[s], c, z)
+        total = total + vec_line[s]
+    vec_sum[...] = total
+    own_vec = pltpu.make_async_copy(vec_sum, vec_out, local_sem.at[19])
+    own_vec.start()
+    for plane in planes + [plane_w]:
+        for b in plane.others():
+            plane.wait(b)
+        plane.finish()
+    for w in range(3):
+        pltpu.make_async_copy(fin3.at[w], out_piece(w, c), local_sem.at[16]).wait()
+        left(land_p.at[w], p_send.at[w], p_recv.at[w], c, z)
+        left(land_f.at[w], f_send.at[w], f_recv.at[w], c, z)
+        left(land_s.at[w], s_send.at[w], s_recv.at[w], c, z)
+        for k in range(1, n_wsh):
+            left(land_z.at[w, 0], z_send.at[w, k], z_recv.at[w, 0], c, z)
+    for k in range(1, n_ctx):
+        left(go_land.at[0], go_send.at[k], go_recv.at[0], c, z)
+        left(vec, vp_send.at[k], vp_recv.at[0], c, z)
+    for k in range(1, n_wsh):
+        left(vec, vl_send.at[k], vl_recv.at[0], c, z)
+    for s in range(n_wsh):
+
+        @pl.when(z != s)
+        def _():
+            left(win_out.at[s], w_send.at[s], w_recv.at[s], c, z)
+
+    for i in range(n_ctx // 2):
+        left(part.at[0], hp_send.at[i], hp_recv.at[i], c, z)
+    for i in range(2):
+        left(part.at[0], hf_send.at[i], hf_recv.at[i], c, z)
+    left(part.at[0], hs_send.at[0], hs_recv.at[0], c, z)
+    own_fin.wait()
+    own_tok.wait()
+    own_vec.wait()
+
+
+def backward_call(dims, go, dw3, tok, dx, vec, gain, saved):
+    n_ctx, n_wsh, hd, heads = dims
+    rows, width = tok.shape
+    span, length, shard = hd * heads, rows * n_ctx, width // n_wsh
+    half, cut = width // 2, shard // 4
+    f32, bf16 = jnp.float32, jnp.bfloat16
+    hbm = pl.BlockSpec(memory_space=pl.ANY)
+    shape = jax.ShapeDtypeStruct
+    dma = pltpu.SemaphoreType.DMA
+    vm = pltpu.VMEM
+    size = windows(width, n_wsh)[1]
+    outs = (
+        shape((rows, width), bf16),
+        shape((3, shard, width), bf16),
+        shape((n_ctx, 3 * span, size), bf16),
+        shape((8, width), f32),
+    )
+    scratch = [
+        vm((n_ctx, span, rows), bf16), vm((n_ctx, rows, width), bf16), vm(saved[1].shape, bf16),
+        vm((heads, length, 128), bf16), vm((heads, length, 128), bf16), vm((heads, hd, length), bf16),
+        vm((n_ctx, heads, 128, rows), bf16), vm((n_ctx, span, rows), f32), vm((n_ctx, span, rows), f32),
+        vm((n_ctx, heads, 128, rows), bf16), vm((heads, length, 128), bf16), vm((heads, length, 128), bf16),
+        vm((heads, length, 128), f32), vm((heads, length, 128), f32), vm((saved[1].shape[1], length), bf16),
+        vm((hd, rows), f32),
+        vm((n_wsh, 3 * span, size), bf16), vm((n_wsh, 3 * span, size), bf16), vm((3 * span, size), bf16),
+        vm((n_ctx, width, rows), bf16), vm((n_ctx // 2, width, rows), bf16), vm((2, width, rows), bf16),
+        vm((width, rows), bf16),
+        vm((3, n_wsh, shard, half), bf16), vm((3, n_wsh, shard, half), bf16), vm((3, n_wsh, 2 * cut, half), bf16),
+        vm((3, n_wsh, cut, half), bf16), vm((3, n_wsh, cut, half), bf16), vm((3, cut, half), bf16),
+        vm((rows, width), f32), vm((rows, width), f32), vm((rows, width), bf16), vm((8, width), f32),
+        vm((rows, width), bf16), vm((8, width), f32), vm((n_ctx, 8, width), f32), vm((n_wsh, 8, width), f32),
+        vm((8, width), f32), vm((8, width), f32),
+        dma((n_ctx,)), dma((n_ctx,)), dma((3,)), dma((3,)), dma((3,)), dma((3,)), dma((3,)), dma((3,)),
+        dma((3, n_wsh)), dma((3, n_wsh)), dma((3, 7)), dma((3, n_ctx)),
+        dma((n_ctx // 2,)), dma((n_ctx // 2,)), dma((2,)), dma((2,)), dma((1,)), dma((1,)),
+        dma((n_wsh,)), dma((n_wsh,)), dma((7,)), dma((n_ctx,)),
+        dma((n_ctx,)), dma((n_ctx,)), dma((n_wsh,)), dma((n_wsh,)), dma((20,)),
+    ]
+    h1, wc, kaug, vaug, kt, qaug, qraw, o = saved
+    operands = (go, *[w.reshape(n_wsh, shard, width) for w in dw3], tok, dx, vec, gain, *saved)
+    return pl.pallas_call(
+        functools.partial(backward_kernel, dims),
+        out_shape=outs,
+        in_specs=[hbm] * len(operands),
+        out_specs=[hbm] * len(outs),
+        scratch_shapes=scratch,
+        compiler_params=pltpu.CompilerParams(
+            collective_id=1, has_side_effects=True, vmem_limit_bytes=VMEM_BYTES
+        ),
+    )(*operands)
+
+
+def head_split(
+    tokens, cotangent, block_lengths, group_order, w_query, w_key, w_value, w_out, w_up, w_down,
+    gain_attn, gain_mlp, query_scale,
+):
+    f32, bf16 = jnp.float32, jnp.bfloat16
+    n_ctx, n_wsh = lax.axis_size("ctx"), lax.axis_size("wsh")
+    c, z = lax.axis_index("ctx"), lax.axis_index("wsh")
+    rows, width = tokens.shape[1:]
+    hd, heads = width // H, H // n_ctx
+    span, shard = hd * heads, width // n_wsh
+    dims = (n_ctx, n_wsh, hd, heads)
+    mine = [lax.dynamic_slice_in_dim(w, c * span, span, 1) for w in (w_query, w_key, w_value)]
+    lanes = -(-3 * span // 128) * 128
+    wqkv = jnp.pad(jnp.concatenate(mine, 1), ((0, 0), (0, lanes - 3 * span)))
+    w3 = jnp.stack([w_out, w_up, w_down])
+    lanes = -(-shard // 128) * 128
+    pack = jnp.concatenate(
+        [jnp.pad(v.astype(f32), (0, lanes - v.shape[0]))[None] for v in (gain_attn, gain_mlp, query_scale)]
+        + [jnp.zeros((5, lanes), f32)]
+    )
+    *saved, ob, full, gains = forward_call(dims, tokens[0], wqkv, w3, pack, group_order, block_lengths)
+    full_out, full_up, full_down = full[0], full[1], full[2]
+    ob = ob.reshape(width, rows)
+    inputs = tokens[0].astype(f32)
+    norm_mlp = gains[1]
+    mixed = inputs + lax.dot_general(ob, full_out, (((0,), (0,)), ((), ())), preferred_element_type=f32)
+    inverse_two = inverse_rms(mixed)
+    normed_two = mixed * inverse_two
+    hidden_two = (normed_two * norm_mlp).astype(bf16)
+    up_raw = jnp.dot(hidden_two, full_up, preferred_element_type=f32)
+    active = jax.nn.silu(up_raw).astype(bf16)
+    outputs = mixed + jnp.dot(active, full_down, preferred_element_type=f32)
+    grad_mlp = cotangent[0]
+    grad_output = grad_mlp.astype(f32)
+    grad_active = back_product(grad_mlp, full_down)
+    sigmoid_up = jax.nn.sigmoid(up_raw)
+    grad_up_raw = (grad_active * sigmoid_up * (1.0 + up_raw * (1.0 - sigmoid_up))).astype(bf16)
+    grad_hidden_two = back_product(grad_up_raw, full_up)
+    grad_gain_mlp = jnp.sum(grad_hidden_two * normed_two, 0)
+    grad_mixed = grad_output + norm_back(normed_two, inverse_two, grad_hidden_two * norm_mlp)
+    grad_branch = grad_mixed.astype(bf16)
+    go = lax.dot_general(
+        full_out, grad_branch, (((1,), (1,)), ((), ())), preferred_element_type=f32
+    ).astype(bf16)
+    dw3 = (
+        jnp.dot(ob, grad_branch, preferred_element_type=f32).astype(bf16),
+        outer_product(hidden_two, grad_up_raw).astype(bf16),
+        outer_product(active, grad_mlp).astype(bf16),
+    )
+    vec = jnp.pad(grad_gain_mlp[None], ((1, 6), (0, 0)))
+    gtok, dw3_own, dwqkv, sums = backward_call(
+        dims, go.reshape(n_ctx, span, rows), dw3, tokens[0], grad_mixed, vec, gains, saved
+    )
+    starts, size = windows(width, n_wsh)
+    at = z * shard - jnp.asarray(starts, jnp.int32)[z]
+    dwqkv = lax.dynamic_slice_in_dim(dwqkv.reshape(n_ctx, 3, span, size), at, shard, 3)
+    dwqkv = dwqkv.transpose(1, 3, 0, 2).reshape(3, shard, width).astype(f32)
+    dw3_own = dw3_own.astype(f32)
+    own = [lax.dynamic_slice_in_dim(sums[i], z * shard, shard, 0) for i in (0, 1)]
+    scale_grad = (
+        lax.dynamic_slice_in_dim(sums[2], z * (hd // n_wsh), hd // n_wsh, 0)
+        * (LOG_BASE / math.sqrt(hd))
+        * jax.nn.sigmoid(query_scale.astype(f32))
+    )
+    return (
+        outputs.reshape(tokens.shape).astype(bf16), gtok.reshape(tokens.shape),
+        dwqkv[0], dwqkv[1], dwqkv[2], dw3_own[0], dw3_own[1], dw3_own[2], own[0], own[1], scale_grad,
+    )
+
+
 def solution(mesh):
     in_specs = (
         P("wsh", "ctx", None),
@@ -321,6 +1248,8 @@
         P("wsh"),
         P("wsh"),
     )
+    n_ctx, n_wsh = mesh.shape["ctx"], mesh.shape["wsh"]
+    plan = head_split if (n_ctx, n_wsh) == (8, 4) else per_device
     return jax.shard_map(
-        per_device, mesh=mesh, in_specs=in_specs, out_specs=out_specs, check_vma=False
-    )
+        plan, mesh=mesh, in_specs=in_specs, out_specs=out_specs, check_vma=False
+    )

time: 1210 us -> 280 us (0.23)
  waiting for transfers between devices: 918 us -> 0 us
  Pallas kernels: 0 us -> 225 us
  matrix products: 113 us -> 21.4 us
  local copies, waits for them, and re-layouts: 92 us -> 19 us
  blocking collectives: 36.5 us -> 0 us
  between operations: 17.5 us -> 1.59 us
  other arithmetic: 23.1 us -> 10.6 us
    reduce_scatter x8 -> x0, waiting for transfers between devices: 461 us -> none  [the longest x1 64.7 us: per_device(): lax.psum_scatter(grad_outw.astype(jnp.bfloat16), 'wsh', scatter_dimension...]
    all_gather x8 -> x0, waiting for transfers between devices: 397 us -> none  [the longest x1 62.8 us: per_device(): lax.all_gather(w_up, 'wsh', axis=0, tiled=True)]
    pallas_call x0 -> x2, Pallas kernels: none -> 225 us  [the longest x1 129 us: backward_call(): pl.pallas_call(functools.partial(backward_kernel, dims), out_shape=outs,...]
    dot_general x34 -> x5, matrix products: 82.5 us -> 13.1 us  [the longest x1 3.43 us: head_split(): lax.dot_general(ob, full_out, (((0,), (0,)), ((), ())), preferred_element...]
    psum x1 -> x0, waiting for transfers between devices: 56.1 us -> none  [per_device(): lax.psum(owned[0].astype(jnp.bfloat16), 'ctx').astype(jnp.float32)]
    dynamic_slice x33 -> x5, local copies, waits for them, and re-layouts: 42.3 us -> 3.44 us  [the longest x2 1.51 us: head_split(): lax.dynamic_slice_in_dim(w, c * span, span, 1)]
    unnamed x2 -> x0, blocking collectives: 24.1 us -> none
    unnamed x103 -> x32, local copies, waits for them, and re-layouts: 24.3 us -> 8.05 us
  transfers between devices with their start and end apart: 17 -> 0, of which waited for: 17 -> 0; matrix products, arithmetic and copies ran while one was open for 10% -> 0% of each run, Pallas kernels for 0% -> 0%
where the time goes in v1:
time: 280 us; the launch traced here: 278 us
  Pallas kernels  225 us (80%)
  matrix products  21.4 us (8%)
  local copies, waits for them, and re-layouts  19 us (7%)
  other arithmetic  10.6 us (4%)
    pallas_call x1, Pallas kernels, backward_call(): pl.pallas_call(functools.partial(backward_kernel, dims), out_shape=outs,...  129 us
    pallas_call x1, Pallas kernels, forward_call(): pl.pallas_call(functools.partial(forward_kernel, dims), out_shape=outs, i...  96.2 us
    unnamed x32, local copies, waits for them, and re-layouts  8.05 us
    dot_general x2, matrix products, outer_product(): lax.dot_general(left, right, (((0,), (0,)), ((), ())), preferred_element_...  5.98 us

profile of v1, /device:TPU:0, one launch (start us, length us, event | category | flops | bytes accessed | tf_op | source)
XLA Modules:
  0.0 277.7 jit_solution(18124150109320395511)
XLA Ops:
  0.7 1.4 constant_dynamic-slice_fusion.4
  2.2 0.9 fusion.51.wqkv_ref
  3.2 2.8 %pad_maximum_fusion.w3_ref = bf16[3,320,1280]{2,1,0:T(8,128)(2,1)} fusion(bf16[1,320,1280]{2,1,0:T(8,128)(2,1)S(1)} %bitcast.96, bf16[1,320,1280]{2,1,0:T(8,128)(2,1)S(1)} %bitcast.97, bf16[1,320,1280]{2,1,0:T(8,128)(2,1)} %bitcast.98), kind=kLoop, calls=%fused_computation.31 | loop fusion | flops 2457600 | bytes 4915200 | tf_op jit(solution)/shard_map/stack | solution.py:1166
  6.9 96.2 %shard_map.221 = (bf16[8,256,1280]{2,1,0:T(8,128)(2,1)}, bf16[1280,512]{1,0:T(8,128)(2,1)}, bf16[2,2048,128]{2,1,0:T(8,128)(2,1)}, bf16[2,2048,128]{2,1,0:T(8,12...) custom-call(bf16[256,1280]{1,0:T(8,128)(2,1)} %bitcast.92, ...), custom_call_target="tpu_custom_call" | custom-call | tf_op jit(solution)/shard_map/pallas_call | solution.py:735
  103.1 3.4 %multiply_reduce_fusion.2 = (f32[256]{0:T(256)S(1)}, f32[256,1280]{1,0:T(8,128)S(1)}) fusion(bf16[1280,256]{1,0:T(8,128)(2,1)} %bitcast.94, bf16[3,1280,1280]{2,1,0:T(8,128)(2,1)} %get-tuple-element.27, bf16[1,256,1280]{2,1,0:T(8,128)(2,1)S(1)} %copy-done.3), kind=kOutput, calls=%fused_computation.41 | convolution fusion | flops 840171264 | bytes 5899264 | tf_op jit(solution)/shard_map/dot_general | solution.py:1177
  106.5 1.3 slice_reduce_fusion
  107.9 3.0 %fusion.6 = f32[256,1280]{1,0:T(8,128)S(1)} fusion(bf16[3,1280,1280]{2,1,0:T(8,128)(2,1)} %get-tuple-element.27, f32[256,1280]{1,0:T(8,128)S(1)} %get-tuple-element.64, f32[1280]{0:T(1024)S(1)} %slice_reduce_fusion, f32[256]{0:T(256)S(1)} %add_rsqrt_fusion), kind=kOutput, calls=%fused_computation.10 | convolution fusion | flops 839843840 | bytes 5904384 | tf_op jit(solution)/shard_map/dot_general | solution.py:1181
  110.9 2.0 fusion.42
  113.0 1.1 fusion.39
  114.1 1.2 multiply_reduce_fusion
  115.7 1.9 fusion.33
  117.7 2.7 convolution_convert_fusion.2
  120.3 2.9 %convolution_convert_fusion.1 = bf16[1280,1280]{1,0:T(8,128)(2,1)} fusion(bf16[256,1280]{1,0:T(8,128)(2,1)S(1)} %fusion.39, f32[256,1280]{1,0:T(8,128)S(1)} %get-tuple-element.64, f32[1280]{0:T(1024)S(1)} %slice_reduce_fusion, f32[256]{0:T(256)S(1)} %add_rsqrt_fusion), kind=kOutput, calls=%fused_computation.1 | convolution fusion | flops 841482240 | bytes 5249024 | tf_op jit(solution)/shard_map/dot_general | solution.py:39
  123.2 3.1 %convolution_convert_fusion = bf16[1280,1280]{1,0:T(8,128)(2,1)} fusion(bf16[1,256,1280]{2,1,0:T(8,128)(2,1)S(1)} %copy-done.8, f32[256,1280]{1,0:T(8,128)S(1)} %fusion.6), kind=kOutput, calls=%fused_computation | convolution fusion | flops 842137600 | bytes 5242880 | tf_op jit(solution)/shard_map/dot_general | solution.py:39
  127.0 128.9 %shard_map.222 = (bf16[256,1280]{1,0:T(8,128)(2,1)}, bf16[3,320,1280]{2,1,0:T(8,128)(2,1)}, bf16[8,480,384]{2,1,0:T(8,128)(2,1)}, f32[8,1280]{1,0:T(8,128)}) custom-call(bf16[8,160,256]{2,1,0:T(8,128)(2,1)} %bitcast.99, bf16[4,320,1280]{2,1,0:T(8,128)(2,1)} %bitcast.85, bf16[4,320,1280]{2,1,0:T(8,128)(2,1)} %bitcast.86, bf16[4,320,1280]{2,1,0:T(8,128)(2,1)} %bitcast.90, ...), custom_call_target="tpu_custom_call" | custom-call | tf_op jit(solution)/shard_map/pallas_call | solution.py:1140
  257.2 3.0 %convert_bitcast_fusion = f32[3,320,8,160]{1,3,2,0:T(8,128)S(1)} fusion(bf16[8,3,160,384]{3,2,1,0:T(8,128)(2,1)} %bitcast.91, s32[]{:T(128)S(6)} %select_n.20), kind=kLoop, calls=%fused_computation.3 | loop fusion | flops 1228800 | bytes 7864324 | tf_op jit(solution)/shard_map/convert_element_type | solution.py:1208
  260.2 2.2 fusion.58
  262.4 2.7 copy.31
  265.2 2.7 copy.32
  267.9 1.7 copy.33
  269.6 2.1 convert_element_type.76
  271.7 2.4 slice_bitcast_fusion
  274.1 0.9 fusion.59
  276.9 0.8 copy.38
  (47 shorter events, 4.5 us)
Async XLA Ops:
  0.6 1.4 copy-start
  0.7 2.5 copy-start.5
  0.7 2.5 copy-start.6
  3.2 2.9 %copy-start.9 = (bf16[20]{0:T(256)(128)(2,1)S(1)}, bf16[20]{0:T(256)(128)(2,1)}, u32[]{:S(2)}) copy-start(bf16[20]{0:T(256)(128)(2,1)} %param.26) | copy-start | bytes 124
  3.2 2.9 %copy-start.10 = (bf16[320]{0:T(512)(128)(2,1)S(1)}, bf16[320]{0:T(512)(128)(2,1)}, u32[]{:S(2)}) copy-start(bf16[320]{0:T(512)(128)(2,1)} %param.25) | copy-start | bytes 1924
  3.2 2.9 %copy-start.11 = (bf16[320]{0:T(512)(128)(2,1)S(1)}, bf16[320]{0:T(512)(128)(2,1)}, u32[]{:S(2)}) copy-start(bf16[320]{0:T(512)(128)(2,1)} %param.24) | copy-start | bytes 1924
  6.9 96.2 %copy-start.3 = (bf16[1,256,1280]{2,1,0:T(8,128)(2,1)S(1)}, bf16[1,256,1280]{2,1,0:T(8,128)(2,1)}, u32[]{:S(2)}) copy-start(bf16[1,256,1280]{2,1,0:T(8,128)(2,1)} %param.14) | copy-start | bytes 1966084
  103.1 7.8 %copy-start.12 = (bf16[3,1280,1280]{2,1,0:T(8,128)(2,1)S(1)}, bf16[3,1280,1280]{2,1,0:T(8,128)(2,1)}, u32[]{:S(2)}) copy-start(bf16[3,1280,1280]{2,1,0:T(8,128)(2,1)} %get-tuple-element.27) | copy-start | bytes 29491204
  110.9 2.1 copy-start.8
  115.7 1.9 copy-start.2
  115.7 1.9 copy-start.4
  127.0 129.0 %copy-start.13 = (s32[4]{0:T(128)S(1)}, s32[4]{0:T(128)}, u32[]{:S(2)}) copy-start(s32[4]{0:T(128)} %constant.48.clone) | copy-start | bytes 52
  271.7 5.2 %copy-start.7 = (bf16[256,1280]{1,0:T(8,128)(2,1)S(1)}, bf16[256,1280]{1,0:T(8,128)(2,1)}, u32[]{:S(2)}) copy-start(bf16[256,1280]{1,0:T(8,128)(2,1)} %get-tuple-element.37) | copy-start | bytes 1966084
  271.7 6.0 %copy-start.1 = (bf16[320,1280]{1,0:T(8,128)(2,1)S(1)}, bf16[320,1280]{1,0:T(8,128)(2,1)}, u32[]{:S(2)}) copy-start(bf16[320,1280]{1,0:T(8,128)(2,1)} %param.18) | copy-start | bytes 2457604

commit v2 on v0

--- a/solution.py
+++ b/solution.py
@@ -1,8 +1,11 @@
+import functools
 import math
 
 import jax
 import jax.numpy as jnp
 from jax import lax
+from jax.experimental import pallas as pl
+from jax.experimental.pallas import tpu as pltpu
 from jax.sharding import PartitionSpec as P
 
 H = 16
@@ -292,6 +295,1011 @@
     )
 
 
+MESH = pl.DeviceIdType.MESH
+NEG = -1e30
+VMEM_BYTES = 60 * 1024 * 1024
+
+
+def place():
+    c, z = lax.axis_index("ctx"), lax.axis_index("wsh")
+    core, x, y = lax.rem(c, 2), lax.rem(c // 2, 2), c // 4
+    sib = c + 1 - 2 * core
+    over_x, over_y = c + 2 - 4 * x, c + 4 - 8 * y
+    first = over_x * (1 - core) + over_y * core
+    second = over_y * (1 - core) + over_x * core
+    diag = over_x + over_y - c
+    return c, z, sib, first, second, diag
+
+
+def enter(c, z, n_ctx, n_wsh):
+    barrier = pltpu.get_barrier_semaphore()
+    for k in range(1, n_ctx):
+        pl.semaphore_signal(
+            barrier, inc=1, device_id=(lax.rem(c + k, n_ctx), z), device_id_type=MESH
+        )
+    for k in range(1, n_wsh):
+        pl.semaphore_signal(
+            barrier, inc=1, device_id=(c, lax.rem(z + k, n_wsh)), device_id_type=MESH
+        )
+    pl.semaphore_wait(barrier, n_ctx + n_wsh - 2)
+
+
+def send(src, dst, send_sem, recv_sem, c, z):
+    copy = pltpu.make_async_remote_copy(
+        src_ref=src, dst_ref=dst, send_sem=send_sem, recv_sem=recv_sem,
+        device_id=(c, z), device_id_type=MESH,
+    )
+    copy.start()
+    return copy
+
+
+def arrive(dst, send_sem, recv_sem, c, z):
+    pltpu.make_async_remote_copy(
+        src_ref=dst, dst_ref=dst, send_sem=send_sem, recv_sem=recv_sem,
+        device_id=(c, z), device_id_type=MESH,
+    ).wait_recv()
+
+
+def left(src, send_sem, recv_sem, c, z):
+    pltpu.make_async_remote_copy(
+        src_ref=src, dst_ref=src, send_sem=send_sem, recv_sem=recv_sem,
+        device_id=(c, z), device_id_type=MESH,
+    ).wait_send()
+
+
+class Line:
+    def __init__(self, at, c, z, n, send_sem, recv_sem):
+        self.at, self.c, self.z, self.n = at, c, z, n
+        self.send_sem, self.recv_sem = send_sem, recv_sem
+
+    def start(self, own):
+        c, z = self.c, self.z
+
+        @pl.when(z < self.n - 1)
+        def _():
+            send(own, self.at(z), self.send_sem.at[0], self.recv_sem.at[z], c, z + 1)
+
+        @pl.when(z > 0)
+        def _():
+            send(own, self.at(z), self.send_sem.at[1], self.recv_sem.at[z], c, z - 1)
+
+    def forward(self, distance, then=None):
+        c, z, n = self.c, self.z, self.n
+        below, above = z - distance, z + distance
+
+        @pl.when(below >= 0)
+        def _():
+            arrive(self.at(below), self.send_sem.at[0], self.recv_sem.at[below], c, z)
+
+            @pl.when(z < n - 1)
+            def _():
+                send(self.at(below), self.at(below), self.send_sem.at[2 * distance], self.recv_sem.at[below], c, z + 1)
+
+            if then is not None:
+                then(below)
+
+        @pl.when(above < n)
+        def _():
+            arrive(self.at(above), self.send_sem.at[0], self.recv_sem.at[above], c, z)
+
+            @pl.when(z > 0)
+            def _():
+                send(self.at(above), self.at(above), self.send_sem.at[2 * distance + 1], self.recv_sem.at[above], c, z - 1)
+
+            if then is not None:
+                then(above)
+
+    def finish(self, own):
+        c, z, n = self.c, self.z, self.n
+
+        @pl.when(z < n - 1)
+        def _():
+            left(own, self.send_sem.at[0], self.recv_sem.at[z], c, z)
+
+        @pl.when(z > 0)
+        def _():
+            left(own, self.send_sem.at[1], self.recv_sem.at[z], c, z)
+
+        for distance in range(1, n):
+            below, above = z - distance, z + distance
+
+            @pl.when((below >= 0) & (z < n - 1))
+            def _():
+                left(self.at(below), self.send_sem.at[2 * distance], self.recv_sem.at[below], c, z)
+
+            @pl.when((above < n) & (z > 0))
+            def _():
+                left(self.at(above), self.send_sem.at[2 * distance + 1], self.recv_sem.at[above], c, z)
+
+
+class Plane:
+    def __init__(self, at, c, z, around, send_sem, recv_sem):
+        self.at, self.c, self.z = at, c, z
+        self.sib, self.first, self.second, self.diag = around
+        self.send_sem, self.recv_sem = send_sem, recv_sem
+
+    def push(self, slot, block, target, src=None):
+        src = self.at(block) if src is None else src
+        send(src, self.at(block), self.send_sem.at[slot], self.recv_sem.at[block], target, self.z)
+
+    def wait(self, block):
+        arrive(self.at(block), self.send_sem.at[0], self.recv_sem.at[block], self.c, self.z)
+
+    def start(self, own=None):
+        self.push(0, self.c, self.first, own)
+        self.push(1, self.c, self.second, own)
+        self.push(2, self.c, self.sib, own)
+
+    def from_first(self):
+        self.wait(self.first)
+        self.push(3, self.first, self.second)
+        self.push(4, self.first, self.sib)
+
+    def from_second(self):
+        self.wait(self.second)
+        self.push(5, self.second, self.sib)
+
+    def from_diag(self):
+        self.wait(self.diag)
+        self.push(6, self.diag, self.sib)
+
+    def others(self):
+        shift = self.sib - self.c
+        return (self.sib, self.second + shift, self.first + shift, self.diag + shift)
+
+    def finish(self):
+        for slot in range(7):
+            left(self.at(self.c), self.send_sem.at[slot], self.recv_sem.at[self.c], self.c, self.z)
+
+
+def block_ids_of(block, order_ref, lengths_ref, rows):
+    n_blk = lengths_ref.shape[1]
+    position = order_ref[block] * rows + lax.broadcasted_iota(jnp.int32, (8, rows), 1)
+    ids = jnp.zeros((8, rows), jnp.int32)
+    bound = jnp.int32(0)
+    for b in range(n_blk):
+        bound = bound + lengths_ref[0, b]
+        ids = ids + jnp.where(position >= bound, 1, 0)
+    return ids, lax.broadcasted_iota(jnp.int32, (8, rows), 0)
+
+
+def three_rows(value, rows):
+    f32 = jnp.float32
+    high = value.astype(jnp.bfloat16).astype(f32)
+    rest = value - high
+    mid = rest.astype(jnp.bfloat16).astype(f32)
+    low = rest - mid
+    row = lax.broadcasted_iota(jnp.int32, (8, rows), 0)
+    return jnp.where(row == 0, high, 0.0) + jnp.where(row == 1, mid, 0.0) + jnp.where(row == 2, low, 0.0)
+
+
+def add_rows(target, index, at, other, other_index, other_at, rows, step=16):
+    f32 = jnp.float32
+
+    def some_rows(i, _):
+        here = pl.ds(pl.multiple_of(at + i * step, 16), step)
+        there = pl.ds(pl.multiple_of(other_at + i * step, 16), step)
+        left_part = target[index + (here, slice(None))].astype(f32)
+        right_part = other[other_index + (there, slice(None))].astype(f32)
+        target[index + (here, slice(None))] = (left_part + right_part).astype(target.dtype)
+        return 0
+
+    lax.fori_loop(0, rows // step, some_rows, 0)
+
+
+def windows(width, n):
+    part = width // n
+    tiles = -(-part // 128) + (0 if part % 128 == 0 else 0)
+    size = tiles * 128
+    return [min(s * part // 128 * 128, width - size) for s in range(n)], size
+
+
+def whole_kernel(
+    dims,
+    tok_ref, cot_ref, wqkv_ref, wout_ref, wup_ref, wdown_ref, pack_ref, order_ref, lengths_ref,
+    out_out, gtok_out, dwo_out, dwu_out, dwd_out, dwqkv_out, vec_out,
+    tok_hbm, w_hbm, h1_hbm, land_p,
+    w_c, packs, gains, kaug, vaug, kt, qaug, qraw, o_all, ob_stage, ob_land, go_stage, go_land,
+    acc, land_f, land_s, land_z, fin3, win_out, win_land, fin_qkv, part_p, part_f, part_s,
+    dx, dh, tok, cot, gtok, vec, vec_plane, vec_line, vec_mid, vec_sum, scale_acc,
+    tok_send, tok_recv, wz_send, wz_recv, pk_send, pk_recv, ob_send, ob_recv,
+    w3z_send, w3z_recv, w3p_send, w3p_recv,
+    go_send, go_recv, p_send, p_recv, f_send, f_recv, s_send, s_recv, z_send, z_recv, g_send, g_recv,
+    hp_send, hp_recv, hf_send, hf_recv, hs_send, hs_recv, w_send, w_recv, wg_send, wg_recv,
+    vp_send, vp_recv, vl_send, vl_recv, local_sem, norm_sem, load_sem,
+):
+    n_ctx, n_wsh, hd, heads = dims
+    f32, bf16 = jnp.float32, jnp.bfloat16
+    c, z, sib, first, second, diag = place()
+    around = (sib, first, second, diag)
+    core, x, y = lax.rem(c, 2), lax.rem(c // 2, 2), c // 4
+    f_bit, s_bit = x * (1 - core) + y * core, y * (1 - core) + x * core
+    rows, width = tok_ref.shape
+    span, length = hd * heads, rows * n_ctx
+    shard, half = width // n_wsh, width // 2
+    two, cut = shard // 2, shard // (n_ctx // 2)
+    w3_refs = (wout_ref, wup_ref, wdown_ref)
+    OUT, UP, DOWN = 0, 1, 2
+    from_first, from_second, from_diag = Plane.from_first, Plane.from_second, Plane.from_diag
+    enter(c, z, n_ctx, n_wsh)
+
+    part_rows = rows // 2
+    tokens = [
+        Plane(
+            lambda b, i=i: tok_hbm.at[b, pl.ds(i * part_rows, part_rows)], c, z, around,
+            tok_send.at[i], tok_recv.at[i],
+        )
+        for i in range(2)
+    ]
+    for i in range(2):
+        tokens[i].start(tok_ref.at[pl.ds(i * part_rows, part_rows)])
+    wline = Line(lambda s: w_c.at[pl.ds(pl.multiple_of(s * shard, 16), shard)], c, z, n_wsh, wz_send, wz_recv)
+    for k in range(1, n_wsh):
+        send(pack_ref, packs.at[z], pk_send.at[k], pk_recv.at[z], c, lax.rem(z + k, n_wsh))
+    wline.start(wqkv_ref)
+    own_tok = pltpu.make_async_copy(tok_ref, tok, local_sem.at[0])
+    own_w = pltpu.make_async_copy(wqkv_ref, wline.at(z), local_sem.at[1])
+    own_pack = pltpu.make_async_copy(pack_ref, packs.at[z], local_sem.at[2])
+    own_cot = pltpu.make_async_copy(cot_ref, cot, local_sem.at[3])
+    for copy in (own_tok, own_pack, own_w, own_cot):
+        copy.start()
+    vec[...] = jnp.zeros_like(vec)
+    scale_acc[...] = jnp.zeros_like(scale_acc)
+
+    def columns(b):
+        return pl.ds(pl.multiple_of(lax.rem(b, 2) * half, 128), half)
+
+    def piece(w, s, b):
+        top = pl.multiple_of(s * shard + (b // 2) * cut, 16)
+        return w_hbm.at[w, pl.ds(top, cut), columns(b)]
+
+    my_piece = [ref.at[pl.ds(pl.multiple_of((c // 2) * cut, 16), cut), columns(c)] for ref in w3_refs]
+    lines = [
+        Line(lambda s, w=w: piece(w, s, c), c, z, n_wsh, w3z_send.at[w], w3z_recv.at[w]) for w in range(3)
+    ]
+
+    def plane_of(w, s):
+        k = lax.rem(s - z + n_wsh, n_wsh)
+        return Plane(lambda b: piece(w, s, b), c, z, around, w3p_send.at[w, k], w3p_recv.at[w, k])
+
+    def shards_at(distance, step, weights=(0, 1, 2)):
+        below, above = z - distance, z + distance
+
+        @pl.when(below >= 0)
+        def _():
+            for w in weights:
+                step(plane_of(w, below))
+
+        @pl.when(above < n_wsh)
+        def _():
+            for w in weights:
+                step(plane_of(w, above))
+
+    def spread(distance):
+        for w in range(3):
+            lines[w].forward(distance, lambda s, w=w: plane_of(w, s).start())
+
+    def all_others(plane):
+        for b in plane.others():
+            plane.wait(b)
+
+    own_tok.wait()
+    own_pack.wait()
+    for k in range(1, n_wsh):
+        other = lax.rem(z + k, n_wsh)
+        arrive(packs.at[other], pk_send.at[0], pk_recv.at[other], c, z)
+    row8 = lax.broadcasted_iota(jnp.int32, (8, width), 0)
+    total = jnp.zeros((8, width), f32)
+    for s in range(n_wsh):
+        wide = jnp.concatenate([packs[s], jnp.zeros((8, width - packs.shape[2]), f32)], axis=1)
+        by_shard = pltpu.roll(wide, s * shard, 1) if s else wide
+        by_dim = pltpu.roll(wide, s * (hd // n_wsh), 1) if s else wide
+        total = total + jnp.where(row8 < 2, by_shard, by_dim)
+    gains[...] = total
+
+    def gain_column():
+        scale = jnp.concatenate([gains[2:3, 0:128], jnp.zeros((7, 128), f32)], axis=0)
+        soft = jnp.maximum(scale, 0.0) + jnp.log(1.0 + jnp.exp(-jnp.abs(scale)))
+        return (LOG_BASE / math.sqrt(hd) * soft).T[0:hd, 0:1]
+
+    def attention_forward(h1_all, tok_buf, vt, qneg, s_buf):
+        def load(slot, b):
+            return pltpu.make_async_copy(tok_hbm.at[b], tok_buf.at[slot], load_sem.at[slot])
+
+        def norm_block(b, source):
+            gain = gains[0:1, :]
+
+            def some_rows(i, _):
+                at = pl.ds(pl.multiple_of(i * 32, 32), 32)
+                t = source[at, :].astype(f32)
+                inverse = lax.rsqrt(jnp.mean(t * t, -1, keepdims=True) + EPS)
+                h1_all[b, at, :] = (t * inverse * gain).astype(bf16)
+                return 0
+
+            lax.fori_loop(0, rows // 32, some_rows, 0)
+            pltpu.make_async_copy(h1_all.at[b], h1_hbm.at[b], norm_sem.at[0]).start()
+
+        def arrived(b):
+            for i in range(2):
+                tokens[i].wait(b)
+
+        def norm_loaded(slot, b):
+            load(slot, b).wait()
+            norm_block(b, tok_buf.at[slot])
+
+        others = tokens[0].others()
+        norm_block(c, tok)
+        arrived(others[0])
+        load(0, others[0]).start()
+        tokens[0].from_first()
+        norm_loaded(0, others[0])
+        wline.forward(1)
+        tokens[1].from_first()
+        load(1, first).start()
+        tokens[0].from_second()
+        norm_loaded(1, first)
+        tokens[1].from_second()
+        load(0, second).start()
+        norm_loaded(0, second)
+        wline.forward(2)
+        for w in range(3):
+            lines[w].start(my_piece[w])
+        arrived(others[1])
+        load(1, others[1]).start()
+        norm_loaded(1, others[1])
+        arrived(others[2])
+        load(0, others[2]).start()
+        norm_loaded(0, others[2])
+        tokens[0].from_diag()
+        tokens[1].from_diag()
+        load(1, diag).start()
+        norm_loaded(1, diag)
+        arrived(others[3])
+        load(0, others[3]).start()
+        norm_loaded(0, others[3])
+        wline.forward(3)
+        own_w.wait()
+        spread(1)
+        gain_col = gain_column()
+
+        def project(b, _):
+            raw = jnp.dot(h1_all[b], w_c[...], preferred_element_type=f32).T
+            at = pl.ds(pl.multiple_of(b * rows, 128), rows)
+            ids, row = block_ids_of(b, order_ref, lengths_ref, rows)
+            hot = jnp.where(ids == row, 1.0, 0.0)
+            neg = jnp.where(row > ids, NEG, 0.0)
+            ones = jnp.ones((8, rows), f32)
+            qneg[b] = neg
+            qraw[b] = raw[0:span]
+            for h in range(heads):
+                q = raw[h * hd : (h + 1) * hd] * gain_col
+                qaug[b, h, 0:hd, :] = q.astype(bf16)
+                qaug[b, h, hd : hd + 16, :] = jnp.concatenate([neg, jnp.zeros((8, rows), f32)], axis=0).astype(bf16)
+                qaug[b, h, hd + 16 : 128, :] = jnp.zeros((112 - hd, rows), bf16)
+                k = raw[span + h * hd : span + (h + 1) * hd].astype(bf16)
+                v = raw[2 * span + h * hd : 2 * span + (h + 1) * hd].astype(bf16)
+                tail = jnp.zeros((112 - hd, rows), f32)
+                kt[h, :, at] = k
+                vt[h, 0:hd, at] = v
+                vt[h, hd : hd + 16, at] = jnp.ones((16, rows), bf16)
+                kaug[h, at, :] = jnp.concatenate([k.astype(f32), hot, ones, tail], axis=0).T.astype(bf16)
+                vaug[h, at, :] = jnp.concatenate([v.astype(f32), ones, ones, tail], axis=0).T.astype(bf16)
+            return 0
+
+        lax.fori_loop(0, n_ctx, project, 0)
+        keys = length // 2
+        events = (
+            ((0, lambda: spread(2)), (2, lambda: shards_at(1, from_first)), (4, lambda: shards_at(1, from_second))),
+            ((3, lambda: spread(3)), (5, lambda: shards_at(2, from_first)), (6, lambda: shards_at(1, from_diag))),
+        )
+
+        def attend(i, _):
+            g = lax.rem(c + 1 + i, n_ctx)
+            for h in range(heads):
+                q = qaug[g, h]
+                top = jnp.full((1, rows), -jnp.inf, f32)
+                for j in range(2):
+                    s = jnp.dot(kaug[h, j * keys : (j + 1) * keys, :], q, preferred_element_type=f32)
+                    s_buf[j * keys : (j + 1) * keys, :] = s
+                    top = jnp.maximum(top, jnp.max(s, axis=0, keepdims=True))
+                out = jnp.zeros((hd + 16, rows), f32)
+                for j in range(2):
+                    p = jnp.exp(s_buf[j * keys : (j + 1) * keys, :] - top).astype(bf16)
+                    out = out + jnp.dot(vt[h, :, j * keys : (j + 1) * keys], p, preferred_element_type=f32)
+                total = out[hd : hd + 1]
+                o = out[0:hd] / total
+                lse = top + jnp.log(total)
+                o_all[g, h * hd : (h + 1) * hd, :] = o
+                ob_stage[g, h * hd : (h + 1) * hd, :] = o.astype(bf16)
+                qaug[g, h, hd : hd + 16, :] = jnp.concatenate([qneg[g], three_rows(-lse, rows)], axis=0).astype(bf16)
+                for step, event in events[h]:
+                    pl.when(i == step)(event)
+
+            @pl.when(i < n_ctx - 1)
+            def _():
+                send(ob_stage.at[g], my_heads(ob_land), ob_send.at[g], ob_recv.at[c], g, z)
+
+            return 0
+
+        lax.fori_loop(0, n_ctx, attend, 0)
+        for b in range(n_ctx):
+            pltpu.make_async_copy(h1_all.at[b], h1_hbm.at[b], norm_sem.at[0]).wait()
+
+    def my_heads(ref):
+        return ref.at[pl.ds(pl.multiple_of(c * span, 16), span)]
+
+    def heads_of(ref, g):
+        return ref.at[pl.ds(pl.multiple_of(g * span, 16), span)]
+
+    vm = pltpu.VMEM
+    pl.run_scoped(
+        attention_forward,
+        vm((n_ctx, rows, width), bf16), vm((2, rows, width), bf16), vm((heads, hd + 16, length), bf16),
+        vm((n_ctx, 8, rows), f32), vm((length, rows), f32),
+    )
+    own_o = pltpu.make_async_copy(ob_stage.at[c], my_heads(ob_land), local_sem.at[4])
+    own_o.start()
+
+    mine = pl.ds(pl.multiple_of(core * half, 128), half)
+    theirs = pl.ds(pl.multiple_of((1 - core) * half, 128), half)
+    my_top = f_bit * two + s_bit * cut
+    dw_outs = (dwo_out, dwu_out, dwd_out)
+
+    def pair_sum(w, tmp):
+        arrive(land_p.at[w], p_send.at[w], p_recv.at[w], c, z)
+        copies = [
+            pltpu.make_async_copy(land_p.at[w, s], tmp.at[s % 2], load_sem.at[s % 2]) for s in range(n_wsh)
+        ]
+        copies[0].start()
+        for s in range(n_wsh):
+            copies[s].wait()
+            if s + 1 < n_wsh:
+                copies[s + 1].start()
+            add_rows(acc, (w, s), 0, tmp, (s % 2,), 0, shard, 64)
+        at = pl.ds(pl.multiple_of((1 - f_bit) * two, 16), two)
+        send(acc.at[w, :, at], land_f.at[w], f_send.at[w], f_recv.at[w], first, z)
+
+    def first_sum(w):
+        arrive(land_f.at[w], f_send.at[w], f_recv.at[w], c, z)
+        for s in range(n_wsh):
+            add_rows(acc, (w, s), f_bit * two, land_f, (w, s), 0, two, 80)
+        at = pl.ds(pl.multiple_of(f_bit * two + (1 - s_bit) * cut, 16), cut)
+        send(acc.at[w, :, at], land_s.at[w], s_send.at[w], s_recv.at[w], second, z)
+
+    def second_sum(w):
+        arrive(land_s.at[w], s_send.at[w], s_recv.at[w], c, z)
+        for s in range(n_wsh):
+            add_rows(acc, (w, s), my_top, land_s, (w, s), 0, cut, 80)
+        at = pl.ds(pl.multiple_of(my_top, 16), cut)
+        for k in range(1, n_wsh):
+            s = lax.rem(z + k, n_wsh)
+            send(acc.at[w, s, at], land_z.at[w, z], z_send.at[w, k], z_recv.at[w, z], c, s)
+
+    def out_piece(w, b):
+        b_core, b_x, b_y = lax.rem(b, 2), lax.rem(b // 2, 2), b // 4
+        r = (1 - b_core) * (2 * b_x + b_y) + b_core * (2 * b_y + b_x)
+        return dw_outs[w].at[pl.ds(pl.multiple_of(r * cut, 16), cut), columns(b)]
+
+    planes = [
+        Plane(lambda b, w=w: out_piece(w, b), c, z, around, g_send.at[w], g_recv.at[w]) for w in range(3)
+    ]
+
+    def line_sum(w):
+        for k in range(1, n_wsh):
+            s = lax.rem(z + k, n_wsh)
+            arrive(land_z.at[w, s], z_send.at[w, 0], z_recv.at[w, s], c, z)
+
+        def some_rows(i, _):
+            at = pl.ds(pl.multiple_of(i * 16, 16), 16)
+            total = acc[w, z, pl.ds(pl.multiple_of(my_top + i * 16, 16), 16), :].astype(f32)
+            for k in range(1, n_wsh):
+                total = total + land_z[w, lax.rem(z + k, n_wsh), at, :].astype(f32)
+            fin3[w, at, :] = total.astype(bf16)
+            return 0
+
+        lax.fori_loop(0, cut // 16, some_rows, 0)
+        planes[w].start(fin3.at[w])
+        pltpu.make_async_copy(fin3.at[w], out_piece(w, c), local_sem.at[8 + w]).start()
+
+    def feed_forward(w_full, x1, h2, a, gu, ob, turned, ga, inv2, outb, stage, tmp):
+        def load(w, k):
+            at = pl.ds(pl.multiple_of(lax.rem(z + k, n_wsh) * shard, 16), shard)
+            source = w_hbm.at[w, at] if k else w3_refs[w]
+            return pltpu.make_async_copy(source, w_full.at[w, at], load_sem.at[2 + n_wsh * w + k])
+
+        def whole(w):
+            for k in range(1, n_wsh):
+                load(w, k).start()
+
+        def ready(w):
+            for k in range(n_wsh):
+                load(w, k).wait()
+
+        def tiles(step, size=256):
+            def one(i, _):
+                step(pl.ds(pl.multiple_of(i * size, size), size))
+                return 0
+
+            lax.fori_loop(0, width // size, one, 0)
+
+        def turn(source, target):
+            def one(at):
+                target[at, :] = source[:, at].T
+
+            tiles(one, 128)
+
+        def weight_gradient(w, left_t, right):
+            for s in range(n_wsh):
+                at = slice(s * shard, (s + 1) * shard)
+                stage[w, s] = jnp.dot(left_t[at, :], right[:, theirs], preferred_element_type=f32).astype(bf16)
+            send(stage.at[w], land_p.at[w], p_send.at[w], p_recv.at[w], sib, z)
+            for s in range(n_wsh):
+                at = slice(s * shard, (s + 1) * shard)
+                acc[w, s] = jnp.dot(left_t[at, :], right[:, mine], preferred_element_type=f32).astype(bf16)
+
+        for w in range(3):
+            load(w, 0).start()
+        shards_at(3, from_first, (OUT,))
+        shards_at(2, from_second, (OUT,))
+        shards_at(3, from_second, (OUT,))
+        shards_at(2, from_diag, (OUT,))
+        shards_at(3, from_diag, (OUT,))
+        shards_at(3, from_first, (UP, DOWN))
+        shards_at(2, from_second, (UP, DOWN))
+        for distance in range(1, n_wsh):
+            shards_at(distance, all_others, (OUT,))
+        whole(OUT)
+        own_o.wait()
+        for k in range(1, n_ctx):
+            g = lax.rem(c + k, n_ctx)
+            arrive(heads_of(ob_land, g), ob_send.at[0], ob_recv.at[g], c, z)
+
+        def turn_ob(at):
+            ob[:, at] = ob_land[at, :].T
+
+        tiles(turn_ob, 128)
+        shards_at(3, from_second, (UP, DOWN))
+        shards_at(2, from_diag, (UP, DOWN))
+        ready(OUT)
+
+        def mix(at):
+            x1[:, at] = tok[:, at].astype(f32) + jnp.dot(ob[...], w_full[OUT, :, at], preferred_element_type=f32)
+
+        tiles(mix)
+        shards_at(3, from_diag, (UP, DOWN))
+        for distance in range(1, n_wsh):
+            shards_at(distance, all_others, (UP, DOWN))
+        whole(UP)
+        whole(DOWN)
+
+        def norm_rows(i, _):
+            at = pl.ds(pl.multiple_of(i * 32, 32), 32)
+            t = x1[at, :]
+            inverse = lax.rsqrt(jnp.mean(t * t, -1, keepdims=True) + EPS)
+            inv2[at, :] = jnp.broadcast_to(inverse, (32, 128))
+            h2[at, :] = (t * inverse * gains[1:2, :]).astype(bf16)
+            return 0
+
+        lax.fori_loop(0, rows // 32, norm_rows, 0)
+        own_cot.wait()
+        ready(UP)
+        ready(DOWN)
+
+        def hidden(at):
+            up = jnp.dot(h2[...], w_full[UP, :, at], preferred_element_type=f32)
+            da = lax.dot_general(
+                cot[...], w_full[DOWN, at, :], (((1,), (1,)), ((), ())), preferred_element_type=f32
+            )
+            sig = 1.0 / (1.0 + jnp.exp(-up))
+            act = up * sig
+            a[:, at] = act.astype(bf16)
+            turned[at, :] = act.T.astype(bf16)
+            gu[:, at] = (da * sig * (1.0 + up * (1.0 - sig))).astype(bf16)
+
+        tiles(hidden)
+        weight_gradient(DOWN, turned, cot)
+
+        def back(at):
+            dh[:, at] = lax.dot_general(
+                gu[...], w_full[UP, at, :], (((1,), (1,)), ((), ())), preferred_element_type=f32
+            )
+
+        tiles(back)
+
+        def norm_back_rows(i, total):
+            at = pl.ds(pl.multiple_of(i * 16, 16), 16)
+            inverse = inv2[at, 0:1]
+            normed = x1[at, :] * inverse
+            grad = dh[at, :]
+            both = grad * normed
+            slope = jnp.mean(both * gains[1:2, :], -1, keepdims=True)
+            result = cot[at, :].astype(f32) + inverse * (grad * gains[1:2, :] - normed * slope)
+            dx[at, :] = result
+            ga[at, :] = result.astype(bf16)
+            return total + both
+
+        gain_sum = lax.fori_loop(0, rows // 16, norm_back_rows, jnp.zeros((16, width), f32))
+        vec[1:2, :] = jnp.sum(gain_sum, axis=0, keepdims=True)
+
+        def back_out(at):
+            go_stage[at, :] = lax.dot_general(
+                w_full[OUT, at, :], ga[...], (((1,), (1,)), ((), ())), preferred_element_type=f32
+            ).astype(bf16)
+
+        tiles(back_out)
+        for k in range(1, n_ctx):
+            g = lax.rem(c + k, n_ctx)
+            send(heads_of(go_stage, g), go_land.at[c], go_send.at[k], go_recv.at[c], g, z)
+        pltpu.make_async_copy(my_heads(go_stage), go_land.at[c], local_sem.at[5]).start()
+        pair_sum(DOWN, tmp)
+        turn(h2, turned)
+        weight_gradient(UP, turned, gu)
+        weight_gradient(OUT, ob_land, ga)
+
+        def finish(at):
+            outb[:, at] = (
+                x1[:, at] + jnp.dot(a[...], w_full[DOWN, :, at], preferred_element_type=f32)
+            ).astype(bf16)
+
+        tiles(finish)
+        own_out = pltpu.make_async_copy(outb, out_out, local_sem.at[6])
+        own_out.start()
+        pair_sum(UP, tmp)
+        pair_sum(OUT, tmp)
+        own_out.wait()
+        for w in range(3):
+            left(stage.at[w], p_send.at[w], p_recv.at[w], c, z)
+
+    wide = (rows, width)
+    pl.run_scoped(
+        feed_forward,
+        vm((3, width, width), bf16), vm(wide, f32), vm(wide, bf16), vm(wide, bf16), vm(wide, bf16), vm(wide, bf16),
+        vm((width, rows), bf16), vm(wide, bf16), vm((rows, 128), f32), vm(wide, bf16),
+        vm((3, n_wsh, shard, half), bf16), vm((2, shard, half), bf16),
+    )
+
+    def attention_backward(h1_all, goaug, go_tm, q_tm, dk, dv, dqkv, part):
+        def reload(b):
+            return pltpu.make_async_copy(h1_hbm.at[b], h1_all.at[b], norm_sem.at[1])
+
+        for b in range(n_ctx):
+            reload(b).start()
+        dk[...] = jnp.zeros_like(dk)
+        dv[...] = jnp.zeros_like(dv)
+        dqkv[3 * span :, :] = jnp.zeros((dqkv.shape[0] - 3 * span, length), bf16)
+        gain_col = gain_column()
+
+        def prepare(g):
+            at = pl.ds(pl.multiple_of(g * rows, 16), rows)
+            for h in range(heads):
+                go = go_land[g, h * hd : (h + 1) * hd, :]
+                wide = go.astype(f32)
+                delta = jnp.sum(wide * o_all[g, h * hd : (h + 1) * hd, :], axis=0, keepdims=True)
+                tail = jnp.concatenate([three_rows(-delta, rows), jnp.zeros((120 - hd, rows), f32)], axis=0)
+                goaug[g, h, 0:hd, :] = go
+                goaug[g, h, hd:128, :] = tail.astype(bf16)
+                go_tm[h, at, :] = jnp.concatenate([wide, jnp.zeros((128 - hd, rows), f32)], axis=0).T.astype(bf16)
+                q = qaug[g, h, 0:hd, :].astype(f32)
+                q_tm[h, at, :] = jnp.concatenate([q, jnp.zeros((128 - hd, rows), f32)], axis=0).T.astype(bf16)
+
+        pltpu.make_async_copy(my_heads(go_stage), go_land.at[c], local_sem.at[5]).wait()
+        prepare(c)
+
+        def prepare_other(k, _):
+            g = lax.rem(c + k, n_ctx)
+            arrive(go_land.at[g], go_send.at[0], go_recv.at[g], c, z)
+            prepare(g)
+            return 0
+
+        lax.fori_loop(1, n_ctx, prepare_other, 0)
+        chunk = length // 2
+        events = (
+            ((1, lambda: first_sum(DOWN)), (4, lambda: first_sum(UP)), (6, lambda: line_sum(DOWN))),
+            ((3, lambda: second_sum(DOWN)), (6, lambda: second_sum(UP)), (7, lambda: first_sum(OUT))),
+        )
+
+        def attend(g, _):
+            at = pl.ds(pl.multiple_of(g * rows, 16), rows)
+            for h in range(heads):
+                dq = jnp.zeros((hd, rows), f32)
+                for j in range(2):
+                    keys = slice(j * chunk, (j + 1) * chunk)
+                    p = jnp.exp(jnp.dot(kaug[h, keys, :], qaug[g, h], preferred_element_type=f32))
+                    ds = (p * jnp.dot(vaug[h, keys, :], goaug[g, h], preferred_element_type=f32)).astype(bf16)
+                    dq = dq + jnp.dot(kt[h, :, keys], ds, preferred_element_type=f32)
+                    dk[h, keys, :] += jnp.dot(ds, q_tm[h, at, :], preferred_element_type=f32)
+                    dv[h, keys, :] += jnp.dot(p.astype(bf16), go_tm[h, at, :], preferred_element_type=f32)
+                scale_acc[...] += dq * qraw[g, h * hd : (h + 1) * hd, :]
+                lanes = pl.ds(pl.multiple_of(g * rows, 128), rows)
+                dqkv[h * hd : (h + 1) * hd, lanes] = (dq * gain_col).astype(bf16)
+                for step, event in events[h]:
+                    pl.when(g == step)(event)
+            return 0
+
+        lax.fori_loop(0, n_ctx, attend, 0)
+
+        def settle(g, _):
+            at = pl.ds(pl.multiple_of(g * rows, 16), rows)
+            lanes = pl.ds(pl.multiple_of(g * rows, 128), rows)
+            for h in range(heads):
+                for source, top in ((dk, span), (dv, 2 * span)):
+                    turned = source[h, at, :].T
+                    dqkv[top + h * hd : top + (h + 1) * hd, lanes] = turned[0:hd].astype(bf16)
+            return 0
+
+        lax.fori_loop(0, n_ctx, settle, 0)
+
+        def partial(b):
+            lanes = pl.ds(pl.multiple_of(b * rows, 128), rows)
+            part[b] = jnp.dot(w_c[...], dqkv[:, lanes], preferred_element_type=f32).astype(bf16)
+
+        def to_sib(i, _):
+            b = 2 * i + (1 - core)
+            partial(b)
+            send(part.at[b], part_p.at[i], hp_send.at[i], hp_recv.at[i], sib, z)
+            return 0
+
+        lax.fori_loop(0, n_ctx // 2, to_sib, 0)
+        planes[DOWN].from_first()
+
+        def own_core(i, _):
+            partial(2 * i + core)
+            return 0
+
+        lax.fori_loop(0, n_ctx // 2, own_core, 0)
+
+        def pair(i, b):
+            arrive(part_p.at[b // 2], hp_send.at[0], hp_recv.at[b // 2], c, z)
+            add_rows(part, (b,), 0, part_p, (b // 2,), 0, width, 128)
+            if i < 2:
+                slot = s_bit if i == 0 else 1 - s_bit
+                send(part.at[b], part_f.at[slot], hf_send.at[i], hf_recv.at[slot], first, z)
+
+        pair(1, diag)
+        pair(0, first)
+        second_sum(OUT)
+        line_sum(UP)
+        planes[DOWN].from_second()
+
+        for b in range(n_ctx):
+            reload(b).wait()
+        starts, size = windows(width, n_wsh)
+        for s in range(n_wsh):
+            total = jnp.zeros((3 * span, size), f32)
+            for b in range(n_ctx):
+                total = total + jnp.dot(
+                    dqkv[0 : 3 * span, b * rows : (b + 1) * rows], h1_all[b, :, starts[s] : starts[s] + size],
+                    preferred_element_type=f32,
+                )
+            win_out[s] = total.astype(bf16)
+
+            @pl.when(z != s)
+            def _():
+                send(win_out.at[s], win_land.at[z], w_send.at[s], w_recv.at[z], c, s)
+
+        pair(2, second)
+        planes[DOWN].from_diag()
+        pair(3, c)
+        planes[UP].from_first()
+        arrive(part_f.at[1 - s_bit], hf_send.at[0], hf_recv.at[1 - s_bit], c, z)
+        add_rows(part, (second,), 0, part_f, (1 - s_bit,), 0, width, 128)
+        send(part.at[second], part_s, hs_send.at[0], hs_recv.at[0], second, z)
+        line_sum(OUT)
+        arrive(part_f.at[s_bit], hf_send.at[0], hf_recv.at[s_bit], c, z)
+        add_rows(part, (c,), 0, part_f, (s_bit,), 0, width, 128)
+        planes[UP].from_second()
+        planes[UP].from_diag()
+
+        for k in range(1, n_wsh):
+            s = lax.rem(z + k, n_wsh)
+            arrive(win_land.at[s], w_send.at[0], w_recv.at[s], c, z)
+
+        def sum_windows(i, _):
+            at = pl.ds(pl.multiple_of(i * 32, 32), 32)
+            total = win_out[z, at, :].astype(f32)
+            for k in range(1, n_wsh):
+                total = total + win_land[lax.rem(z + k, n_wsh), at, :].astype(f32)
+            fin_qkv[at, :] = total.astype(bf16)
+            return 0
+
+        lax.fori_loop(0, 3 * span // 32, sum_windows, 0)
+        plane_w = Plane(lambda b: dwqkv_out.at[b], c, z, around, wg_send, wg_recv)
+        plane_w.start(fin_qkv)
+        own_fin = pltpu.make_async_copy(fin_qkv, dwqkv_out.at[c], local_sem.at[7])
+        own_fin.start()
+        planes[OUT].from_first()
+        planes[OUT].from_second()
+        arrive(part_s, hs_send.at[0], hs_recv.at[0], c, z)
+
+        def turn_dh(i, _):
+            at = pl.ds(pl.multiple_of(i * 128, 128), 128)
+            dh[:, at] = (part[c, at, :].astype(f32) + part_s[at, :].astype(f32)).T
+            return 0
+
+        lax.fori_loop(0, width // 128, turn_dh, 0)
+
+        def last_rows(i, total):
+            at = pl.ds(pl.multiple_of(i * 16, 16), 16)
+            t = tok[at, :].astype(f32)
+            inverse = lax.rsqrt(jnp.mean(t * t, -1, keepdims=True) + EPS)
+            normed = t * inverse
+            grad = dh[at, :]
+            both = grad * normed
+            slope = jnp.mean(both * gains[0:1, :], -1, keepdims=True)
+            gtok[at, :] = (dx[at, :] + inverse * (grad * gains[0:1, :] - normed * slope)).astype(bf16)
+            return total + both
+
+        gain_sum = lax.fori_loop(0, rows // 16, last_rows, jnp.zeros((16, width), f32))
+        scale_sum = jnp.sum(scale_acc[...], axis=1, keepdims=True)
+        scale_row = jnp.concatenate(
+            [jnp.broadcast_to(scale_sum, (hd, 128)), jnp.zeros((128 - hd, 128), f32)], axis=0
+        ).T[0:1, :]
+        vec[0:1, :] = jnp.sum(gain_sum, axis=0, keepdims=True)
+        vec[2:3, 0:128] = scale_row
+        own_gtok = pltpu.make_async_copy(gtok, gtok_out, local_sem.at[11])
+        own_gtok.start()
+        for k in range(1, n_ctx):
+            g = lax.rem(c + k, n_ctx)
+            send(vec, vec_plane.at[c], vp_send.at[k], vp_recv.at[c], g, z)
+        planes[OUT].from_diag()
+        plane_w.from_first()
+        plane_w.from_second()
+        total = vec[...]
+        for k in range(1, n_ctx):
+            g = lax.rem(c + k, n_ctx)
+            arrive(vec_plane.at[g], vp_send.at[0], vp_recv.at[g], c, z)
+            total = total + vec_plane[g]
+        vec_mid[...] = total
+        for k in range(1, n_wsh):
+            send(vec_mid, vec_line.at[z], vl_send.at[k], vl_recv.at[z], c, lax.rem(z + k, n_wsh))
+        plane_w.from_diag()
+        for k in range(1, n_wsh):
+            s = lax.rem(z + k, n_wsh)
+            arrive(vec_line.at[s], vl_send.at[0], vl_recv.at[s], c, z)
+            total = total + vec_line[s]
+        vec_sum[...] = total
+        own_vec = pltpu.make_async_copy(vec_sum, vec_out, local_sem.at[12])
+        own_vec.start()
+        for plane in planes + [plane_w]:
+            all_others(plane)
+            plane.finish()
+        for i in range(n_ctx // 2):
+            left(part.at[0], hp_send.at[i], hp_recv.at[i], c, z)
+        for i in range(2):
+            left(part.at[0], hf_send.at[i], hf_recv.at[i], c, z)
+        left(part.at[0], hs_send.at[0], hs_recv.at[0], c, z)
+        for copy in (own_fin, own_gtok, own_vec):
+            copy.wait()
+
+    pl.run_scoped(
+        attention_backward,
+        vm((n_ctx, rows, width), bf16), vm((n_ctx, heads, 128, rows), bf16), vm((heads, length, 128), bf16),
+        vm((heads, length, 128), bf16), vm((heads, length, 128), f32), vm((heads, length, 128), f32),
+        vm((w_c.shape[1], length), bf16), vm((n_ctx, width, rows), bf16),
+    )
+
+    for i in range(2):
+        tokens[i].finish()
+    wline.finish(wqkv_ref)
+    for w in range(3):
+        lines[w].finish(my_piece[w])
+    for distance in range(1, n_wsh):
+        shards_at(distance, Plane.finish)
+    for k in range(1, n_wsh):
+        left(pack_ref, pk_send.at[k], pk_recv.at[z], c, z)
+        left(vec, vl_send.at[k], vl_recv.at[0], c, z)
+    for k in range(1, n_ctx):
+        g = lax.rem(c + k, n_ctx)
+        left(ob_stage.at[g], ob_send.at[g], ob_recv.at[g], c, z)
+        left(go_land.at[0], go_send.at[k], go_recv.at[0], c, z)
+        left(vec, vp_send.at[k], vp_recv.at[0], c, z)
+    for w in range(3):
+        pltpu.make_async_copy(fin3.at[w], out_piece(w, c), local_sem.at[8 + w]).wait()
+        left(land_f.at[w], f_send.at[w], f_recv.at[w], c, z)
+        left(land_s.at[w], s_send.at[w], s_recv.at[w], c, z)
+        for k in range(1, n_wsh):
+            left(land_z.at[w, 0], z_send.at[w, k], z_recv.at[w, 0], c, z)
+    for s in range(n_wsh):
+
+        @pl.when(z != s)
+        def _():
+            left(win_out.at[s], w_send.at[s], w_recv.at[s], c, z)
+
+
+def whole_call(dims, tok, cot, wqkv, w3, pack, order, lengths):
+    n_ctx, n_wsh, hd, heads = dims
+    rows, width = tok.shape
+    span, length, shard = hd * heads, rows * n_ctx, width // n_wsh
+    half, cut = width // 2, shard // (n_ctx // 2)
+    f32, bf16 = jnp.float32, jnp.bfloat16
+    hbm = pl.BlockSpec(memory_space=pl.ANY)
+    smem = pl.BlockSpec(memory_space=pltpu.SMEM)
+    shape = jax.ShapeDtypeStruct
+    dma = pltpu.SemaphoreType.DMA
+    vm = pltpu.VMEM
+    size = windows(width, n_wsh)[1]
+    wide = (rows, width)
+    outs = (
+        shape(wide, bf16), shape(wide, bf16),
+        shape((shard, width), bf16), shape((shard, width), bf16), shape((shard, width), bf16),
+        shape((n_ctx, 3 * span, size), bf16), shape((8, width), f32),
+        shape((n_ctx, rows, width), bf16), shape((3, width, width), bf16), shape((n_ctx, rows, width), bf16),
+        shape((3, n_wsh, shard, half), bf16),
+    )
+    scratch = [
+        vm(( width, wqkv.shape[1]), bf16), vm((n_wsh,) + pack.shape, f32), vm((8, width), f32),
+        vm((heads, length, 128), bf16), vm((heads, length, 128), bf16), vm((heads, hd, length), bf16),
+        vm((n_ctx, heads, 128, rows), bf16), vm((n_ctx, span, rows), f32), vm((n_ctx, span, rows), f32),
+        vm((n_ctx, span, rows), bf16), vm((width, rows), bf16), vm((width, rows), bf16), vm((n_ctx, span, rows), bf16),
+        vm((3, n_wsh, shard, half), bf16), vm((3, n_wsh, 2 * cut, half), bf16), vm((3, n_wsh, cut, half), bf16),
+        vm((3, n_wsh, cut, half), bf16), vm((3, cut, half), bf16),
+        vm((n_wsh, 3 * span, size), bf16), vm((n_wsh, 3 * span, size), bf16), vm((3 * span, size), bf16),
+        vm((n_ctx // 2, width, rows), bf16), vm((2, width, rows), bf16), vm((width, rows), bf16),
+        vm(wide, f32), vm(wide, f32), vm(wide, bf16), vm(wide, bf16), vm(wide, bf16),
+        vm((8, width), f32), vm((n_ctx, 8, width), f32), vm((n_wsh, 8, width), f32), vm((8, width), f32),
+        vm((8, width), f32), vm((hd, rows), f32),
+        dma((2, 7)), dma((2, n_ctx)), dma((2 * n_wsh,)), dma((n_wsh,)), dma((n_wsh,)), dma((n_wsh,)),
+        dma((n_ctx,)), dma((n_ctx,)), dma((3, 2 * n_wsh)), dma((3, n_wsh)),
+        dma((3, n_wsh, 7)), dma((3, n_wsh, n_ctx)),
+        dma((n_ctx,)), dma((n_ctx,)), dma((3,)), dma((3,)), dma((3,)), dma((3,)), dma((3,)), dma((3,)),
+        dma((3, n_wsh)), dma((3, n_wsh)), dma((3, 7)), dma((3, n_ctx)),
+        dma((n_ctx // 2,)), dma((n_ctx // 2,)), dma((2,)), dma((2,)), dma((1,)), dma((1,)),
+        dma((n_wsh,)), dma((n_wsh,)), dma((7,)), dma((n_ctx,)),
+        dma((n_ctx,)), dma((n_ctx,)), dma((n_wsh,)), dma((n_wsh,)), dma((13,)), dma((2,)), dma((2 + 3 * n_wsh,)),
+    ]
+    return pl.pallas_call(
+        functools.partial(whole_kernel, dims),
+        out_shape=outs,
+        in_specs=[hbm] * 7 + [smem] * 2,
+        out_specs=[hbm] * len(outs),
+        scratch_shapes=scratch,
+        compiler_params=pltpu.CompilerParams(
+            collective_id=0, has_side_effects=True, vmem_limit_bytes=VMEM_BYTES
+        ),
+    )(tok, cot, wqkv, *w3, pack, order, lengths)
+
+
+def head_split(
+    tokens, cotangent, block_lengths, group_order, w_query, w_key, w_value, w_out, w_up, w_down,
+    gain_attn, gain_mlp, query_scale,
+):
+    f32 = jnp.float32
+    n_ctx, n_wsh = lax.axis_size("ctx"), lax.axis_size("wsh")
+    c, z = lax.axis_index("ctx"), lax.axis_index("wsh")
+    width = tokens.shape[2]
+    hd, heads = width // H, H // n_ctx
+    span, shard = hd * heads, width // n_wsh
+    dims = (n_ctx, n_wsh, hd, heads)
+    mine = [lax.dynamic_slice_in_dim(w, c * span, span, 1) for w in (w_query, w_key, w_value)]
+    lanes = -(-3 * span // 128) * 128
+    wqkv = jnp.pad(jnp.concatenate(mine, 1), ((0, 0), (0, lanes - 3 * span)))
+    lanes = -(-shard // 128) * 128
+    pack = jnp.concatenate(
+        [jnp.pad(v.astype(f32), (0, lanes - v.shape[0]))[None] for v in (gain_attn, gain_mlp, query_scale)]
+        + [jnp.zeros((5, lanes), f32)]
+    )
+    outputs, gtok, dwo, dwu, dwd, dwqkv, sums = whole_call(
+        dims, tokens[0], cotangent[0], wqkv, (w_out, w_up, w_down), pack, group_order, block_lengths
+    )[:7]
+    starts, size = windows(width, n_wsh)
+    at = z * shard - jnp.asarray(starts, jnp.int32)[z]
+    dwqkv = dwqkv.reshape(n_ctx, 3, span, size)
+    projections = [
+        lax.dynamic_slice_in_dim(dwqkv[:, i], at, shard, 2).transpose(2, 0, 1).reshape(shard, width).astype(f32)
+        for i in range(3)
+    ]
+    own = [lax.dynamic_slice_in_dim(sums[i], z * shard, shard, 0) for i in (0, 1)]
+    scale_grad = (
+        lax.dynamic_slice_in_dim(sums[2], z * (hd // n_wsh), hd // n_wsh, 0)
+        * (LOG_BASE / math.sqrt(hd))
+        * jax.nn.sigmoid(query_scale.astype(f32))
+    )
+    return (
+        outputs.reshape(tokens.shape), gtok.reshape(tokens.shape), *projections,
+        dwo.astype(f32), dwu.astype(f32), dwd.astype(f32), own[0], own[1], scale_grad,
+    )
+
+
 def solution(mesh):
     in_specs = (
         P("wsh", "ctx", None),
@@ -321,6 +1329,8 @@
         P("wsh"),
         P("wsh"),
     )
+    n_ctx, n_wsh = mesh.shape["ctx"], mesh.shape["wsh"]
+    plan = head_split if (n_ctx, n_wsh) == (8, 4) else per_device
     return jax.shard_map(
-        per_device, mesh=mesh, in_specs=in_specs, out_specs=out_specs, check_vma=False
-    )
+        plan, mesh=mesh, in_specs=in_specs, out_specs=out_specs, check_vma=False
+    )

time: 1210 us -> 251 us (0.21)
  waiting for transfers between devices: 918 us -> 0 us
  Pallas kernels: 0 us -> 217 us
  matrix products: 113 us -> 0 us
  local copies, waits for them, and re-layouts: 92 us -> 15.3 us
  blocking collectives: 36.5 us -> 0 us
  between operations: 17.5 us -> 1.39 us
    reduce_scatter x8 -> x0, waiting for transfers between devices: 461 us -> none  [the longest x1 64.7 us: per_device(): lax.psum_scatter(grad_outw.astype(jnp.bfloat16), 'wsh', scatter_dimension...]
    all_gather x8 -> x0, waiting for transfers between devices: 397 us -> none  [the longest x1 62.8 us: per_device(): lax.all_gather(w_up, 'wsh', axis=0, tiled=True)]
    pallas_call x0 -> x1, Pallas kernels: none -> 217 us  [whole_call(): pl.pallas_call(functools.partial(whole_kernel, dims), out_shape=outs, in_...]
    dot_general x46 -> x0, matrix products: 113 us -> none  [the longest x6 19.4 us: outer_product(): lax.dot_general(left, right, (((0,), (0,)), ((), ())), preferred_element_...]
    psum x1 -> x0, waiting for transfers between devices: 56.1 us -> none  [per_device(): lax.psum(owned[0].astype(jnp.bfloat16), 'ctx').astype(jnp.float32)]
    dynamic_slice x33 -> x5, local copies, waits for them, and re-layouts: 42.3 us -> 3.35 us  [the longest x2 1.42 us: head_split(): lax.dynamic_slice_in_dim(w, c * span, span, 1)]
    unnamed x2 -> x0, blocking collectives: 24.1 us -> none
    unnamed x103 -> x19, local copies, waits for them, and re-layouts: 24.3 us -> 6.81 us
  transfers between devices with their start and end apart: 17 -> 0, of which waited for: 17 -> 0; matrix products, arithmetic and copies ran while one was open for 10% -> 0% of each run, Pallas kernels for 0% -> 0%
where the time goes in v2:
time: 251 us; the launch traced here: 247 us
  Pallas kernels  217 us (86%)
  local copies, waits for them, and re-layouts  15.3 us (6%)
  other arithmetic  13.3 us (5%)
    pallas_call x1, Pallas kernels, whole_call(): pl.pallas_call(functools.partial(whole_kernel, dims), out_shape=outs, in_...  217 us
    unnamed x19, local copies, waits for them, and re-layouts  6.81 us

profile of v2, /device:TPU:0, one launch (start us, length us, event | category | flops | bytes accessed | tf_op | source)
XLA Modules:
  0.0 247.4 jit_solution(3497878371150132737)
XLA Ops:
  0.7 1.3 constant_dynamic-slice_fusion.3
  2.2 0.9 fusion.4.wqkv_ref
  3.1 0.7 pad.20
  3.7 0.7 pad_convert_fusion
  4.4 0.7 pad_convert_fusion.1
  5.2 0.7 maximum_maximum_fusion.pack_ref
  5.9 217.4 %shard_map.221 = (bf16[256,1280]{1,0:T(8,128)(2,1)}, bf16[256,1280]{1,0:T(8,128)(2,1)}, bf16[320,1280]{1,0:T(8,128)(2,1)}, bf16[320,1280]{1,0:T(8,128)(2,1)}, bf...) custom-call(bf16[256,1280]{1,0:T(8,128)(2,1)} %bitcast.43, ...), custom_call_target="tpu_custom_call" | custom-call | tf_op jit(solution)/shard_map/pallas_call | solution.py:1250
  223.3 3.5 %fusion.9 = (bf16[8,1,160,384]{3,2,1,0:T(8,128)(2,1)}, bf16[8,1,160,384]{3,2,1,0:T(8,128)(2,1)}, bf16[8,1,160,384]{3,2,1,0:T(8,128)(2,1)}) fusion(bf16[8,3,160,384]{3,2,1,0:T(8,128)(2,1)} %bitcast.40), kind=kLoop, calls=%fused_computation.23 | loop fusion | bytes 5898240 | tf_op jit(solution)/shard_map/slice | solution.py:1288
  226.8 0.6 dynamic_slice.37
  228.0 1.6 bitcast_convert_fusion.2
  229.6 1.7 copy.31
  231.3 1.6 bitcast_convert_fusion.1
  232.8 1.7 copy.32
  234.5 1.6 bitcast_convert_fusion
  236.1 1.7 copy.33
  237.8 2.5 %convert_element_type.71 = f32[320,1280]{1,0:T(8,128)} convert(bf16[320,1280]{1,0:T(8,128)(2,1)} %get-tuple-element.21) | non-fusion elementwise | flops 409600 | bytes 2457600 | tf_op jit(solution)/shard_map/convert_element_type | solution.py:1299
  240.3 1.3 convert_element_type.72
  241.6 1.3 convert_element_type.73
  242.9 0.9 fusion.10
  243.8 0.7 fusion.5
  244.5 0.7 fusion.6
  245.1 0.6 divide_multiply_fusion
  245.7 0.8 copy.42
  246.6 0.8 copy.43
  (20 shorter events, 0.3 us)
Async XLA Ops:
  0.6 1.4 copy-start
  223.3 3.5 %copy-start.6 = (s32[4]{0:T(128)S(1)}, s32[4]{0:T(128)}, u32[]{:S(2)}) copy-start(s32[4]{0:T(128)} %constant.41.clone) | copy-start | bytes 52
  237.8 2.5 %copy-start.2 = (bf16[320,1280]{1,0:T(8,128)(2,1)S(1)}, bf16[320,1280]{1,0:T(8,128)(2,1)}, u32[]{:S(2)}) copy-start(bf16[320,1280]{1,0:T(8,128)(2,1)} %get-tuple-element.22) | copy-start | bytes 2457604
  237.8 3.8 %copy-start.1 = (bf16[320,1280]{1,0:T(8,128)(2,1)S(1)}, bf16[320,1280]{1,0:T(8,128)(2,1)}, u32[]{:S(2)}) copy-start(bf16[320,1280]{1,0:T(8,128)(2,1)} %get-tuple-element.23) | copy-start | bytes 2457604
  240.3 4.8 %copy-start.5 = (bf16[20]{0:T(256)(128)(2,1)S(1)}, bf16[20]{0:T(256)(128)(2,1)}, u32[]{:S(2)}) copy-start(bf16[20]{0:T(256)(128)(2,1)} %param.26) | copy-start | bytes 124
  240.3 5.4 %copy-start.4 = (bf16[256,1280]{1,0:T(8,128)(2,1)S(1)}, bf16[256,1280]{1,0:T(8,128)(2,1)}, u32[]{:S(2)}) copy-start(bf16[256,1280]{1,0:T(8,128)(2,1)} %get-tuple-element.18) | copy-start | bytes 1966084
  241.6 5.0 %copy-start.3 = (bf16[256,1280]{1,0:T(8,128)(2,1)S(1)}, bf16[256,1280]{1,0:T(8,128)(2,1)}, u32[]{:S(2)}) copy-start(bf16[256,1280]{1,0:T(8,128)(2,1)} %get-tuple-element.19) | copy-start | bytes 1966084

commit v3 on v2

--- a/solution.py
+++ b/solution.py
@@ -297,7 +297,7 @@
 
 MESH = pl.DeviceIdType.MESH
 NEG = -1e30
-VMEM_BYTES = 60 * 1024 * 1024
+VMEM_BYTES = 62 * 1024 * 1024
 
 
 def place():
@@ -473,15 +473,13 @@
     return jnp.where(row == 0, high, 0.0) + jnp.where(row == 1, mid, 0.0) + jnp.where(row == 2, low, 0.0)
 
 
-def add_rows(target, index, at, other, other_index, other_at, rows, step=16):
+def add_rows(target, at, other, other_at, rows, step):
     f32 = jnp.float32
 
     def some_rows(i, _):
         here = pl.ds(pl.multiple_of(at + i * step, 16), step)
         there = pl.ds(pl.multiple_of(other_at + i * step, 16), step)
-        left_part = target[index + (here, slice(None))].astype(f32)
-        right_part = other[other_index + (there, slice(None))].astype(f32)
-        target[index + (here, slice(None))] = (left_part + right_part).astype(target.dtype)
+        target[here, :] = (target[here, :].astype(f32) + other[there, :].astype(f32)).astype(target.dtype)
         return 0
 
     lax.fori_loop(0, rows // step, some_rows, 0)
@@ -497,16 +495,15 @@
 def whole_kernel(
     dims,
     tok_ref, cot_ref, wqkv_ref, wout_ref, wup_ref, wdown_ref, pack_ref, order_ref, lengths_ref,
-    out_out, gtok_out, dwo_out, dwu_out, dwd_out, dwqkv_out, vec_out,
-    tok_hbm, w_hbm, h1_hbm, land_p,
-    w_c, packs, gains, kaug, vaug, kt, qaug, qraw, o_all, ob_stage, ob_land, go_stage, go_land,
-    acc, land_f, land_s, land_z, fin3, win_out, win_land, fin_qkv, part_p, part_f, part_s,
+    out_out, gtok_out, dw3_out, dwqkv_out, vec_out,
+    h1_all, w_full, big, w_c, packs, gains, kaug, vaug, kt, qaug, qraw, o_all, ob_stage, ob_land, go_stage, go_land,
+    acc, land_f, land_s, land_near, land_far, win_out, win_near, win_far,
     dx, dh, tok, cot, gtok, vec, vec_plane, vec_line, vec_mid, vec_sum, scale_acc,
     tok_send, tok_recv, wz_send, wz_recv, pk_send, pk_recv, ob_send, ob_recv,
     w3z_send, w3z_recv, w3p_send, w3p_recv,
-    go_send, go_recv, p_send, p_recv, f_send, f_recv, s_send, s_recv, z_send, z_recv, g_send, g_recv,
-    hp_send, hp_recv, hf_send, hf_recv, hs_send, hs_recv, w_send, w_recv, wg_send, wg_recv,
-    vp_send, vp_recv, vl_send, vl_recv, local_sem, norm_sem, load_sem,
+    go_send, go_recv, p_send, p_recv, f_send, f_recv, s_send, s_recv, zn_send, zn_recv, zf_send, zf_recv, g_send, g_recv,
+    hp_send, hp_recv, hf_send, hf_recv, hs_send, hs_recv, wn_send, wn_recv, wf_send, wf_recv, wg_send, wg_recv,
+    vp_send, vp_recv, vl_send, vl_recv, local_sem, load_sem,
 ):
     n_ctx, n_wsh, hd, heads = dims
     f32, bf16 = jnp.float32, jnp.bfloat16
@@ -526,7 +523,7 @@
     part_rows = rows // 2
     tokens = [
         Plane(
-            lambda b, i=i: tok_hbm.at[b, pl.ds(i * part_rows, part_rows)], c, z, around,
+            lambda b, i=i: big.at[pl.ds(pl.multiple_of(b * rows + i * part_rows, 16), part_rows)], c, z, around,
             tok_send.at[i], tok_recv.at[i],
         )
         for i in range(2)
@@ -541,7 +538,13 @@
     own_w = pltpu.make_async_copy(wqkv_ref, wline.at(z), local_sem.at[1])
     own_pack = pltpu.make_async_copy(pack_ref, packs.at[z], local_sem.at[2])
     own_cot = pltpu.make_async_copy(cot_ref, cot, local_sem.at[3])
-    for copy in (own_tok, own_pack, own_w, own_cot):
+    own_full = [
+        pltpu.make_async_copy(
+            w3_refs[w], w_full.at[w, pl.ds(pl.multiple_of(z * shard, 16), shard)], load_sem.at[heads + w]
+        )
+        for w in range(3)
+    ]
+    for copy in (own_tok, own_pack, own_w, own_cot, *own_full):
         copy.start()
     vec[...] = jnp.zeros_like(vec)
     scale_acc[...] = jnp.zeros_like(scale_acc)
@@ -551,7 +554,7 @@
 
     def piece(w, s, b):
         top = pl.multiple_of(s * shard + (b // 2) * cut, 16)
-        return w_hbm.at[w, pl.ds(top, cut), columns(b)]
+        return w_full.at[w, pl.ds(top, cut), columns(b)]
 
     my_piece = [ref.at[pl.ds(pl.multiple_of((c // 2) * cut, 16), cut), columns(c)] for ref in w3_refs]
     lines = [
@@ -602,61 +605,45 @@
         soft = jnp.maximum(scale, 0.0) + jnp.log(1.0 + jnp.exp(-jnp.abs(scale)))
         return (LOG_BASE / math.sqrt(hd) * soft).T[0:hd, 0:1]
 
-    def attention_forward(h1_all, tok_buf, vt, qneg, s_buf):
-        def load(slot, b):
-            return pltpu.make_async_copy(tok_hbm.at[b], tok_buf.at[slot], load_sem.at[slot])
-
-        def norm_block(b, source):
+    def attention_forward(vt, qneg, s_buf):
+        def norm_block(b, source, top):
             gain = gains[0:1, :]
 
             def some_rows(i, _):
-                at = pl.ds(pl.multiple_of(i * 32, 32), 32)
-                t = source[at, :].astype(f32)
+                t = source[pl.ds(pl.multiple_of(top + i * 32, 32), 32), :].astype(f32)
                 inverse = lax.rsqrt(jnp.mean(t * t, -1, keepdims=True) + EPS)
-                h1_all[b, at, :] = (t * inverse * gain).astype(bf16)
+                h1_all[b, pl.ds(pl.multiple_of(i * 32, 32), 32), :] = (t * inverse * gain).astype(bf16)
                 return 0
 
             lax.fori_loop(0, rows // 32, some_rows, 0)
-            pltpu.make_async_copy(h1_all.at[b], h1_hbm.at[b], norm_sem.at[0]).start()
+
+        def norm_arrived(b):
+            norm_block(b, big, b * rows)
 
         def arrived(b):
             for i in range(2):
                 tokens[i].wait(b)
-
-        def norm_loaded(slot, b):
-            load(slot, b).wait()
-            norm_block(b, tok_buf.at[slot])
+            norm_arrived(b)
 
         others = tokens[0].others()
-        norm_block(c, tok)
+        norm_block(c, tok, 0)
         arrived(others[0])
-        load(0, others[0]).start()
         tokens[0].from_first()
-        norm_loaded(0, others[0])
         wline.forward(1)
         tokens[1].from_first()
-        load(1, first).start()
+        norm_arrived(first)
         tokens[0].from_second()
-        norm_loaded(1, first)
         tokens[1].from_second()
-        load(0, second).start()
-        norm_loaded(0, second)
+        norm_arrived(second)
         wline.forward(2)
         for w in range(3):
             lines[w].start(my_piece[w])
         arrived(others[1])
-        load(1, others[1]).start()
-        norm_loaded(1, others[1])
         arrived(others[2])
-        load(0, others[2]).start()
-        norm_loaded(0, others[2])
         tokens[0].from_diag()
         tokens[1].from_diag()
-        load(1, diag).start()
-        norm_loaded(1, diag)
+        norm_arrived(diag)
         arrived(others[3])
-        load(0, others[3]).start()
-        norm_loaded(0, others[3])
         wline.forward(3)
         own_w.wait()
         spread(1)
@@ -670,14 +657,16 @@
             neg = jnp.where(row > ids, NEG, 0.0)
             ones = jnp.ones((8, rows), f32)
             qneg[b] = neg
-            qraw[b] = raw[0:span]
             for h in range(heads):
-                q = raw[h * hd : (h + 1) * hd] * gain_col
+                top = 3 * h * hd
+                q = raw[top : top + hd]
+                qraw[b, h * hd : (h + 1) * hd, :] = q
+                q = q * gain_col
                 qaug[b, h, 0:hd, :] = q.astype(bf16)
                 qaug[b, h, hd : hd + 16, :] = jnp.concatenate([neg, jnp.zeros((8, rows), f32)], axis=0).astype(bf16)
                 qaug[b, h, hd + 16 : 128, :] = jnp.zeros((112 - hd, rows), bf16)
-                k = raw[span + h * hd : span + (h + 1) * hd].astype(bf16)
-                v = raw[2 * span + h * hd : 2 * span + (h + 1) * hd].astype(bf16)
+                k = raw[top + hd : top + 2 * hd].astype(bf16)
+                v = raw[top + 2 * hd : top + 3 * hd].astype(bf16)
                 tail = jnp.zeros((112 - hd, rows), f32)
                 kt[h, :, at] = k
                 vt[h, 0:hd, at] = v
@@ -687,6 +676,8 @@
             return 0
 
         lax.fori_loop(0, n_ctx, project, 0)
+        for i in range(2):
+            tokens[i].finish()
         keys = length // 2
         events = (
             ((0, lambda: spread(2)), (2, lambda: shards_at(1, from_first)), (4, lambda: shards_at(1, from_second))),
@@ -722,8 +713,6 @@
             return 0
 
         lax.fori_loop(0, n_ctx, attend, 0)
-        for b in range(n_ctx):
-            pltpu.make_async_copy(h1_all.at[b], h1_hbm.at[b], norm_sem.at[0]).wait()
 
     def my_heads(ref):
         return ref.at[pl.ds(pl.multiple_of(c * span, 16), span)]
@@ -734,8 +723,7 @@
     vm = pltpu.VMEM
     pl.run_scoped(
         attention_forward,
-        vm((n_ctx, rows, width), bf16), vm((2, rows, width), bf16), vm((heads, hd + 16, length), bf16),
-        vm((n_ctx, 8, rows), f32), vm((length, rows), f32),
+        vm((heads, hd + 16, length), bf16), vm((n_ctx, 8, rows), f32), vm((length, rows), f32),
     )
     own_o = pltpu.make_async_copy(ob_stage.at[c], my_heads(ob_land), local_sem.at[4])
     own_o.start()
@@ -743,78 +731,61 @@
     mine = pl.ds(pl.multiple_of(core * half, 128), half)
     theirs = pl.ds(pl.multiple_of((1 - core) * half, 128), half)
     my_top = f_bit * two + s_bit * cut
-    dw_outs = (dwo_out, dwu_out, dwd_out)
-
-    def pair_sum(w, tmp):
-        arrive(land_p.at[w], p_send.at[w], p_recv.at[w], c, z)
-        copies = [
-            pltpu.make_async_copy(land_p.at[w, s], tmp.at[s % 2], load_sem.at[s % 2]) for s in range(n_wsh)
-        ]
-        copies[0].start()
+    near, far = z + 1 - 2 * lax.rem(z, 2), z + 2 - 4 * (z // 2)
+
+    def pair_at(w):
+        return big.at[pl.ds(2 * w * shard, 2 * shard)]
+
+    def pair_sum(w):
+        arrive(pair_at(w), p_send.at[w], p_recv.at[w], c, z)
         for s in range(n_wsh):
-            copies[s].wait()
-            if s + 1 < n_wsh:
-                copies[s + 1].start()
-            add_rows(acc, (w, s), 0, tmp, (s % 2,), 0, shard, 64)
+            other = big.at[:, pl.ds(s % 2 * half, half)]
+            add_rows(acc.at[w, s], 0, other, (2 * w + s // 2) * shard, shard, 64)
         at = pl.ds(pl.multiple_of((1 - f_bit) * two, 16), two)
         send(acc.at[w, :, at], land_f.at[w], f_send.at[w], f_recv.at[w], first, z)
 
     def first_sum(w):
         arrive(land_f.at[w], f_send.at[w], f_recv.at[w], c, z)
         for s in range(n_wsh):
-            add_rows(acc, (w, s), f_bit * two, land_f, (w, s), 0, two, 80)
+            add_rows(acc.at[w, s], f_bit * two, land_f.at[w, s], 0, two, 80)
         at = pl.ds(pl.multiple_of(f_bit * two + (1 - s_bit) * cut, 16), cut)
         send(acc.at[w, :, at], land_s.at[w], s_send.at[w], s_recv.at[w], second, z)
 
     def second_sum(w):
         arrive(land_s.at[w], s_send.at[w], s_recv.at[w], c, z)
         for s in range(n_wsh):
-            add_rows(acc, (w, s), my_top, land_s, (w, s), 0, cut, 80)
+            add_rows(acc.at[w, s], my_top, land_s.at[w, s], 0, cut, 80)
         at = pl.ds(pl.multiple_of(my_top, 16), cut)
-        for k in range(1, n_wsh):
-            s = lax.rem(z + k, n_wsh)
-            send(acc.at[w, s, at], land_z.at[w, z], z_send.at[w, k], z_recv.at[w, z], c, s)
+        for j in range(2):
+            s = 2 * j + lax.rem(near, 2)
+            send(acc.at[w, s, at], land_near.at[w, j], zn_send.at[w, j], zn_recv.at[w, j], c, near)
+
+    def near_sum(w):
+        for j in range(2):
+            arrive(land_near.at[w, j], zn_send.at[w, j], zn_recv.at[w, j], c, z)
+            add_rows(acc.at[w, 2 * j + lax.rem(z, 2)], my_top, land_near.at[w, j], 0, cut, 80)
+        at = pl.ds(pl.multiple_of(my_top, 16), cut)
+        send(acc.at[w, far, at], land_far.at[w], zf_send.at[w], zf_recv.at[w], c, far)
 
     def out_piece(w, b):
         b_core, b_x, b_y = lax.rem(b, 2), lax.rem(b // 2, 2), b // 4
         r = (1 - b_core) * (2 * b_x + b_y) + b_core * (2 * b_y + b_x)
-        return dw_outs[w].at[pl.ds(pl.multiple_of(r * cut, 16), cut), columns(b)]
+        return dw3_out.at[w, pl.ds(pl.multiple_of(r * cut, 16), cut), columns(b)]
 
     planes = [
         Plane(lambda b, w=w: out_piece(w, b), c, z, around, g_send.at[w], g_recv.at[w]) for w in range(3)
     ]
 
-    def line_sum(w):
-        for k in range(1, n_wsh):
-            s = lax.rem(z + k, n_wsh)
-            arrive(land_z.at[w, s], z_send.at[w, 0], z_recv.at[w, s], c, z)
-
-        def some_rows(i, _):
-            at = pl.ds(pl.multiple_of(i * 16, 16), 16)
-            total = acc[w, z, pl.ds(pl.multiple_of(my_top + i * 16, 16), 16), :].astype(f32)
-            for k in range(1, n_wsh):
-                total = total + land_z[w, lax.rem(z + k, n_wsh), at, :].astype(f32)
-            fin3[w, at, :] = total.astype(bf16)
-            return 0
-
-        lax.fori_loop(0, cut // 16, some_rows, 0)
-        planes[w].start(fin3.at[w])
-        pltpu.make_async_copy(fin3.at[w], out_piece(w, c), local_sem.at[8 + w]).start()
-
-    def feed_forward(w_full, x1, h2, a, gu, ob, turned, ga, inv2, outb, stage, tmp):
-        def load(w, k):
-            at = pl.ds(pl.multiple_of(lax.rem(z + k, n_wsh) * shard, 16), shard)
-            source = w_hbm.at[w, at] if k else w3_refs[w]
-            return pltpu.make_async_copy(source, w_full.at[w, at], load_sem.at[2 + n_wsh * w + k])
-
-        def whole(w):
-            for k in range(1, n_wsh):
-                load(w, k).start()
-
-        def ready(w):
-            for k in range(n_wsh):
-                load(w, k).wait()
-
+    def final_piece(w):
+        return acc.at[w, z, pl.ds(pl.multiple_of(my_top, 16), cut)]
+
+    def far_sum(w):
+        arrive(land_far.at[w], zf_send.at[w], zf_recv.at[w], c, z)
+        add_rows(acc.at[w, z], my_top, land_far.at[w], 0, cut, 80)
+        planes[w].start(final_piece(w))
+        pltpu.make_async_copy(final_piece(w), out_piece(w, c), local_sem.at[8 + w]).start()
+
+    def feed_forward(x1, h2, a, gu, ob, turned, ga, inv2, outb, stage):
         def tiles(step, size=256):
             def one(i, _):
                 step(pl.ds(pl.multiple_of(i * size, size), size))
@@ -830,15 +801,14 @@
 
         def weight_gradient(w, left_t, right):
             for s in range(n_wsh):
-                at = slice(s * shard, (s + 1) * shard)
-                stage[w, s] = jnp.dot(left_t[at, :], right[:, theirs], preferred_element_type=f32).astype(bf16)
-            send(stage.at[w], land_p.at[w], p_send.at[w], p_recv.at[w], sib, z)
+                stage[w, s // 2 * shard : (s // 2 + 1) * shard, s % 2 * half : (s % 2 + 1) * half] = jnp.dot(
+                    left_t[s * shard : (s + 1) * shard, :], right[:, theirs], preferred_element_type=f32
+                ).astype(bf16)
+            send(stage.at[w], pair_at(w), p_send.at[w], p_recv.at[w], sib, z)
             for s in range(n_wsh):
                 at = slice(s * shard, (s + 1) * shard)
                 acc[w, s] = jnp.dot(left_t[at, :], right[:, mine], preferred_element_type=f32).astype(bf16)
 
-        for w in range(3):
-            load(w, 0).start()
         shards_at(3, from_first, (OUT,))
         shards_at(2, from_second, (OUT,))
         shards_at(3, from_second, (OUT,))
@@ -848,7 +818,6 @@
         shards_at(2, from_second, (UP, DOWN))
         for distance in range(1, n_wsh):
             shards_at(distance, all_others, (OUT,))
-        whole(OUT)
         own_o.wait()
         for k in range(1, n_ctx):
             g = lax.rem(c + k, n_ctx)
@@ -860,7 +829,7 @@
         tiles(turn_ob, 128)
         shards_at(3, from_second, (UP, DOWN))
         shards_at(2, from_diag, (UP, DOWN))
-        ready(OUT)
+        own_full[OUT].wait()
 
         def mix(at):
             x1[:, at] = tok[:, at].astype(f32) + jnp.dot(ob[...], w_full[OUT, :, at], preferred_element_type=f32)
@@ -869,8 +838,6 @@
         shards_at(3, from_diag, (UP, DOWN))
         for distance in range(1, n_wsh):
             shards_at(distance, all_others, (UP, DOWN))
-        whole(UP)
-        whole(DOWN)
 
         def norm_rows(i, _):
             at = pl.ds(pl.multiple_of(i * 32, 32), 32)
@@ -882,8 +849,8 @@
 
         lax.fori_loop(0, rows // 32, norm_rows, 0)
         own_cot.wait()
-        ready(UP)
-        ready(DOWN)
+        own_full[UP].wait()
+        own_full[DOWN].wait()
 
         def hidden(at):
             up = jnp.dot(h2[...], w_full[UP, :, at], preferred_element_type=f32)
@@ -927,11 +894,15 @@
             ).astype(bf16)
 
         tiles(back_out)
+        for w in range(3):
+            lines[w].finish(my_piece[w])
+        for distance in range(1, n_wsh):
+            shards_at(distance, Plane.finish)
         for k in range(1, n_ctx):
             g = lax.rem(c + k, n_ctx)
             send(heads_of(go_stage, g), go_land.at[c], go_send.at[k], go_recv.at[c], g, z)
         pltpu.make_async_copy(my_heads(go_stage), go_land.at[c], local_sem.at[5]).start()
-        pair_sum(DOWN, tmp)
+        pair_sum(DOWN)
         turn(h2, turned)
         weight_gradient(UP, turned, gu)
         weight_gradient(OUT, ob_land, ga)
@@ -944,8 +915,8 @@
         tiles(finish)
         own_out = pltpu.make_async_copy(outb, out_out, local_sem.at[6])
         own_out.start()
-        pair_sum(UP, tmp)
-        pair_sum(OUT, tmp)
+        pair_sum(UP)
+        pair_sum(OUT)
         own_out.wait()
         for w in range(3):
             left(stage.at[w], p_send.at[w], p_recv.at[w], c, z)
@@ -953,17 +924,28 @@
     wide = (rows, width)
     pl.run_scoped(
         feed_forward,
-        vm((3, width, width), bf16), vm(wide, f32), vm(wide, bf16), vm(wide, bf16), vm(wide, bf16), vm(wide, bf16),
+        vm(wide, f32), vm(wide, bf16), vm(wide, bf16), vm(wide, bf16), vm(wide, bf16),
         vm((width, rows), bf16), vm(wide, bf16), vm((rows, 128), f32), vm(wide, bf16),
-        vm((3, n_wsh, shard, half), bf16), vm((2, shard, half), bf16),
-    )
-
-    def attention_backward(h1_all, goaug, go_tm, q_tm, dk, dv, dqkv, part):
-        def reload(b):
-            return pltpu.make_async_copy(h1_hbm.at[b], h1_all.at[b], norm_sem.at[1])
-
-        for b in range(n_ctx):
-            reload(b).start()
+        vm((3, 2 * shard, width), bf16),
+    )
+
+    def attention_backward(goaug, go_tm, q_tm, dk, dv, dqkv):
+        per = width // rows
+
+        def block(i):
+            return w_full.at[i // per, :, pl.ds(pl.multiple_of(lax.rem(i, per) * rows, 128), rows)]
+
+        def part_p(i):
+            return block(i)
+
+        def part_f(i):
+            return block(n_ctx // 2 + i)
+
+        part_s = block(jnp.int32(n_ctx // 2 + 2))
+
+        def part(b):
+            return block(n_ctx // 2 + 3 + b)
+
         dk[...] = jnp.zeros_like(dk)
         dv[...] = jnp.zeros_like(dv)
         dqkv[3 * span :, :] = jnp.zeros((dqkv.shape[0] - 3 * span, length), bf16)
@@ -993,14 +975,12 @@
 
         lax.fori_loop(1, n_ctx, prepare_other, 0)
         chunk = length // 2
-        events = (
-            ((1, lambda: first_sum(DOWN)), (4, lambda: first_sum(UP)), (6, lambda: line_sum(DOWN))),
-            ((3, lambda: second_sum(DOWN)), (6, lambda: second_sum(UP)), (7, lambda: first_sum(OUT))),
-        )
-
-        def attend(g, _):
-            at = pl.ds(pl.multiple_of(g * rows, 16), rows)
-            for h in range(heads):
+        three = 3 * hd
+        starts, size = windows(width, n_wsh)
+
+        def head_gradients(h, events):
+            def attend(g, _):
+                at = pl.ds(pl.multiple_of(g * rows, 16), rows)
                 dq = jnp.zeros((hd, rows), f32)
                 for j in range(2):
                     keys = slice(j * chunk, (j + 1) * chunk)
@@ -1011,36 +991,73 @@
                     dv[h, keys, :] += jnp.dot(p.astype(bf16), go_tm[h, at, :], preferred_element_type=f32)
                 scale_acc[...] += dq * qraw[g, h * hd : (h + 1) * hd, :]
                 lanes = pl.ds(pl.multiple_of(g * rows, 128), rows)
-                dqkv[h * hd : (h + 1) * hd, lanes] = (dq * gain_col).astype(bf16)
-                for step, event in events[h]:
+                dqkv[h * three : h * three + hd, lanes] = (dq * gain_col).astype(bf16)
+                for step, event in events:
                     pl.when(g == step)(event)
-            return 0
-
-        lax.fori_loop(0, n_ctx, attend, 0)
-
-        def settle(g, _):
-            at = pl.ds(pl.multiple_of(g * rows, 16), rows)
-            lanes = pl.ds(pl.multiple_of(g * rows, 128), rows)
-            for h in range(heads):
-                for source, top in ((dk, span), (dv, 2 * span)):
+                return 0
+
+            lax.fori_loop(0, n_ctx, attend, 0)
+
+            def settle(g, _):
+                at = pl.ds(pl.multiple_of(g * rows, 16), rows)
+                lanes = pl.ds(pl.multiple_of(g * rows, 128), rows)
+                for i, source in enumerate((dk, dv)):
                     turned = source[h, at, :].T
-                    dqkv[top + h * hd : top + (h + 1) * hd, lanes] = turned[0:hd].astype(bf16)
-            return 0
-
-        lax.fori_loop(0, n_ctx, settle, 0)
+                    top = h * three + (i + 1) * hd
+                    dqkv[top : top + hd, lanes] = turned[0:hd].astype(bf16)
+                return 0
+
+            lax.fori_loop(0, n_ctx, settle, 0)
+            for s in range(n_wsh):
+                total = jnp.zeros((three, size), f32)
+                for b in range(n_ctx):
+                    total = total + jnp.dot(
+                        dqkv[h * three : (h + 1) * three, b * rows : (b + 1) * rows],
+                        h1_all[b, :, starts[s] : starts[s] + size], preferred_element_type=f32,
+                    )
+                win_out[h, s] = total.astype(bf16)
+            for j in range(2):
+                s = 2 * j + lax.rem(near, 2)
+                send(win_out.at[h, s], win_near.at[h, j], wn_send.at[h, j], wn_recv.at[h, j], c, near)
+
+        def near_window(h):
+            for j in range(2):
+                arrive(win_near.at[h, j], wn_send.at[h, j], wn_recv.at[h, j], c, z)
+                add_rows(win_out.at[h, 2 * j + lax.rem(z, 2)], 0, win_near.at[h, j], 0, three, 80)
+            send(win_out.at[h, far], win_far.at[h], wf_send.at[h], wf_recv.at[h], c, far)
+
+        plane_w = [
+            Plane(lambda b, h=h: dwqkv_out.at[b, h], c, z, around, wg_send.at[h], wg_recv.at[h]) for h in range(heads)
+        ]
+
+        def own_window(h):
+            return pltpu.make_async_copy(win_out.at[h, z], dwqkv_out.at[c, h], load_sem.at[h])
+
+        def far_window(h):
+            arrive(win_far.at[h], wf_send.at[h], wf_recv.at[h], c, z)
+            add_rows(win_out.at[h, z], 0, win_far.at[h], 0, three, 80)
+            plane_w[h].start(win_out.at[h, z])
+            own_window(h).start()
+
+        head_gradients(0, ((3, lambda: first_sum(DOWN)), (7, lambda: second_sum(DOWN))))
+        head_gradients(1, (
+            (0, lambda: first_sum(UP)), (3, lambda: near_sum(DOWN)), (4, lambda: second_sum(UP)),
+            (5, lambda: near_window(0)), (7, lambda: first_sum(OUT)),
+        ))
 
         def partial(b):
             lanes = pl.ds(pl.multiple_of(b * rows, 128), rows)
-            part[b] = jnp.dot(w_c[...], dqkv[:, lanes], preferred_element_type=f32).astype(bf16)
+            part(b)[...] = jnp.dot(w_c[...], dqkv[:, lanes], preferred_element_type=f32).astype(bf16)
 
         def to_sib(i, _):
             b = 2 * i + (1 - core)
             partial(b)
-            send(part.at[b], part_p.at[i], hp_send.at[i], hp_recv.at[i], sib, z)
+            send(part(b), part_p(i), hp_send.at[i], hp_recv.at[i], sib, z)
             return 0
 
         lax.fori_loop(0, n_ctx // 2, to_sib, 0)
-        planes[DOWN].from_first()
+        far_sum(DOWN)
+        near_sum(UP)
 
         def own_core(i, _):
             partial(2 * i + core)
@@ -1049,71 +1066,42 @@
         lax.fori_loop(0, n_ctx // 2, own_core, 0)
 
         def pair(i, b):
-            arrive(part_p.at[b // 2], hp_send.at[0], hp_recv.at[b // 2], c, z)
-            add_rows(part, (b,), 0, part_p, (b // 2,), 0, width, 128)
+            arrive(part_p(b // 2), hp_send.at[0], hp_recv.at[b // 2], c, z)
+            add_rows(part(b), 0, part_p(b // 2), 0, width, 128)
             if i < 2:
                 slot = s_bit if i == 0 else 1 - s_bit
-                send(part.at[b], part_f.at[slot], hf_send.at[i], hf_recv.at[slot], first, z)
+                send(part(b), part_f(slot), hf_send.at[i], hf_recv.at[slot], first, z)
 
         pair(1, diag)
         pair(0, first)
         second_sum(OUT)
-        line_sum(UP)
+        far_window(0)
+        pair(2, second)
+        pair(3, c)
+        near_window(1)
+        far_sum(UP)
+        near_sum(OUT)
+        arrive(part_f(1 - s_bit), hf_send.at[0], hf_recv.at[1 - s_bit], c, z)
+        add_rows(part(second), 0, part_f(1 - s_bit), 0, width, 128)
+        send(part(second), part_s, hs_send.at[0], hs_recv.at[0], second, z)
+        planes[DOWN].from_first()
         planes[DOWN].from_second()
-
-        for b in range(n_ctx):
-            reload(b).wait()
-        starts, size = windows(width, n_wsh)
-        for s in range(n_wsh):
-            total = jnp.zeros((3 * span, size), f32)
-            for b in range(n_ctx):
-                total = total + jnp.dot(
-                    dqkv[0 : 3 * span, b * rows : (b + 1) * rows], h1_all[b, :, starts[s] : starts[s] + size],
-                    preferred_element_type=f32,
-                )
-            win_out[s] = total.astype(bf16)
-
-            @pl.when(z != s)
-            def _():
-                send(win_out.at[s], win_land.at[z], w_send.at[s], w_recv.at[z], c, s)
-
-        pair(2, second)
+        arrive(part_f(s_bit), hf_send.at[0], hf_recv.at[s_bit], c, z)
+        add_rows(part(c), 0, part_f(s_bit), 0, width, 128)
+        far_window(1)
+        far_sum(OUT)
         planes[DOWN].from_diag()
-        pair(3, c)
+        plane_w[0].from_first()
+        plane_w[0].from_second()
         planes[UP].from_first()
-        arrive(part_f.at[1 - s_bit], hf_send.at[0], hf_recv.at[1 - s_bit], c, z)
-        add_rows(part, (second,), 0, part_f, (1 - s_bit,), 0, width, 128)
-        send(part.at[second], part_s, hs_send.at[0], hs_recv.at[0], second, z)
-        line_sum(OUT)
-        arrive(part_f.at[s_bit], hf_send.at[0], hf_recv.at[s_bit], c, z)
-        add_rows(part, (c,), 0, part_f, (s_bit,), 0, width, 128)
         planes[UP].from_second()
-        planes[UP].from_diag()
-
-        for k in range(1, n_wsh):
-            s = lax.rem(z + k, n_wsh)
-            arrive(win_land.at[s], w_send.at[0], w_recv.at[s], c, z)
-
-        def sum_windows(i, _):
-            at = pl.ds(pl.multiple_of(i * 32, 32), 32)
-            total = win_out[z, at, :].astype(f32)
-            for k in range(1, n_wsh):
-                total = total + win_land[lax.rem(z + k, n_wsh), at, :].astype(f32)
-            fin_qkv[at, :] = total.astype(bf16)
-            return 0
-
-        lax.fori_loop(0, 3 * span // 32, sum_windows, 0)
-        plane_w = Plane(lambda b: dwqkv_out.at[b], c, z, around, wg_send, wg_recv)
-        plane_w.start(fin_qkv)
-        own_fin = pltpu.make_async_copy(fin_qkv, dwqkv_out.at[c], local_sem.at[7])
-        own_fin.start()
-        planes[OUT].from_first()
-        planes[OUT].from_second()
         arrive(part_s, hs_send.at[0], hs_recv.at[0], c, z)
+
+        mine_part = part(c)
 
         def turn_dh(i, _):
             at = pl.ds(pl.multiple_of(i * 128, 128), 128)
-            dh[:, at] = (part[c, at, :].astype(f32) + part_s[at, :].astype(f32)).T
+            dh[:, at] = (mine_part[at, :].astype(f32) + part_s[at, :].astype(f32)).T
             return 0
 
         lax.fori_loop(0, width // 128, turn_dh, 0)
@@ -1141,9 +1129,12 @@
         for k in range(1, n_ctx):
             g = lax.rem(c + k, n_ctx)
             send(vec, vec_plane.at[c], vp_send.at[k], vp_recv.at[c], g, z)
-        planes[OUT].from_diag()
-        plane_w.from_first()
-        plane_w.from_second()
+        plane_w[0].from_diag()
+        planes[UP].from_diag()
+        plane_w[1].from_first()
+        planes[OUT].from_first()
+        plane_w[1].from_second()
+        planes[OUT].from_second()
         total = vec[...]
         for k in range(1, n_ctx):
             g = lax.rem(c + k, n_ctx)
@@ -1152,7 +1143,8 @@
         vec_mid[...] = total
         for k in range(1, n_wsh):
             send(vec_mid, vec_line.at[z], vl_send.at[k], vl_recv.at[z], c, lax.rem(z + k, n_wsh))
-        plane_w.from_diag()
+        plane_w[1].from_diag()
+        planes[OUT].from_diag()
         for k in range(1, n_wsh):
             s = lax.rem(z + k, n_wsh)
             arrive(vec_line.at[s], vl_send.at[0], vl_recv.at[s], c, z)
@@ -1160,31 +1152,24 @@
         vec_sum[...] = total
         own_vec = pltpu.make_async_copy(vec_sum, vec_out, local_sem.at[12])
         own_vec.start()
-        for plane in planes + [plane_w]:
+        for plane in planes + plane_w:
             all_others(plane)
             plane.finish()
         for i in range(n_ctx // 2):
-            left(part.at[0], hp_send.at[i], hp_recv.at[i], c, z)
+            left(part(c), hp_send.at[i], hp_recv.at[i], c, z)
         for i in range(2):
-            left(part.at[0], hf_send.at[i], hf_recv.at[i], c, z)
-        left(part.at[0], hs_send.at[0], hs_recv.at[0], c, z)
-        for copy in (own_fin, own_gtok, own_vec):
+            left(part(c), hf_send.at[i], hf_recv.at[i], c, z)
+        left(part(c), hs_send.at[0], hs_recv.at[0], c, z)
+        for copy in (own_gtok, own_vec, *[own_window(h) for h in range(heads)]):
             copy.wait()
 
     pl.run_scoped(
         attention_backward,
-        vm((n_ctx, rows, width), bf16), vm((n_ctx, heads, 128, rows), bf16), vm((heads, length, 128), bf16),
-        vm((heads, length, 128), bf16), vm((heads, length, 128), f32), vm((heads, length, 128), f32),
-        vm((w_c.shape[1], length), bf16), vm((n_ctx, width, rows), bf16),
-    )
-
-    for i in range(2):
-        tokens[i].finish()
+        vm((n_ctx, heads, 128, rows), bf16), vm((heads, length, 128), bf16), vm((heads, length, 128), bf16),
+        vm((heads, length, 128), f32), vm((heads, length, 128), f32), vm((w_c.shape[1], length), bf16),
+    )
+
     wline.finish(wqkv_ref)
-    for w in range(3):
-        lines[w].finish(my_piece[w])
-    for distance in range(1, n_wsh):
-        shards_at(distance, Plane.finish)
     for k in range(1, n_wsh):
         left(pack_ref, pk_send.at[k], pk_recv.at[z], c, z)
         left(vec, vl_send.at[k], vl_recv.at[0], c, z)
@@ -1194,16 +1179,16 @@
         left(go_land.at[0], go_send.at[k], go_recv.at[0], c, z)
         left(vec, vp_send.at[k], vp_recv.at[0], c, z)
     for w in range(3):
-        pltpu.make_async_copy(fin3.at[w], out_piece(w, c), local_sem.at[8 + w]).wait()
+        pltpu.make_async_copy(final_piece(w), out_piece(w, c), local_sem.at[8 + w]).wait()
         left(land_f.at[w], f_send.at[w], f_recv.at[w], c, z)
         left(land_s.at[w], s_send.at[w], s_recv.at[w], c, z)
-        for k in range(1, n_wsh):
-            left(land_z.at[w, 0], z_send.at[w, k], z_recv.at[w, 0], c, z)
-    for s in range(n_wsh):
-
-        @pl.when(z != s)
-        def _():
-            left(win_out.at[s], w_send.at[s], w_recv.at[s], c, z)
+        for j in range(2):
+            left(land_near.at[w, j], zn_send.at[w, j], zn_recv.at[w, j], c, z)
+        left(land_far.at[w], zf_send.at[w], zf_recv.at[w], c, z)
+    for h in range(heads):
+        for j in range(2):
+            left(win_near.at[h, j], wn_send.at[h, j], wn_recv.at[h, j], c, z)
+        left(win_far.at[h], wf_send.at[h], wf_recv.at[h], c, z)
 
 
 def whole_call(dims, tok, cot, wqkv, w3, pack, order, lengths):
@@ -1221,20 +1206,17 @@
     wide = (rows, width)
     outs = (
         shape(wide, bf16), shape(wide, bf16),
-        shape((shard, width), bf16), shape((shard, width), bf16), shape((shard, width), bf16),
-        shape((n_ctx, 3 * span, size), bf16), shape((8, width), f32),
-        shape((n_ctx, rows, width), bf16), shape((3, width, width), bf16), shape((n_ctx, rows, width), bf16),
-        shape((3, n_wsh, shard, half), bf16),
+        shape((3, shard, width), bf16), shape((n_ctx, heads, 3 * hd, size), bf16), shape((8, width), f32),
     )
     scratch = [
-        vm(( width, wqkv.shape[1]), bf16), vm((n_wsh,) + pack.shape, f32), vm((8, width), f32),
+        vm((n_ctx, rows, width), bf16), vm((3, width, width), bf16), vm((length, width), bf16),
+        vm((width, wqkv.shape[1]), bf16), vm((n_wsh,) + pack.shape, f32), vm((8, width), f32),
         vm((heads, length, 128), bf16), vm((heads, length, 128), bf16), vm((heads, hd, length), bf16),
         vm((n_ctx, heads, 128, rows), bf16), vm((n_ctx, span, rows), f32), vm((n_ctx, span, rows), f32),
         vm((n_ctx, span, rows), bf16), vm((width, rows), bf16), vm((width, rows), bf16), vm((n_ctx, span, rows), bf16),
         vm((3, n_wsh, shard, half), bf16), vm((3, n_wsh, 2 * cut, half), bf16), vm((3, n_wsh, cut, half), bf16),
-        vm((3, n_wsh, cut, half), bf16), vm((3, cut, half), bf16),
-        vm((n_wsh, 3 * span, size), bf16), vm((n_wsh, 3 * span, size), bf16), vm((3 * span, size), bf16),
-        vm((n_ctx // 2, width, rows), bf16), vm((2, width, rows), bf16), vm((width, rows), bf16),
+        vm((3, 2, cut, half), bf16), vm((3, cut, half), bf16),
+        vm((heads, n_wsh, 3 * hd, size), bf16), vm((heads, 2, 3 * hd, size), bf16), vm((heads, 3 * hd, size), bf16),
         vm(wide, f32), vm(wide, f32), vm(wide, bf16), vm(wide, bf16), vm(wide, bf16),
         vm((8, width), f32), vm((n_ctx, 8, width), f32), vm((n_wsh, 8, width), f32), vm((8, width), f32),
         vm((8, width), f32), vm((hd, rows), f32),
@@ -1242,10 +1224,10 @@
         dma((n_ctx,)), dma((n_ctx,)), dma((3, 2 * n_wsh)), dma((3, n_wsh)),
         dma((3, n_wsh, 7)), dma((3, n_wsh, n_ctx)),
         dma((n_ctx,)), dma((n_ctx,)), dma((3,)), dma((3,)), dma((3,)), dma((3,)), dma((3,)), dma((3,)),
-        dma((3, n_wsh)), dma((3, n_wsh)), dma((3, 7)), dma((3, n_ctx)),
+        dma((3, 2)), dma((3, 2)), dma((3,)), dma((3,)), dma((3, 7)), dma((3, n_ctx)),
         dma((n_ctx // 2,)), dma((n_ctx // 2,)), dma((2,)), dma((2,)), dma((1,)), dma((1,)),
-        dma((n_wsh,)), dma((n_wsh,)), dma((7,)), dma((n_ctx,)),
-        dma((n_ctx,)), dma((n_ctx,)), dma((n_wsh,)), dma((n_wsh,)), dma((13,)), dma((2,)), dma((2 + 3 * n_wsh,)),
+        dma((heads, 2)), dma((heads, 2)), dma((heads,)), dma((heads,)), dma((heads, 7)), dma((heads, n_ctx)),
+        dma((n_ctx,)), dma((n_ctx,)), dma((n_wsh,)), dma((n_wsh,)), dma((13,)), dma((heads + 3,)),
     ]
     return pl.pallas_call(
         functools.partial(whole_kernel, dims),
@@ -1257,6 +1239,77 @@
             collective_id=0, has_side_effects=True, vmem_limit_bytes=VMEM_BYTES
         ),
     )(tok, cot, wqkv, *w3, pack, order, lengths)
+
+
+def finish_kernel(dims, dwqkv_ref, dw3_ref, *refs):
+    outs, (pieces, plain, wide, turned, results, in_sem, out_sem) = refs[:6], refs[6:]
+    n_ctx, n_wsh, hd, heads = dims
+    z = lax.axis_index("wsh")
+    f32 = jnp.float32
+    shard, width = outs[0].shape
+    starts, size = windows(width, n_wsh)
+    offset = jnp.int32(0)
+    for s in range(n_wsh):
+        offset = jnp.where(z == s, s * shard - starts[s], offset)
+    ins = [pltpu.make_async_copy(dw3_ref.at[w], plain.at[w], in_sem.at[w]) for w in range(3)]
+    for i in range(3):
+        at = pl.ds(i * hd, hd)
+        ins.append(pltpu.make_async_copy(dwqkv_ref.at[:, :, at], pieces.at[i], in_sem.at[3 + i]))
+    for copy in ins:
+        copy.start()
+    done = []
+
+    def store(i):
+        copy = pltpu.make_async_copy(results.at[i], outs[i], out_sem.at[i])
+        copy.start()
+        done.append(copy)
+
+    for w in range(3):
+        ins[w].wait()
+        results[3 + w] = plain[w].astype(f32)
+        store(3 + w)
+    for i in range(3):
+        ins[3 + i].wait()
+
+        def lay(b, _):
+            for h in range(heads):
+                at = pl.ds(pl.multiple_of((b * heads + h) * hd, 16), hd)
+                wide[at, :] = pieces[i, b, h].astype(f32)
+            return 0
+
+        lax.fori_loop(0, n_ctx, lay, 0)
+
+        def turn(j, _):
+            at = pl.ds(pl.multiple_of(j * 128, 128), 128)
+            turned[:, at] = wide[at, :].T
+            return 0
+
+        lax.fori_loop(0, width // 128, turn, 0)
+        results[i] = turned[pl.ds(pl.multiple_of(offset, 8), shard), :]
+        store(i)
+    for copy in done:
+        copy.wait()
+
+
+def finish_call(dims, dwqkv, dw3):
+    n_ctx, n_wsh, hd, heads = dims
+    shard, width = dw3.shape[1:]
+    size = dwqkv.shape[3]
+    f32, bf16 = jnp.float32, jnp.bfloat16
+    hbm = pl.BlockSpec(memory_space=pl.ANY)
+    dma = pltpu.SemaphoreType.DMA
+    return pl.pallas_call(
+        functools.partial(finish_kernel, dims),
+        out_shape=(jax.ShapeDtypeStruct((shard, width), f32),) * 6,
+        in_specs=[hbm] * 2,
+        out_specs=[hbm] * 6,
+        scratch_shapes=[
+            pltpu.VMEM((3, n_ctx, heads, hd, size), bf16), pltpu.VMEM((3, shard, width), bf16),
+            pltpu.VMEM((width, size), f32), pltpu.VMEM((size, width), f32), pltpu.VMEM((6, shard, width), f32),
+            dma((6,)), dma((6,)),
+        ],
+        compiler_params=pltpu.CompilerParams(vmem_limit_bytes=VMEM_BYTES),
+    )(dwqkv, dw3)
 
 
 def head_split(
@@ -1271,23 +1324,18 @@
     span, shard = hd * heads, width // n_wsh
     dims = (n_ctx, n_wsh, hd, heads)
     mine = [lax.dynamic_slice_in_dim(w, c * span, span, 1) for w in (w_query, w_key, w_value)]
+    mine = [w[:, h * hd : (h + 1) * hd] for h in range(heads) for w in mine]
     lanes = -(-3 * span // 128) * 128
     wqkv = jnp.pad(jnp.concatenate(mine, 1), ((0, 0), (0, lanes - 3 * span)))
     lanes = -(-shard // 128) * 128
-    pack = jnp.concatenate(
-        [jnp.pad(v.astype(f32), (0, lanes - v.shape[0]))[None] for v in (gain_attn, gain_mlp, query_scale)]
-        + [jnp.zeros((5, lanes), f32)]
-    )
-    outputs, gtok, dwo, dwu, dwd, dwqkv, sums = whole_call(
+    pack = sum(
+        jnp.pad(v.astype(f32)[None], ((i, 7 - i), (0, lanes - v.shape[0])))
+        for i, v in enumerate((gain_attn, gain_mlp, query_scale))
+    )
+    outputs, gtok, dw3, dwqkv, sums = whole_call(
         dims, tokens[0], cotangent[0], wqkv, (w_out, w_up, w_down), pack, group_order, block_lengths
-    )[:7]
-    starts, size = windows(width, n_wsh)
-    at = z * shard - jnp.asarray(starts, jnp.int32)[z]
-    dwqkv = dwqkv.reshape(n_ctx, 3, span, size)
-    projections = [
-        lax.dynamic_slice_in_dim(dwqkv[:, i], at, shard, 2).transpose(2, 0, 1).reshape(shard, width).astype(f32)
-        for i in range(3)
-    ]
+    )[:5]
+    weight_grads = finish_call(dims, dwqkv, dw3)
     own = [lax.dynamic_slice_in_dim(sums[i], z * shard, shard, 0) for i in (0, 1)]
     scale_grad = (
         lax.dynamic_slice_in_dim(sums[2], z * (hd // n_wsh), hd // n_wsh, 0)
@@ -1295,8 +1343,7 @@
         * jax.nn.sigmoid(query_scale.astype(f32))
     )
     return (
-        outputs.reshape(tokens.shape), gtok.reshape(tokens.shape), *projections,
-        dwo.astype(f32), dwu.astype(f32), dwd.astype(f32), own[0], own[1], scale_grad,
+        outputs.reshape(tokens.shape), gtok.reshape(tokens.shape), *weight_grads, own[0], own[1], scale_grad,
     )
 
 

time: 251 us -> 224 us (0.89); the launches traced: 247 us -> 224 us
  other arithmetic: 13.3 us -> 1.86 us
  local copies, waits for them, and re-layouts: 15.3 us -> 9.2 us
  Pallas kernels: 217 us -> 212 us
    pallas_call x1, Pallas kernels: 217 us -> 204 us  [whole_call(): pl.pallas_call(functools.partial(whole_kernel, dims), out_shape=outs, in_...]
    convert_element_type x6 -> x0, other arithmetic: 9.78 us -> none  [the longest x3 4.7 us: head_split(): lax.dynamic_slice_in_dim(dwqkv[:, i], at, shard, 2).transpose(2, 0, 1)]
    pallas_call x0 -> x1, Pallas kernels: none -> 8.08 us  [finish_call(): pl.pallas_call(functools.partial(finish_kernel, dims), out_shape=(jax.Sha...]
    unnamed x19 -> x8, local copies, waits for them, and re-layouts: 6.81 us -> 2.15 us
where the time goes in v3:
time: 224 us
  Pallas kernels  212 us (95%)
  local copies, waits for them, and re-layouts  9.2 us (4%)
    pallas_call x1, Pallas kernels, whole_call(): pl.pallas_call(functools.partial(whole_kernel, dims), out_shape=outs, in_...  204 us
    pallas_call x1, Pallas kernels, finish_call(): pl.pallas_call(functools.partial(finish_kernel, dims), out_shape=(jax.Sha...  8.08 us

profile of v3, /device:TPU:0, one launch (start us, length us, event | category | flops | bytes accessed | tf_op | source)
XLA Modules:
  0.0 223.8 jit_solution(6398905309751113763)
XLA Ops:
  0.6 0.7 convert_bitcast_fusion
  1.3 0.7 broadcast_in_dim.11
  2.0 0.7 broadcast_in_dim.12
  2.7 0.6 pad_add_fusion.pack_ref
  3.3 1.1 constant_dynamic-slice_fusion.8
  4.4 1.3 constant_dynamic-slice_fusion.6
  5.7 0.2 concatenate.3
  6.0 0.8 pad.22.wqkv_ref
  6.7 0.0 copy-start.2
  6.7 203.9 %shard_map.212 = (bf16[256,1280]{1,0:T(8,128)(2,1)}, bf16[256,1280]{1,0:T(8,128)(2,1)}, bf16[3,320,1280]{2,1,0:T(8,128)(2,1)}, bf16[8,2,240,384]{3,2,1,0:T(8,128)(2,1)}, f32[8,1280]{1,0:T(8,128)}) custom-call(bf16[256,1280]{1,0:T(8,128)(2,1)} %bitcast.12, bf16[256,1280]{1,0:T(8,128)(2,1)} %bitcast.13, bf16[320,512]{1,0:T(8,128)(2,1)} %pad.22.wqkv_ref, ...), custom_call_target="tpu_custom_call" | custom-call | tf_op jit(solution)/shard_map/pallas_call | solution.py:1232
  210.7 0.9 fusion.4
  211.6 0.0 copy-done.2
  211.6 0.6 divide_multiply_fusion
  212.2 0.7 fusion.1
  212.9 0.7 fusion
  213.5 0.0 copy-start.1
  213.5 8.1 %shard_map.213 = (f32[320,1280]{1,0:T(8,128)}, f32[320,1280]{1,0:T(8,128)}, f32[320,1280]{1,0:T(8,128)}, f32[320,1280]{1,0:T(8,128)}, f32[320,1280]{1,0:T(8,128)}, /*index=5*/f32[320,1280]{1,0:T(8,128)}) custom-call(bf16[8,2,240,384]{3,2,1,0:T(8,128)(2,1)} %get-tuple-element.24.dwqkv_ref, bf16[3,320,1280]{2,1,0:T(8,128)(2,1)} %get-tuple-element.25.dw3_ref), custom_call_target="tpu_custom_call" | custom-call | tf_op jit(solution)/shard_map/pallas_call | solution.py:1301
  221.6 0.0 copy-start
  221.6 0.0 copy-done.1
  221.6 0.8 copy.26
  222.5 0.5 copy-done
  222.9 0.8 copy.27
Async XLA Ops:
  6.7 204.8 %copy-start.2 = (bf16[20]{0:T(256)(128)(2,1)S(1)}, bf16[20]{0:T(256)(128)(2,1)}, u32[]{:S(2)}) copy-start(bf16[20]{0:T(256)(128)(2,1)} %param.25) | copy-start | bytes 124
  213.5 8.1 %copy-start.1 = (bf16[256,1280]{1,0:T(8,128)(2,1)S(1)}, bf16[256,1280]{1,0:T(8,128)(2,1)}, u32[]{:S(2)}) copy-start(bf16[256,1280]{1,0:T(8,128)(2,1)} %get-tuple-element.22) | copy-start | bytes 1966084
  221.6 1.3 copy-start

commit v4 on v3

--- a/solution.py
+++ b/solution.py
@@ -497,13 +497,13 @@
     tok_ref, cot_ref, wqkv_ref, wout_ref, wup_ref, wdown_ref, pack_ref, order_ref, lengths_ref,
     out_out, gtok_out, dw3_out, dwqkv_out, vec_out,
     h1_all, w_full, big, w_c, packs, gains, kaug, vaug, kt, qaug, qraw, o_all, ob_stage, ob_land, go_stage, go_land,
-    acc, land_f, land_s, land_near, land_far, win_out, win_near, win_far,
-    dx, dh, tok, cot, gtok, vec, vec_plane, vec_line, vec_mid, vec_sum, scale_acc,
+    acc, land_f, land_s, land_near, land_far, deep_near, deep_far, deep_f, deep_s, win_out, win_near, win_far,
+    dx, dh, tok, cot, gtok, vec, vec_plane, vec_line, vec_mid, vec_sum, row, row_plane, row_line, row_mid, scale_acc,
     tok_send, tok_recv, wz_send, wz_recv, pk_send, pk_recv, ob_send, ob_recv,
     w3z_send, w3z_recv, w3p_send, w3p_recv,
     go_send, go_recv, p_send, p_recv, f_send, f_recv, s_send, s_recv, zn_send, zn_recv, zf_send, zf_recv, g_send, g_recv,
     hp_send, hp_recv, hf_send, hf_recv, hs_send, hs_recv, wn_send, wn_recv, wf_send, wf_recv, wg_send, wg_recv,
-    vp_send, vp_recv, vl_send, vl_recv, local_sem, load_sem,
+    vp_send, vp_recv, vl_send, vl_recv, rp_send, rp_recv, rl_send, rl_recv, local_sem, load_sem,
 ):
     n_ctx, n_wsh, hd, heads = dims
     f32, bf16 = jnp.float32, jnp.bfloat16
@@ -517,7 +517,18 @@
     two, cut = shard // 2, shard // (n_ctx // 2)
     w3_refs = (wout_ref, wup_ref, wdown_ref)
     OUT, UP, DOWN = 0, 1, 2
-    from_first, from_second, from_diag = Plane.from_first, Plane.from_second, Plane.from_diag
+    own_tok = pltpu.make_async_copy(tok_ref, tok, local_sem.at[0])
+    own_w = pltpu.make_async_copy(wqkv_ref, w_c.at[pl.ds(pl.multiple_of(z * shard, 16), shard)], local_sem.at[1])
+    own_pack = pltpu.make_async_copy(pack_ref, packs.at[z], local_sem.at[2])
+    own_cot = pltpu.make_async_copy(cot_ref, cot, local_sem.at[3])
+    own_full = [
+        pltpu.make_async_copy(
+            w3_refs[w], w_full.at[w, pl.ds(pl.multiple_of(z * shard, 16), shard)], load_sem.at[heads + w]
+        )
+        for w in range(3)
+    ]
+    for copy in (own_tok, own_pack, own_w, own_cot, *own_full):
+        copy.start()
     enter(c, z, n_ctx, n_wsh)
 
     part_rows = rows // 2
@@ -534,19 +545,6 @@
     for k in range(1, n_wsh):
         send(pack_ref, packs.at[z], pk_send.at[k], pk_recv.at[z], c, lax.rem(z + k, n_wsh))
     wline.start(wqkv_ref)
-    own_tok = pltpu.make_async_copy(tok_ref, tok, local_sem.at[0])
-    own_w = pltpu.make_async_copy(wqkv_ref, wline.at(z), local_sem.at[1])
-    own_pack = pltpu.make_async_copy(pack_ref, packs.at[z], local_sem.at[2])
-    own_cot = pltpu.make_async_copy(cot_ref, cot, local_sem.at[3])
-    own_full = [
-        pltpu.make_async_copy(
-            w3_refs[w], w_full.at[w, pl.ds(pl.multiple_of(z * shard, 16), shard)], load_sem.at[heads + w]
-        )
-        for w in range(3)
-    ]
-    for copy in (own_tok, own_pack, own_w, own_cot, *own_full):
-        copy.start()
-    vec[...] = jnp.zeros_like(vec)
     scale_acc[...] = jnp.zeros_like(scale_acc)
 
     def columns(b):
@@ -565,22 +563,24 @@
         k = lax.rem(s - z + n_wsh, n_wsh)
         return Plane(lambda b: piece(w, s, b), c, z, around, w3p_send.at[w, k], w3p_recv.at[w, k])
 
-    def shards_at(distance, step, weights=(0, 1, 2)):
+    def shards_at(w, distance, step):
         below, above = z - distance, z + distance
 
         @pl.when(below >= 0)
         def _():
-            for w in weights:
-                step(plane_of(w, below))
+            step(plane_of(w, below))
 
         @pl.when(above < n_wsh)
         def _():
-            for w in weights:
-                step(plane_of(w, above))
-
-    def spread(distance):
-        for w in range(3):
-            lines[w].forward(distance, lambda s, w=w: plane_of(w, s).start())
+            step(plane_of(w, above))
+
+    def spread(w, distance):
+        lines[w].forward(distance, lambda s: plane_of(w, s).start())
+
+    def step_of(step):
+        return lambda w, distance: shards_at(w, distance, step)
+
+    by_first, by_second, by_diag = step_of(Plane.from_first), step_of(Plane.from_second), step_of(Plane.from_diag)
 
     def all_others(plane):
         for b in plane.others():
@@ -626,27 +626,30 @@
             norm_arrived(b)
 
         others = tokens[0].others()
+        lines[OUT].start(my_piece[OUT])
         norm_block(c, tok, 0)
         arrived(others[0])
         tokens[0].from_first()
         wline.forward(1)
+        lines[UP].start(my_piece[UP])
         tokens[1].from_first()
         norm_arrived(first)
         tokens[0].from_second()
         tokens[1].from_second()
         norm_arrived(second)
+        spread(OUT, 1)
         wline.forward(2)
-        for w in range(3):
-            lines[w].start(my_piece[w])
+        lines[DOWN].start(my_piece[DOWN])
         arrived(others[1])
         arrived(others[2])
         tokens[0].from_diag()
         tokens[1].from_diag()
         norm_arrived(diag)
         arrived(others[3])
+        spread(OUT, 2)
         wline.forward(3)
         own_w.wait()
-        spread(1)
+        spread(UP, 1)
         gain_col = gain_column()
 
         def project(b, _):
@@ -679,9 +682,14 @@
         for i in range(2):
             tokens[i].finish()
         keys = length // 2
-        events = (
-            ((0, lambda: spread(2)), (2, lambda: shards_at(1, from_first)), (4, lambda: shards_at(1, from_second))),
-            ((3, lambda: spread(3)), (5, lambda: shards_at(2, from_first)), (6, lambda: shards_at(1, from_diag))),
+        plan = (
+            (0, spread, OUT, 3), (0, by_first, OUT, 1), (1, by_first, OUT, 2), (1, spread, UP, 2),
+            (2, by_second, OUT, 1), (2, by_second, OUT, 2), (3, spread, DOWN, 1), (3, by_first, OUT, 3),
+            (4, by_diag, OUT, 1), (4, spread, UP, 3), (5, by_second, OUT, 3), (5, by_first, UP, 1),
+            (6, spread, DOWN, 2), (6, by_diag, OUT, 2), (7, by_first, UP, 2), (8, by_diag, OUT, 3),
+            (8, by_second, UP, 1), (9, by_second, UP, 2), (9, spread, DOWN, 3), (10, by_first, UP, 3),
+            (11, by_diag, UP, 1), (11, by_first, DOWN, 1), (12, by_second, UP, 3), (12, by_diag, UP, 2),
+            (13, by_first, DOWN, 2), (14, by_second, DOWN, 1), (14, by_diag, UP, 3), (15, by_second, DOWN, 2),
         )
 
         def attend(i, _):
@@ -703,8 +711,9 @@
                 o_all[g, h * hd : (h + 1) * hd, :] = o
                 ob_stage[g, h * hd : (h + 1) * hd, :] = o.astype(bf16)
                 qaug[g, h, hd : hd + 16, :] = jnp.concatenate([qneg[g], three_rows(-lse, rows)], axis=0).astype(bf16)
-                for step, event in events[h]:
-                    pl.when(i == step)(event)
+                for slot, event, w, distance in plan:
+                    if slot % heads == h:
+                        pl.when(i == slot // heads)(functools.partial(event, w, distance))
 
             @pl.when(i < n_ctx - 1)
             def _():
@@ -736,13 +745,46 @@
     def pair_at(w):
         return big.at[pl.ds(2 * w * shard, 2 * shard)]
 
-    def pair_sum(w):
+    def add_pair(w):
         arrive(pair_at(w), p_send.at[w], p_recv.at[w], c, z)
         for s in range(n_wsh):
             other = big.at[:, pl.ds(s % 2 * half, half)]
             add_rows(acc.at[w, s], 0, other, (2 * w + s // 2) * shard, shard, 64)
+
+    def pair_sum(w):
+        add_pair(w)
         at = pl.ds(pl.multiple_of((1 - f_bit) * two, 16), two)
         send(acc.at[w, :, at], land_f.at[w], f_send.at[w], f_recv.at[w], first, z)
+
+    def deep_pair_sum(w):
+        add_pair(w)
+        for j in range(2):
+            s = 2 * j + lax.rem(near, 2)
+            send(acc.at[w, s], deep_near.at[j], zn_send.at[w, j], zn_recv.at[w, j], c, near)
+
+    def deep_near_sum(w):
+        for j in range(2):
+            arrive(deep_near.at[j], zn_send.at[w, j], zn_recv.at[w, j], c, z)
+            add_rows(acc.at[w, 2 * j + lax.rem(z, 2)], 0, deep_near.at[j], 0, shard, 80)
+        send(acc.at[w, far], deep_far, zf_send.at[w], zf_recv.at[w], c, far)
+
+    def deep_far_sum(w):
+        arrive(deep_far, zf_send.at[w], zf_recv.at[w], c, z)
+        add_rows(acc.at[w, z], 0, deep_far, 0, shard, 80)
+        at = pl.ds(pl.multiple_of((1 - f_bit) * two, 16), two)
+        send(acc.at[w, z, at], deep_f, f_send.at[w], f_recv.at[w], first, z)
+
+    def deep_first_sum(w):
+        arrive(deep_f, f_send.at[w], f_recv.at[w], c, z)
+        add_rows(acc.at[w, z], f_bit * two, deep_f, 0, two, 80)
+        at = pl.ds(pl.multiple_of(f_bit * two + (1 - s_bit) * cut, 16), cut)
+        send(acc.at[w, z, at], deep_s, s_send.at[w], s_recv.at[w], second, z)
+
+    def deep_second_sum(w):
+        arrive(deep_s, s_send.at[w], s_recv.at[w], c, z)
+        add_rows(acc.at[w, z], my_top, deep_s, 0, cut, 80)
+        planes[w].start(final_piece(w))
+        pltpu.make_async_copy(final_piece(w), out_piece(w, c), local_sem.at[8 + w]).start()
 
     def first_sum(w):
         arrive(land_f.at[w], f_send.at[w], f_recv.at[w], c, z)
@@ -787,11 +829,8 @@
 
     def feed_forward(x1, h2, a, gu, ob, turned, ga, inv2, outb, stage):
         def tiles(step, size=256):
-            def one(i, _):
-                step(pl.ds(pl.multiple_of(i * size, size), size))
-                return 0
-
-            lax.fori_loop(0, width // size, one, 0)
+            for top in range(0, width, size):
+                step(slice(top, top + size))
 
         def turn(source, target):
             def one(at):
@@ -809,15 +848,9 @@
                 at = slice(s * shard, (s + 1) * shard)
                 acc[w, s] = jnp.dot(left_t[at, :], right[:, mine], preferred_element_type=f32).astype(bf16)
 
-        shards_at(3, from_first, (OUT,))
-        shards_at(2, from_second, (OUT,))
-        shards_at(3, from_second, (OUT,))
-        shards_at(2, from_diag, (OUT,))
-        shards_at(3, from_diag, (OUT,))
-        shards_at(3, from_first, (UP, DOWN))
-        shards_at(2, from_second, (UP, DOWN))
+        by_first(DOWN, 3)
         for distance in range(1, n_wsh):
-            shards_at(distance, all_others, (OUT,))
+            shards_at(OUT, distance, all_others)
         own_o.wait()
         for k in range(1, n_ctx):
             g = lax.rem(c + k, n_ctx)
@@ -827,17 +860,15 @@
             ob[:, at] = ob_land[at, :].T
 
         tiles(turn_ob, 128)
-        shards_at(3, from_second, (UP, DOWN))
-        shards_at(2, from_diag, (UP, DOWN))
+        by_diag(DOWN, 1)
+        by_second(DOWN, 3)
         own_full[OUT].wait()
 
         def mix(at):
             x1[:, at] = tok[:, at].astype(f32) + jnp.dot(ob[...], w_full[OUT, :, at], preferred_element_type=f32)
 
         tiles(mix)
-        shards_at(3, from_diag, (UP, DOWN))
-        for distance in range(1, n_wsh):
-            shards_at(distance, all_others, (UP, DOWN))
+        by_diag(DOWN, 2)
 
         def norm_rows(i, _):
             at = pl.ds(pl.multiple_of(i * 32, 32), 32)
@@ -848,12 +879,22 @@
             return 0
 
         lax.fori_loop(0, rows // 32, norm_rows, 0)
+        by_diag(DOWN, 3)
+        for distance in range(1, n_wsh):
+            shards_at(UP, distance, all_others)
+        own_full[UP].wait()
+
+        def lift(at):
+            dh[:, at] = jnp.dot(h2[...], w_full[UP, :, at], preferred_element_type=f32)
+
+        tiles(lift)
         own_cot.wait()
-        own_full[UP].wait()
+        for distance in range(1, n_wsh):
+            shards_at(DOWN, distance, all_others)
         own_full[DOWN].wait()
 
         def hidden(at):
-            up = jnp.dot(h2[...], w_full[UP, :, at], preferred_element_type=f32)
+            up = dh[:, at]
             da = lax.dot_general(
                 cot[...], w_full[DOWN, at, :], (((1,), (1,)), ((), ())), preferred_element_type=f32
             )
@@ -886,7 +927,7 @@
             return total + both
 
         gain_sum = lax.fori_loop(0, rows // 16, norm_back_rows, jnp.zeros((16, width), f32))
-        vec[1:2, :] = jnp.sum(gain_sum, axis=0, keepdims=True)
+        vec[:, 0:width] = jnp.sum(gain_sum, axis=0, keepdims=True)
 
         def back_out(at):
             go_stage[at, :] = lax.dot_general(
@@ -896,16 +937,17 @@
         tiles(back_out)
         for w in range(3):
             lines[w].finish(my_piece[w])
-        for distance in range(1, n_wsh):
-            shards_at(distance, Plane.finish)
+            for distance in range(1, n_wsh):
+                shards_at(w, distance, Plane.finish)
         for k in range(1, n_ctx):
             g = lax.rem(c + k, n_ctx)
             send(heads_of(go_stage, g), go_land.at[c], go_send.at[k], go_recv.at[c], g, z)
         pltpu.make_async_copy(my_heads(go_stage), go_land.at[c], local_sem.at[5]).start()
-        pair_sum(DOWN)
+        deep_pair_sum(DOWN)
         turn(h2, turned)
         weight_gradient(UP, turned, gu)
         weight_gradient(OUT, ob_land, ga)
+        pair_sum(UP)
 
         def finish(at):
             outb[:, at] = (
@@ -915,7 +957,6 @@
         tiles(finish)
         own_out = pltpu.make_async_copy(outb, out_out, local_sem.at[6])
         own_out.start()
-        pair_sum(UP)
         pair_sum(OUT)
         own_out.wait()
         for w in range(3):
@@ -974,21 +1015,17 @@
             return 0
 
         lax.fori_loop(1, n_ctx, prepare_other, 0)
-        chunk = length // 2
         three = 3 * hd
         starts, size = windows(width, n_wsh)
 
         def head_gradients(h, events):
             def attend(g, _):
                 at = pl.ds(pl.multiple_of(g * rows, 16), rows)
-                dq = jnp.zeros((hd, rows), f32)
-                for j in range(2):
-                    keys = slice(j * chunk, (j + 1) * chunk)
-                    p = jnp.exp(jnp.dot(kaug[h, keys, :], qaug[g, h], preferred_element_type=f32))
-                    ds = (p * jnp.dot(vaug[h, keys, :], goaug[g, h], preferred_element_type=f32)).astype(bf16)
-                    dq = dq + jnp.dot(kt[h, :, keys], ds, preferred_element_type=f32)
-                    dk[h, keys, :] += jnp.dot(ds, q_tm[h, at, :], preferred_element_type=f32)
-                    dv[h, keys, :] += jnp.dot(p.astype(bf16), go_tm[h, at, :], preferred_element_type=f32)
+                p = jnp.exp(jnp.dot(kaug[h], qaug[g, h], preferred_element_type=f32))
+                ds = (p * jnp.dot(vaug[h], goaug[g, h], preferred_element_type=f32)).astype(bf16)
+                dq = jnp.dot(kt[h], ds, preferred_element_type=f32)
+                dk[h] += jnp.dot(ds, q_tm[h, at, :], preferred_element_type=f32)
+                dv[h] += jnp.dot(p.astype(bf16), go_tm[h, at, :], preferred_element_type=f32)
                 scale_acc[...] += dq * qraw[g, h * hd : (h + 1) * hd, :]
                 lanes = pl.ds(pl.multiple_of(g * rows, 128), rows)
                 dqkv[h * three : h * three + hd, lanes] = (dq * gain_col).astype(bf16)
@@ -1008,6 +1045,8 @@
                 return 0
 
             lax.fori_loop(0, n_ctx, settle, 0)
+
+        def head_windows(h):
             for s in range(n_wsh):
                 total = jnp.zeros((three, size), f32)
                 for b in range(n_ctx):
@@ -1039,10 +1078,11 @@
             plane_w[h].start(win_out.at[h, z])
             own_window(h).start()
 
-        head_gradients(0, ((3, lambda: first_sum(DOWN)), (7, lambda: second_sum(DOWN))))
+        head_gradients(0, ((6, lambda: first_sum(UP)),))
+        head_windows(0)
         head_gradients(1, (
-            (0, lambda: first_sum(UP)), (3, lambda: near_sum(DOWN)), (4, lambda: second_sum(UP)),
-            (5, lambda: near_window(0)), (7, lambda: first_sum(OUT)),
+            (1, lambda: second_sum(UP)), (2, lambda: deep_near_sum(DOWN)), (4, lambda: first_sum(OUT)),
+            (5, lambda: near_sum(UP)), (6, lambda: near_window(0)), (7, lambda: second_sum(OUT)),
         ))
 
         def partial(b):
@@ -1056,14 +1096,19 @@
             return 0
 
         lax.fori_loop(0, n_ctx // 2, to_sib, 0)
-        far_sum(DOWN)
-        near_sum(UP)
+        head_windows(1)
 
         def own_core(i, _):
             partial(2 * i + core)
             return 0
 
         lax.fori_loop(0, n_ctx // 2, own_core, 0)
+
+        def scale_row():
+            scale_sum = jnp.sum(scale_acc[...], axis=1, keepdims=True)
+            return jnp.concatenate(
+                [jnp.broadcast_to(scale_sum, (hd, 128)), jnp.zeros((128 - hd, 128), f32)], axis=0
+            ).T[0:1, :]
 
         def pair(i, b):
             arrive(part_p(b // 2), hp_send.at[0], hp_recv.at[b // 2], c, z)
@@ -1074,27 +1119,43 @@
 
         pair(1, diag)
         pair(0, first)
-        second_sum(OUT)
+        deep_far_sum(DOWN)
+        far_sum(UP)
+        near_sum(OUT)
+        vec[:, width:] = scale_row()
+        for k in range(1, n_ctx):
+            g = lax.rem(c + k, n_ctx)
+            send(vec, vec_plane.at[c], vp_send.at[k], vp_recv.at[c], g, z)
         far_window(0)
         pair(2, second)
         pair(3, c)
+        deep_first_sum(DOWN)
         near_window(1)
-        far_sum(UP)
-        near_sum(OUT)
+        planes[UP].from_first()
+        far_sum(OUT)
+        planes[UP].from_second()
         arrive(part_f(1 - s_bit), hf_send.at[0], hf_recv.at[1 - s_bit], c, z)
         add_rows(part(second), 0, part_f(1 - s_bit), 0, width, 128)
         send(part(second), part_s, hs_send.at[0], hs_recv.at[0], second, z)
-        planes[DOWN].from_first()
-        planes[DOWN].from_second()
+        deep_second_sum(DOWN)
         arrive(part_f(s_bit), hf_send.at[0], hf_recv.at[s_bit], c, z)
         add_rows(part(c), 0, part_f(s_bit), 0, width, 128)
         far_window(1)
-        far_sum(OUT)
-        planes[DOWN].from_diag()
         plane_w[0].from_first()
         plane_w[0].from_second()
-        planes[UP].from_first()
-        planes[UP].from_second()
+        planes[UP].from_diag()
+        total = vec[...]
+        for k in range(1, n_ctx):
+            g = lax.rem(c + k, n_ctx)
+            arrive(vec_plane.at[g], vp_send.at[0], vp_recv.at[g], c, z)
+            total = total + vec_plane[g]
+        vec_mid[...] = total
+        for k in range(1, n_wsh):
+            send(vec_mid, vec_line.at[z], vl_send.at[k], vl_recv.at[z], c, lax.rem(z + k, n_wsh))
+        planes[OUT].from_first()
+        planes[OUT].from_second()
+        planes[DOWN].from_first()
+        planes[DOWN].from_second()
         arrive(part_s, hs_send.at[0], hs_recv.at[0], c, z)
 
         mine_part = part(c)
@@ -1118,38 +1179,39 @@
             return total + both
 
         gain_sum = lax.fori_loop(0, rows // 16, last_rows, jnp.zeros((16, width), f32))
-        scale_sum = jnp.sum(scale_acc[...], axis=1, keepdims=True)
-        scale_row = jnp.concatenate(
-            [jnp.broadcast_to(scale_sum, (hd, 128)), jnp.zeros((128 - hd, 128), f32)], axis=0
-        ).T[0:1, :]
-        vec[0:1, :] = jnp.sum(gain_sum, axis=0, keepdims=True)
-        vec[2:3, 0:128] = scale_row
+        row[...] = jnp.sum(gain_sum, axis=0, keepdims=True)
+        for k in range(1, n_ctx):
+            g = lax.rem(c + k, n_ctx)
+            send(row, row_plane.at[c], rp_send.at[k], rp_recv.at[c], g, z)
         own_gtok = pltpu.make_async_copy(gtok, gtok_out, local_sem.at[11])
         own_gtok.start()
+        plane_w[0].from_diag()
+        planes[OUT].from_diag()
+        planes[DOWN].from_diag()
+        plane_w[1].from_first()
+        plane_w[1].from_second()
+        total = row[...]
         for k in range(1, n_ctx):
             g = lax.rem(c + k, n_ctx)
-            send(vec, vec_plane.at[c], vp_send.at[k], vp_recv.at[c], g, z)
-        plane_w[0].from_diag()
-        planes[UP].from_diag()
-        plane_w[1].from_first()
-        planes[OUT].from_first()
-        plane_w[1].from_second()
-        planes[OUT].from_second()
-        total = vec[...]
-        for k in range(1, n_ctx):
-            g = lax.rem(c + k, n_ctx)
-            arrive(vec_plane.at[g], vp_send.at[0], vp_recv.at[g], c, z)
-            total = total + vec_plane[g]
-        vec_mid[...] = total
+            arrive(row_plane.at[g], rp_send.at[0], rp_recv.at[g], c, z)
+            total = total + row_plane[g]
+        row_mid[...] = total
         for k in range(1, n_wsh):
-            send(vec_mid, vec_line.at[z], vl_send.at[k], vl_recv.at[z], c, lax.rem(z + k, n_wsh))
+            send(row_mid, row_line.at[z], rl_send.at[k], rl_recv.at[z], c, lax.rem(z + k, n_wsh))
         plane_w[1].from_diag()
-        planes[OUT].from_diag()
+        whole = vec_mid[...]
         for k in range(1, n_wsh):
             s = lax.rem(z + k, n_wsh)
             arrive(vec_line.at[s], vl_send.at[0], vl_recv.at[s], c, z)
-            total = total + vec_line[s]
-        vec_sum[...] = total
+            whole = whole + vec_line[s]
+        vec_sum[...] = jnp.zeros_like(vec_sum)
+        vec_sum[1:2, :] = whole[:, 0:width]
+        vec_sum[2:3, 0:128] = whole[:, width:]
+        for k in range(1, n_wsh):
+            s = lax.rem(z + k, n_wsh)
+            arrive(row_line.at[s], rl_send.at[0], rl_recv.at[s], c, z)
+            total = total + row_line[s]
+        vec_sum[0:1, :] = total
         own_vec = pltpu.make_async_copy(vec_sum, vec_out, local_sem.at[12])
         own_vec.start()
         for plane in planes + plane_w:
@@ -1173,18 +1235,20 @@
     for k in range(1, n_wsh):
         left(pack_ref, pk_send.at[k], pk_recv.at[z], c, z)
         left(vec, vl_send.at[k], vl_recv.at[0], c, z)
+        left(row, rl_send.at[k], rl_recv.at[0], c, z)
     for k in range(1, n_ctx):
         g = lax.rem(c + k, n_ctx)
         left(ob_stage.at[g], ob_send.at[g], ob_recv.at[g], c, z)
         left(go_land.at[0], go_send.at[k], go_recv.at[0], c, z)
         left(vec, vp_send.at[k], vp_recv.at[0], c, z)
+        left(row, rp_send.at[k], rp_recv.at[0], c, z)
     for w in range(3):
         pltpu.make_async_copy(final_piece(w), out_piece(w, c), local_sem.at[8 + w]).wait()
-        left(land_f.at[w], f_send.at[w], f_recv.at[w], c, z)
-        left(land_s.at[w], s_send.at[w], s_recv.at[w], c, z)
+        left(deep_f if w == DOWN else land_f.at[w], f_send.at[w], f_recv.at[w], c, z)
+        left(deep_s if w == DOWN else land_s.at[w], s_send.at[w], s_recv.at[w], c, z)
         for j in range(2):
-            left(land_near.at[w, j], zn_send.at[w, j], zn_recv.at[w, j], c, z)
-        left(land_far.at[w], zf_send.at[w], zf_recv.at[w], c, z)
+            left(deep_near.at[j] if w == DOWN else land_near.at[w, j], zn_send.at[w, j], zn_recv.at[w, j], c, z)
+        left(deep_far if w == DOWN else land_far.at[w], zf_send.at[w], zf_recv.at[w], c, z)
     for h in range(heads):
         for j in range(2):
             left(win_near.at[h, j], wn_send.at[h, j], wn_recv.at[h, j], c, z)
@@ -1214,12 +1278,14 @@
         vm((heads, length, 128), bf16), vm((heads, length, 128), bf16), vm((heads, hd, length), bf16),
         vm((n_ctx, heads, 128, rows), bf16), vm((n_ctx, span, rows), f32), vm((n_ctx, span, rows), f32),
         vm((n_ctx, span, rows), bf16), vm((width, rows), bf16), vm((width, rows), bf16), vm((n_ctx, span, rows), bf16),
-        vm((3, n_wsh, shard, half), bf16), vm((3, n_wsh, 2 * cut, half), bf16), vm((3, n_wsh, cut, half), bf16),
-        vm((3, 2, cut, half), bf16), vm((3, cut, half), bf16),
+        vm((3, n_wsh, shard, half), bf16), vm((2, n_wsh, 2 * cut, half), bf16), vm((2, n_wsh, cut, half), bf16),
+        vm((2, 2, cut, half), bf16), vm((2, cut, half), bf16),
+        vm((2, shard, half), bf16), vm((shard, half), bf16), vm((2 * cut, half), bf16), vm((cut, half), bf16),
         vm((heads, n_wsh, 3 * hd, size), bf16), vm((heads, 2, 3 * hd, size), bf16), vm((heads, 3 * hd, size), bf16),
         vm(wide, f32), vm(wide, f32), vm(wide, bf16), vm(wide, bf16), vm(wide, bf16),
-        vm((8, width), f32), vm((n_ctx, 8, width), f32), vm((n_wsh, 8, width), f32), vm((8, width), f32),
-        vm((8, width), f32), vm((hd, rows), f32),
+        vm((1, width + 128), f32), vm((n_ctx, 1, width + 128), f32), vm((n_wsh, 1, width + 128), f32),
+        vm((1, width + 128), f32), vm((8, width), f32), vm((1, width), f32), vm((n_ctx, 1, width), f32), vm((n_wsh, 1, width), f32),
+        vm((1, width), f32), vm((hd, rows), f32),
         dma((2, 7)), dma((2, n_ctx)), dma((2 * n_wsh,)), dma((n_wsh,)), dma((n_wsh,)), dma((n_wsh,)),
         dma((n_ctx,)), dma((n_ctx,)), dma((3, 2 * n_wsh)), dma((3, n_wsh)),
         dma((3, n_wsh, 7)), dma((3, n_wsh, n_ctx)),
@@ -1227,6 +1293,7 @@
         dma((3, 2)), dma((3, 2)), dma((3,)), dma((3,)), dma((3, 7)), dma((3, n_ctx)),
         dma((n_ctx // 2,)), dma((n_ctx // 2,)), dma((2,)), dma((2,)), dma((1,)), dma((1,)),
         dma((heads, 2)), dma((heads, 2)), dma((heads,)), dma((heads,)), dma((heads, 7)), dma((heads, n_ctx)),
+        dma((n_ctx,)), dma((n_ctx,)), dma((n_wsh,)), dma((n_wsh,)),
         dma((n_ctx,)), dma((n_ctx,)), dma((n_wsh,)), dma((n_wsh,)), dma((13,)), dma((heads + 3,)),
     ]
     return pl.pallas_call(

time: 224 us -> 215 us (0.960)
  Pallas kernels: 212 us -> 203 us
    pallas_call x1, Pallas kernels: 204 us -> 195 us  [whole_call(): pl.pallas_call(functools.partial(whole_kernel, dims), out_shape=outs, in_...]
where the time goes in v4:
time: 215 us
  Pallas kernels  203 us (94%)
  local copies, waits for them, and re-layouts  9.2 us (4%)
    pallas_call x1, Pallas kernels, whole_call(): pl.pallas_call(functools.partial(whole_kernel, dims), out_shape=outs, in_...  195 us
    pallas_call x1, Pallas kernels, finish_call(): pl.pallas_call(functools.partial(finish_kernel, dims), out_shape=(jax.Sha...  8.08 us

profile of v4, /device:TPU:0, one launch (start us, length us, event | category | flops | bytes accessed | tf_op | source)
XLA Modules:
  0.0 215.1 jit_solution(2518283346884025539)
XLA Ops:
  0.6 0.7 convert_bitcast_fusion
  1.3 0.7 broadcast_in_dim.11
  2.0 0.7 broadcast_in_dim.12
  2.7 0.6 pad_add_fusion.pack_ref
  3.3 1.1 constant_dynamic-slice_fusion.8
  4.4 1.3 constant_dynamic-slice_fusion.6
  5.7 0.2 concatenate.3
  6.0 0.8 pad.22.wqkv_ref
  6.7 0.0 copy-start.2
  6.7 195.2 %shard_map.212 = (bf16[256,1280]{1,0:T(8,128)(2,1)}, bf16[256,1280]{1,0:T(8,128)(2,1)}, bf16[3,320,1280]{2,1,0:T(8,128)(2,1)}, bf16[8,2,240,384]{3,2,1,0:T(8,128)(2,1)}, f32[8,1280]{1,0:T(8,128)}) custom-call(bf16[256,1280]{1,0:T(8,128)(2,1)} %bitcast.12, bf16[256,1280]{1,0:T(8,128)(2,1)} %bitcast.13, bf16[320,512]{1,0:T(8,128)(2,1)} %pad.22.wqkv_ref, ...), custom_call_target="tpu_custom_call" | custom-call | tf_op jit(solution)/shard_map/pallas_call | solution.py:1299
  202.0 0.9 fusion.4
  202.9 0.0 copy-done.2
  202.9 0.6 divide_multiply_fusion
  203.5 0.7 fusion.1
  204.1 0.7 fusion
  204.8 0.0 copy-start.1
  204.8 8.1 %shard_map.213 = (f32[320,1280]{1,0:T(8,128)}, f32[320,1280]{1,0:T(8,128)}, f32[320,1280]{1,0:T(8,128)}, f32[320,1280]{1,0:T(8,128)}, f32[320,1280]{1,0:T(8,128)}, /*index=5*/f32[320,1280]{1,0:T(8,128)}) custom-call(bf16[8,2,240,384]{3,2,1,0:T(8,128)(2,1)} %get-tuple-element.24.dwqkv_ref, bf16[3,320,1280]{2,1,0:T(8,128)(2,1)} %get-tuple-element.25.dw3_ref), custom_call_target="tpu_custom_call" | custom-call | tf_op jit(solution)/shard_map/pallas_call | solution.py:1368
  212.9 0.0 copy-start
  212.9 0.0 copy-done.1
  212.9 0.8 copy.26
  213.8 0.5 copy-done
  214.2 0.8 copy.27
Async XLA Ops:
  6.7 196.1 %copy-start.2 = (bf16[20]{0:T(256)(128)(2,1)S(1)}, bf16[20]{0:T(256)(128)(2,1)}, u32[]{:S(2)}) copy-start(bf16[20]{0:T(256)(128)(2,1)} %param.25) | copy-start | bytes 124
  204.8 8.1 %copy-start.1 = (bf16[256,1280]{1,0:T(8,128)(2,1)S(1)}, bf16[256,1280]{1,0:T(8,128)(2,1)}, u32[]{:S(2)}) copy-start(bf16[256,1280]{1,0:T(8,128)(2,1)} %get-tuple-element.22) | copy-start | bytes 1966084
  212.9 1.3 copy-start

commit v5 on v4

--- a/solution.py
+++ b/solution.py
@@ -311,7 +311,7 @@
     return c, z, sib, first, second, diag
 
 
-def enter(c, z, n_ctx, n_wsh):
+def greet(c, z, n_ctx, n_wsh):
     barrier = pltpu.get_barrier_semaphore()
     for k in range(1, n_ctx):
         pl.semaphore_signal(
@@ -321,7 +321,10 @@
         pl.semaphore_signal(
             barrier, inc=1, device_id=(c, lax.rem(z + k, n_wsh)), device_id_type=MESH
         )
-    pl.semaphore_wait(barrier, n_ctx + n_wsh - 2)
+
+
+def met(n_ctx, n_wsh):
+    pl.semaphore_wait(pltpu.get_barrier_semaphore(), n_ctx + n_wsh - 2)
 
 
 def send(src, dst, send_sem, recv_sem, c, z):
@@ -494,16 +497,16 @@
 
 def whole_kernel(
     dims,
-    tok_ref, cot_ref, wqkv_ref, wout_ref, wup_ref, wdown_ref, pack_ref, order_ref, lengths_ref,
+    tok_ref, cot_ref, wq_ref, wk_ref, wv_ref, wout_ref, wup_ref, wdown_ref, pack_ref, order_ref, lengths_ref,
     out_out, gtok_out, dw3_out, dwqkv_out, vec_out,
-    h1_all, w_full, big, w_c, packs, gains, kaug, vaug, kt, qaug, qraw, o_all, ob_stage, ob_land, go_stage, go_land,
+    h1_all, w_full, big, w_c, w_own, packs, gains, kaug, vaug, kt, qaug, qraw, o_all, ob_stage, ob_land, go_stage, go_land,
     acc, land_f, land_s, land_near, land_far, deep_near, deep_far, deep_f, deep_s, win_out, win_near, win_far,
     dx, dh, tok, cot, gtok, vec, vec_plane, vec_line, vec_mid, vec_sum, row, row_plane, row_line, row_mid, scale_acc,
     tok_send, tok_recv, wz_send, wz_recv, pk_send, pk_recv, ob_send, ob_recv,
     w3z_send, w3z_recv, w3p_send, w3p_recv,
     go_send, go_recv, p_send, p_recv, f_send, f_recv, s_send, s_recv, zn_send, zn_recv, zf_send, zf_recv, g_send, g_recv,
     hp_send, hp_recv, hf_send, hf_recv, hs_send, hs_recv, wn_send, wn_recv, wf_send, wf_recv, wg_send, wg_recv,
-    vp_send, vp_recv, vl_send, vl_recv, rp_send, rp_recv, rl_send, rl_recv, local_sem, load_sem,
+    vp_send, vp_recv, vl_send, vl_recv, rp_send, rp_recv, rl_send, rl_recv, local_sem, load_sem, cols_sem,
 ):
     n_ctx, n_wsh, hd, heads = dims
     f32, bf16 = jnp.float32, jnp.bfloat16
@@ -518,7 +521,11 @@
     w3_refs = (wout_ref, wup_ref, wdown_ref)
     OUT, UP, DOWN = 0, 1, 2
     own_tok = pltpu.make_async_copy(tok_ref, tok, local_sem.at[0])
-    own_w = pltpu.make_async_copy(wqkv_ref, w_c.at[pl.ds(pl.multiple_of(z * shard, 16), shard)], local_sem.at[1])
+    columns_in = [
+        pltpu.make_async_copy(ref.at[:, pl.ds(side * half, half)], acc.at[i, side], cols_sem.at[i, side])
+        for i, ref in enumerate((wq_ref, wk_ref, wv_ref))
+        for side in range(2)
+    ]
     own_pack = pltpu.make_async_copy(pack_ref, packs.at[z], local_sem.at[2])
     own_cot = pltpu.make_async_copy(cot_ref, cot, local_sem.at[3])
     own_full = [
@@ -527,9 +534,24 @@
         )
         for w in range(3)
     ]
-    for copy in (own_tok, own_pack, own_w, own_cot, *own_full):
+    for copy in (*columns_in, own_tok, own_pack, own_cot, *own_full):
         copy.start()
-    enter(c, z, n_ctx, n_wsh)
+    greet(c, z, n_ctx, n_wsh)
+    for copy in columns_in:
+        copy.wait()
+    for k in range(n_ctx):
+
+        @pl.when(c == k)
+        def _():
+            for h in range(heads):
+                side, at = divmod(k * span + h * hd, half)
+                for i in range(3):
+                    w_own[:, (3 * h + i) * hd : (3 * h + i + 1) * hd] = acc[i, side, :, at : at + hd]
+
+    w_own[:, 3 * span :] = jnp.zeros((shard, w_own.shape[1] - 3 * span), bf16)
+    own_w = pltpu.make_async_copy(w_own, w_c.at[pl.ds(pl.multiple_of(z * shard, 16), shard)], local_sem.at[1])
+    own_w.start()
+    met(n_ctx, n_wsh)
 
     part_rows = rows // 2
     tokens = [
@@ -544,7 +566,7 @@
     wline = Line(lambda s: w_c.at[pl.ds(pl.multiple_of(s * shard, 16), shard)], c, z, n_wsh, wz_send, wz_recv)
     for k in range(1, n_wsh):
         send(pack_ref, packs.at[z], pk_send.at[k], pk_recv.at[z], c, lax.rem(z + k, n_wsh))
-    wline.start(wqkv_ref)
+    wline.start(w_own)
     scale_acc[...] = jnp.zeros_like(scale_acc)
 
     def columns(b):
@@ -905,7 +927,6 @@
             gu[:, at] = (da * sig * (1.0 + up * (1.0 - sig))).astype(bf16)
 
         tiles(hidden)
-        weight_gradient(DOWN, turned, cot)
 
         def back(at):
             dh[:, at] = lax.dot_general(
@@ -943,9 +964,10 @@
             g = lax.rem(c + k, n_ctx)
             send(heads_of(go_stage, g), go_land.at[c], go_send.at[k], go_recv.at[c], g, z)
         pltpu.make_async_copy(my_heads(go_stage), go_land.at[c], local_sem.at[5]).start()
-        deep_pair_sum(DOWN)
+        weight_gradient(DOWN, turned, cot)
         turn(h2, turned)
         weight_gradient(UP, turned, gu)
+        deep_pair_sum(DOWN)
         weight_gradient(OUT, ob_land, ga)
         pair_sum(UP)
 
@@ -1081,28 +1103,17 @@
         head_gradients(0, ((6, lambda: first_sum(UP)),))
         head_windows(0)
         head_gradients(1, (
-            (1, lambda: second_sum(UP)), (2, lambda: deep_near_sum(DOWN)), (4, lambda: first_sum(OUT)),
-            (5, lambda: near_sum(UP)), (6, lambda: near_window(0)), (7, lambda: second_sum(OUT)),
+            (1, lambda: second_sum(UP)), (4, lambda: deep_near_sum(DOWN)), (5, lambda: first_sum(OUT)),
+            (6, lambda: near_sum(UP)), (6, lambda: near_window(0)), (7, lambda: second_sum(OUT)),
         ))
 
         def partial(b):
             lanes = pl.ds(pl.multiple_of(b * rows, 128), rows)
             part(b)[...] = jnp.dot(w_c[...], dqkv[:, lanes], preferred_element_type=f32).astype(bf16)
 
-        def to_sib(i, _):
-            b = 2 * i + (1 - core)
+        def to_sib(b):
             partial(b)
-            send(part(b), part_p(i), hp_send.at[i], hp_recv.at[i], sib, z)
-            return 0
-
-        lax.fori_loop(0, n_ctx // 2, to_sib, 0)
-        head_windows(1)
-
-        def own_core(i, _):
-            partial(2 * i + core)
-            return 0
-
-        lax.fori_loop(0, n_ctx // 2, own_core, 0)
+            send(part(b), part_p(b // 2), hp_send.at[b // 2], hp_recv.at[b // 2], sib, z)
 
         def scale_row():
             scale_sum = jnp.sum(scale_acc[...], axis=1, keepdims=True)
@@ -1117,8 +1128,18 @@
                 slot = s_bit if i == 0 else 1 - s_bit
                 send(part(b), part_f(slot), hf_send.at[i], hf_recv.at[slot], first, z)
 
+        shift = sib - c
+        to_sib(diag + shift)
+        to_sib(second + shift)
+        partial(diag)
+        to_sib(first + shift)
         pair(1, diag)
+        partial(first)
+        to_sib(sib)
         pair(0, first)
+        partial(second)
+        partial(c)
+        head_windows(1)
         deep_far_sum(DOWN)
         far_sum(UP)
         near_sum(OUT)
@@ -1231,7 +1252,7 @@
         vm((heads, length, 128), f32), vm((heads, length, 128), f32), vm((w_c.shape[1], length), bf16),
     )
 
-    wline.finish(wqkv_ref)
+    wline.finish(w_own)
     for k in range(1, n_wsh):
         left(pack_ref, pk_send.at[k], pk_recv.at[z], c, z)
         left(vec, vl_send.at[k], vl_recv.at[0], c, z)
@@ -1255,7 +1276,7 @@
         left(win_far.at[h], wf_send.at[h], wf_recv.at[h], c, z)
 
 
-def whole_call(dims, tok, cot, wqkv, w3, pack, order, lengths):
+def whole_call(dims, tok, cot, w6, pack, order, lengths):
     n_ctx, n_wsh, hd, heads = dims
     rows, width = tok.shape
     span, length, shard = hd * heads, rows * n_ctx, width // n_wsh
@@ -1267,6 +1288,7 @@
     dma = pltpu.SemaphoreType.DMA
     vm = pltpu.VMEM
     size = windows(width, n_wsh)[1]
+    lanes = -(-3 * span // 128) * 128
     wide = (rows, width)
     outs = (
         shape(wide, bf16), shape(wide, bf16),
@@ -1274,7 +1296,7 @@
     )
     scratch = [
         vm((n_ctx, rows, width), bf16), vm((3, width, width), bf16), vm((length, width), bf16),
-        vm((width, wqkv.shape[1]), bf16), vm((n_wsh,) + pack.shape, f32), vm((8, width), f32),
+        vm((width, lanes), bf16), vm((shard, lanes), bf16), vm((n_wsh,) + pack.shape, f32), vm((8, width), f32),
         vm((heads, length, 128), bf16), vm((heads, length, 128), bf16), vm((heads, hd, length), bf16),
         vm((n_ctx, heads, 128, rows), bf16), vm((n_ctx, span, rows), f32), vm((n_ctx, span, rows), f32),
         vm((n_ctx, span, rows), bf16), vm((width, rows), bf16), vm((width, rows), bf16), vm((n_ctx, span, rows), bf16),
@@ -1294,18 +1316,18 @@
         dma((n_ctx // 2,)), dma((n_ctx // 2,)), dma((2,)), dma((2,)), dma((1,)), dma((1,)),
         dma((heads, 2)), dma((heads, 2)), dma((heads,)), dma((heads,)), dma((heads, 7)), dma((heads, n_ctx)),
         dma((n_ctx,)), dma((n_ctx,)), dma((n_wsh,)), dma((n_wsh,)),
-        dma((n_ctx,)), dma((n_ctx,)), dma((n_wsh,)), dma((n_wsh,)), dma((13,)), dma((heads + 3,)),
+        dma((n_ctx,)), dma((n_ctx,)), dma((n_wsh,)), dma((n_wsh,)), dma((13,)), dma((heads + 3,)), dma((3, 2)),
     ]
     return pl.pallas_call(
         functools.partial(whole_kernel, dims),
         out_shape=outs,
-        in_specs=[hbm] * 7 + [smem] * 2,
+        in_specs=[hbm] * 9 + [smem] * 2,
         out_specs=[hbm] * len(outs),
         scratch_shapes=scratch,
         compiler_params=pltpu.CompilerParams(
             collective_id=0, has_side_effects=True, vmem_limit_bytes=VMEM_BYTES
         ),
-    )(tok, cot, wqkv, *w3, pack, order, lengths)
+    )(tok, cot, *w6, pack, order, lengths)
 
 
 def finish_kernel(dims, dwqkv_ref, dw3_ref, *refs):
@@ -1326,15 +1348,15 @@
         copy.start()
     done = []
 
-    def store(i):
-        copy = pltpu.make_async_copy(results.at[i], outs[i], out_sem.at[i])
+    def store(i, result):
+        copy = pltpu.make_async_copy(result, outs[i], out_sem.at[i])
         copy.start()
         done.append(copy)
 
     for w in range(3):
         ins[w].wait()
-        results[3 + w] = plain[w].astype(f32)
-        store(3 + w)
+        results[w] = plain[w].astype(f32)
+        store(3 + w, results.at[w])
     for i in range(3):
         ins[3 + i].wait()
 
@@ -1348,12 +1370,11 @@
 
         def turn(j, _):
             at = pl.ds(pl.multiple_of(j * 128, 128), 128)
-            turned[:, at] = wide[at, :].T
+            turned[i, :, at] = wide[at, :].T
             return 0
 
         lax.fori_loop(0, width // 128, turn, 0)
-        results[i] = turned[pl.ds(pl.multiple_of(offset, 8), shard), :]
-        store(i)
+        store(i, turned.at[i, pl.ds(pl.multiple_of(offset, 8), shard)])
     for copy in done:
         copy.wait()
 
@@ -1372,7 +1393,7 @@
         out_specs=[hbm] * 6,
         scratch_shapes=[
             pltpu.VMEM((3, n_ctx, heads, hd, size), bf16), pltpu.VMEM((3, shard, width), bf16),
-            pltpu.VMEM((width, size), f32), pltpu.VMEM((size, width), f32), pltpu.VMEM((6, shard, width), f32),
+            pltpu.VMEM((width, size), f32), pltpu.VMEM((3, size, width), f32), pltpu.VMEM((3, shard, width), f32),
             dma((6,)), dma((6,)),
         ],
         compiler_params=pltpu.CompilerParams(vmem_limit_bytes=VMEM_BYTES),
@@ -1385,22 +1406,18 @@
 ):
     f32 = jnp.float32
     n_ctx, n_wsh = lax.axis_size("ctx"), lax.axis_size("wsh")
-    c, z = lax.axis_index("ctx"), lax.axis_index("wsh")
+    z = lax.axis_index("wsh")
     width = tokens.shape[2]
     hd, heads = width // H, H // n_ctx
-    span, shard = hd * heads, width // n_wsh
+    shard = width // n_wsh
     dims = (n_ctx, n_wsh, hd, heads)
-    mine = [lax.dynamic_slice_in_dim(w, c * span, span, 1) for w in (w_query, w_key, w_value)]
-    mine = [w[:, h * hd : (h + 1) * hd] for h in range(heads) for w in mine]
-    lanes = -(-3 * span // 128) * 128
-    wqkv = jnp.pad(jnp.concatenate(mine, 1), ((0, 0), (0, lanes - 3 * span)))
     lanes = -(-shard // 128) * 128
     pack = sum(
         jnp.pad(v.astype(f32)[None], ((i, 7 - i), (0, lanes - v.shape[0])))
         for i, v in enumerate((gain_attn, gain_mlp, query_scale))
     )
     outputs, gtok, dw3, dwqkv, sums = whole_call(
-        dims, tokens[0], cotangent[0], wqkv, (w_out, w_up, w_down), pack, group_order, block_lengths
+        dims, tokens[0], cotangent[0], (w_query, w_key, w_value, w_out, w_up, w_down), pack, group_order, block_lengths
     )[:5]
     weight_grads = finish_call(dims, dwqkv, dw3)
     own = [lax.dynamic_slice_in_dim(sums[i], z * shard, shard, 0) for i in (0, 1)]

time: 215 us -> 206 us (0.958)
  Pallas kernels: 203 us -> 198 us
  local copies, waits for them, and re-layouts: 9.2 us -> 5.09 us
    pallas_call x1, Pallas kernels: 195 us -> 190 us  [whole_call(): pl.pallas_call(functools.partial(whole_kernel, dims), out_shape=outs, in_...]
    slice x2 -> x0, local copies, waits for them, and re-layouts: 2.44 us -> none  [head_split(): mine = [w[:, h * hd:(h + 1) * hd] for h in range(heads) for w in mine]]
where the time goes in v5:
time: 206 us
  Pallas kernels  198 us (96%)
  local copies, waits for them, and re-layouts  5.09 us (2%)
    pallas_call x1, Pallas kernels, whole_call(): pl.pallas_call(functools.partial(whole_kernel, dims), out_shape=outs, in_...  190 us
    pallas_call x1, Pallas kernels, finish_call(): pl.pallas_call(functools.partial(finish_kernel, dims), out_shape=(jax.Sha...  7.76 us

profile of v5, /device:TPU:0, one launch (start us, length us, event | category | flops | bytes accessed | tf_op | source)
XLA Modules:
  0.0 205.8 jit_solution(17484091016176380943)
XLA Ops:
  0.6 0.7 convert_bitcast_fusion
  1.3 0.7 broadcast_in_dim.11
  2.0 0.7 broadcast_in_dim.12
  2.7 0.6 pad_add_fusion.pack_ref
  3.3 0.0 copy-start.2
  3.3 190.4 %shard_map.212 = (bf16[256,1280]{1,0:T(8,128)(2,1)}, bf16[256,1280]{1,0:T(8,128)(2,1)}, bf16[3,320,1280]{2,1,0:T(8,128)(2,1)}, bf16[8,2,240,384]{3,2,1,0:T(8,128)(2,1)}, f32[8,1280]{1,0:T(8,128)}) custom-call(bf16[256,1280]{1,0:T(8,128)(2,1)} %bitcast.10, bf16[256,1280]{1,0:T(8,128)(2,1)} %bitcast.11, bf16[320,1280]{1,0:T(8,128)(2,1)} %wq_ref.1, ...), custom_call_target="tpu_custom_call" | custom-call | tf_op jit(solution)/shard_map/pallas_call | solution.py:1321
  193.7 0.9 fusion.2
  194.6 0.0 copy-done.2
  194.6 0.6 divide_multiply_fusion
  195.2 0.7 dynamic-slice_reduce_fusion
  195.8 0.0 copy-start.1
  195.8 7.8 %shard_map.213 = (f32[320,1280]{1,0:T(8,128)}, f32[320,1280]{1,0:T(8,128)}, f32[320,1280]{1,0:T(8,128)}, f32[320,1280]{1,0:T(8,128)}, f32[320,1280]{1,0:T(8,128)}, /*index=5*/f32[320,1280]{1,0:T(8,128)}) custom-call(bf16[8,2,240,384]{3,2,1,0:T(8,128)(2,1)} %get-tuple-element.24.dwqkv_ref, bf16[3,320,1280]{2,1,0:T(8,128)(2,1)} %get-tuple-element.25.dw3_ref), custom_call_target="tpu_custom_call" | custom-call | tf_op jit(solution)/shard_map/pallas_call | solution.py:1389
  203.6 0.0 copy-start
  203.6 0.0 copy-done.1
  203.6 0.8 copy.26
  204.5 0.5 copy-done
  204.9 0.8 copy.27
Async XLA Ops:
  3.3 191.3 %copy-start.2 = (bf16[20]{0:T(256)(128)(2,1)S(1)}, bf16[20]{0:T(256)(128)(2,1)}, u32[]{:S(2)}) copy-start(bf16[20]{0:T(256)(128)(2,1)} %param.25) | copy-start | bytes 124
  195.8 7.8 %copy-start.1 = (bf16[256,1280]{1,0:T(8,128)(2,1)S(1)}, bf16[256,1280]{1,0:T(8,128)(2,1)}, u32[]{:S(2)}) copy-start(bf16[256,1280]{1,0:T(8,128)(2,1)} %get-tuple-element.22) | copy-start | bytes 1966084
  203.6 1.3 copy-start

commit v6 on v5

--- a/solution.py
+++ b/solution.py
@@ -506,7 +506,7 @@
     w3z_send, w3z_recv, w3p_send, w3p_recv,
     go_send, go_recv, p_send, p_recv, f_send, f_recv, s_send, s_recv, zn_send, zn_recv, zf_send, zf_recv, g_send, g_recv,
     hp_send, hp_recv, hf_send, hf_recv, hs_send, hs_recv, wn_send, wn_recv, wf_send, wf_recv, wg_send, wg_recv,
-    vp_send, vp_recv, vl_send, vl_recv, rp_send, rp_recv, rl_send, rl_recv, local_sem, load_sem, cols_sem,
+    vp_send, vp_recv, vl_send, vl_recv, rp_send, rp_recv, rl_send, rl_recv, sl_send, sl_recv, sx_send, sx_recv, local_sem, load_sem, cols_sem,
 ):
     n_ctx, n_wsh, hd, heads = dims
     f32, bf16 = jnp.float32, jnp.bfloat16
@@ -572,11 +572,31 @@
     def columns(b):
         return pl.ds(pl.multiple_of(lax.rem(b, 2) * half, 128), half)
 
+    straight = shard * 2 // 5
+    cuts = (cut, cut, (shard - straight) // (n_ctx // 2))
+
     def piece(w, s, b):
-        top = pl.multiple_of(s * shard + (b // 2) * cut, 16)
-        return w_full.at[w, pl.ds(top, cut), columns(b)]
-
-    my_piece = [ref.at[pl.ds(pl.multiple_of((c // 2) * cut, 16), cut), columns(c)] for ref in w3_refs]
+        top = pl.multiple_of(s * shard + (b // 2) * cuts[w], 16)
+        return w_full.at[w, pl.ds(top, cuts[w]), columns(b)]
+
+    def straight_rows(s, of_core):
+        top = s * shard + shard - straight + of_core * (straight // 2)
+        return w_full.at[DOWN, pl.ds(pl.multiple_of(top, 16), straight // 2)]
+
+    my_straight = wdown_ref.at[pl.ds(pl.multiple_of(shard - straight + core * (straight // 2), 16), straight // 2)]
+    straight_line = Line(lambda s: straight_rows(s, core), c, z, n_wsh, sl_send, sl_recv)
+
+    def to_other_core(s):
+        k = lax.rem(s - z + n_wsh, n_wsh)
+        send(straight_rows(s, core), straight_rows(s, core), sx_send.at[k], sx_recv.at[k], sib, z)
+
+    def go_straight(w, distance):
+        straight_line.forward(distance, to_other_core)
+
+
+    my_piece = [
+        ref.at[pl.ds(pl.multiple_of((c // 2) * cuts[w], 16), cuts[w]), columns(c)] for w, ref in enumerate(w3_refs)
+    ]
     lines = [
         Line(lambda s, w=w: piece(w, s, c), c, z, n_wsh, w3z_send.at[w], w3z_recv.at[w]) for w in range(3)
     ]
@@ -662,6 +682,7 @@
         spread(OUT, 1)
         wline.forward(2)
         lines[DOWN].start(my_piece[DOWN])
+        straight_line.start(my_straight)
         arrived(others[1])
         arrived(others[2])
         tokens[0].from_diag()
@@ -706,10 +727,10 @@
         keys = length // 2
         plan = (
             (0, spread, OUT, 3), (0, by_first, OUT, 1), (1, by_first, OUT, 2), (1, spread, UP, 2),
-            (2, by_second, OUT, 1), (2, by_second, OUT, 2), (3, spread, DOWN, 1), (3, by_first, OUT, 3),
+            (2, by_second, OUT, 1), (2, by_second, OUT, 2), (3, spread, DOWN, 1), (3, go_straight, DOWN, 1), (3, by_first, OUT, 3),
             (4, by_diag, OUT, 1), (4, spread, UP, 3), (5, by_second, OUT, 3), (5, by_first, UP, 1),
-            (6, spread, DOWN, 2), (6, by_diag, OUT, 2), (7, by_first, UP, 2), (8, by_diag, OUT, 3),
-            (8, by_second, UP, 1), (9, by_second, UP, 2), (9, spread, DOWN, 3), (10, by_first, UP, 3),
+            (6, spread, DOWN, 2), (6, go_straight, DOWN, 2), (6, by_diag, OUT, 2), (7, by_first, UP, 2), (8, by_diag, OUT, 3),
+            (8, by_second, UP, 1), (9, by_second, UP, 2), (9, spread, DOWN, 3), (9, go_straight, DOWN, 3), (10, by_first, UP, 3),
             (11, by_diag, UP, 1), (11, by_first, DOWN, 1), (12, by_second, UP, 3), (12, by_diag, UP, 2),
             (13, by_first, DOWN, 2), (14, by_second, DOWN, 1), (14, by_diag, UP, 3), (15, by_second, DOWN, 2),
         )
@@ -913,6 +934,9 @@
         own_cot.wait()
         for distance in range(1, n_wsh):
             shards_at(DOWN, distance, all_others)
+        for k in range(1, n_wsh):
+            s = lax.rem(z + k, n_wsh)
+            arrive(straight_rows(s, 1 - core), sx_send.at[0], sx_recv.at[k], c, z)
         own_full[DOWN].wait()
 
         def hidden(at):
@@ -956,6 +980,9 @@
             ).astype(bf16)
 
         tiles(back_out)
+        straight_line.finish(my_straight)
+        for k in range(1, n_wsh):
+            left(my_straight, sx_send.at[k], sx_recv.at[k], c, z)
         for w in range(3):
             lines[w].finish(my_piece[w])
             for distance in range(1, n_wsh):
@@ -1316,7 +1343,8 @@
         dma((n_ctx // 2,)), dma((n_ctx // 2,)), dma((2,)), dma((2,)), dma((1,)), dma((1,)),
         dma((heads, 2)), dma((heads, 2)), dma((heads,)), dma((heads,)), dma((heads, 7)), dma((heads, n_ctx)),
         dma((n_ctx,)), dma((n_ctx,)), dma((n_wsh,)), dma((n_wsh,)),
-        dma((n_ctx,)), dma((n_ctx,)), dma((n_wsh,)), dma((n_wsh,)), dma((13,)), dma((heads + 3,)), dma((3, 2)),
+        dma((n_ctx,)), dma((n_ctx,)), dma((n_wsh,)), dma((n_wsh,)), dma((2 * n_wsh,)), dma((n_wsh,)), dma((n_wsh,)), dma((n_wsh,)),
+        dma((13,)), dma((heads + 3,)), dma((3, 2)),
     ]
     return pl.pallas_call(
         functools.partial(whole_kernel, dims),
@@ -1331,7 +1359,8 @@
 
 
 def finish_kernel(dims, dwqkv_ref, dw3_ref, *refs):
-    outs, (pieces, plain, wide, turned, results, in_sem, out_sem) = refs[:6], refs[6:]
+    tok_refs, outs, tok_outs = refs[:2], refs[2:8], refs[8:10]
+    pieces, plain, wide, turned, results, tok_buf, in_sem, out_sem = refs[10:]
     n_ctx, n_wsh, hd, heads = dims
     z = lax.axis_index("wsh")
     f32 = jnp.float32
@@ -1344,7 +1373,8 @@
     for i in range(3):
         at = pl.ds(i * hd, hd)
         ins.append(pltpu.make_async_copy(dwqkv_ref.at[:, :, at], pieces.at[i], in_sem.at[3 + i]))
-    for copy in ins:
+    tok_ins = [pltpu.make_async_copy(tok_refs[i], tok_buf.at[i], in_sem.at[6 + i]) for i in range(2)]
+    for copy in ins + tok_ins:
         copy.start()
     done = []
 
@@ -1375,11 +1405,16 @@
 
         lax.fori_loop(0, width // 128, turn, 0)
         store(i, turned.at[i, pl.ds(pl.multiple_of(offset, 8), shard)])
+    for i in range(2):
+        tok_ins[i].wait()
+        copy = pltpu.make_async_copy(tok_buf.at[i], tok_outs[i], out_sem.at[6 + i])
+        copy.start()
+        done.append(copy)
     for copy in done:
         copy.wait()
 
 
-def finish_call(dims, dwqkv, dw3):
+def finish_call(dims, dwqkv, dw3, outputs, gtok):
     n_ctx, n_wsh, hd, heads = dims
     shard, width = dw3.shape[1:]
     size = dwqkv.shape[3]
@@ -1388,16 +1423,16 @@
     dma = pltpu.SemaphoreType.DMA
     return pl.pallas_call(
         functools.partial(finish_kernel, dims),
-        out_shape=(jax.ShapeDtypeStruct((shard, width), f32),) * 6,
-        in_specs=[hbm] * 2,
-        out_specs=[hbm] * 6,
+        out_shape=(jax.ShapeDtypeStruct((shard, width), f32),) * 6 + (jax.ShapeDtypeStruct(gtok.shape, bf16),) * 2,
+        in_specs=[hbm] * 4,
+        out_specs=[hbm] * 8,
         scratch_shapes=[
             pltpu.VMEM((3, n_ctx, heads, hd, size), bf16), pltpu.VMEM((3, shard, width), bf16),
             pltpu.VMEM((width, size), f32), pltpu.VMEM((3, size, width), f32), pltpu.VMEM((3, shard, width), f32),
-            dma((6,)), dma((6,)),
+            pltpu.VMEM((2,) + gtok.shape, bf16), dma((8,)), dma((8,)),
         ],
         compiler_params=pltpu.CompilerParams(vmem_limit_bytes=VMEM_BYTES),
-    )(dwqkv, dw3)
+    )(dwqkv, dw3, outputs, gtok)
 
 
 def head_split(
@@ -1419,7 +1454,7 @@
     outputs, gtok, dw3, dwqkv, sums = whole_call(
         dims, tokens[0], cotangent[0], (w_query, w_key, w_value, w_out, w_up, w_down), pack, group_order, block_lengths
     )[:5]
-    weight_grads = finish_call(dims, dwqkv, dw3)
+    *weight_grads, outputs, gtok = finish_call(dims, dwqkv, dw3, outputs, gtok)
     own = [lax.dynamic_slice_in_dim(sums[i], z * shard, shard, 0) for i in (0, 1)]
     scale_grad = (
         lax.dynamic_slice_in_dim(sums[2], z * (hd // n_wsh), hd // n_wsh, 0)

time: 206 us -> 203 us (0.985)
  local copies, waits for them, and re-layouts: 5.09 us -> 2.94 us
    unnamed x8 -> x2, local copies, waits for them, and re-layouts: 2.15 us -> 0.01 us
where the time goes in v6:
time: 203 us
  Pallas kernels  197 us (97%)
  local copies, waits for them, and re-layouts  2.94 us (1%)
    pallas_call x1, Pallas kernels, whole_call(): pl.pallas_call(functools.partial(whole_kernel, dims), out_shape=outs, in_...  189 us
    pallas_call x1, Pallas kernels, finish_call(): pl.pallas_call(functools.partial(finish_kernel, dims), out_shape=(jax.Sha...  8.16 us

profile of v6, /device:TPU:0, one launch (start us, length us, event | category | flops | bytes accessed | tf_op | source)
XLA Modules:
  0.0 202.8 jit_solution(8424662660285622801)
XLA Ops:
  0.6 0.7 convert_bitcast_fusion
  1.3 0.7 broadcast_in_dim.11
  2.0 0.7 broadcast_in_dim.12
  2.7 0.6 pad_add_fusion.pack_ref
  3.3 0.0 copy-start
  3.3 189.0 %shard_map.212 = (bf16[256,1280]{1,0:T(8,128)(2,1)}, bf16[256,1280]{1,0:T(8,128)(2,1)}, bf16[3,320,1280]{2,1,0:T(8,128)(2,1)}, bf16[8,2,240,384]{3,2,1,0:T(8,128)(2,1)}, f32[8,1280]{1,0:T(8,128)}) custom-call(bf16[256,1280]{1,0:T(8,128)(2,1)} %bitcast.10, bf16[256,1280]{1,0:T(8,128)(2,1)} %bitcast.11, bf16[320,1280]{1,0:T(8,128)(2,1)} %wq_ref.1, ...), custom_call_target="tpu_custom_call" | custom-call | tf_op jit(solution)/shard_map/pallas_call | solution.py:1349
  192.2 0.9 fusion.2
  193.2 0.0 copy-done
  193.2 0.6 divide_multiply_fusion
  193.8 0.7 dynamic-slice_reduce_fusion
  194.4 8.2 %shard_map.213 = (f32[320,1280]{1,0:T(8,128)}, f32[320,1280]{1,0:T(8,128)}, f32[320,1280]{1,0:T(8,128)}, f32[320,1280]{1,0:T(8,128)}, f32[320,1280]{1,0:T(8,128)...) custom-call(bf16[8,2,240,384]{3,2,1,0:T(8,128)(2,1)} %get-tuple-element.24.dwqkv_ref, ...), custom_call_target="tpu_custom_call" | custom-call | tf_op jit(solution)/shard_map/pallas_call | solution.py:1424
Async XLA Ops:
  3.3 189.9 %copy-start = (bf16[20]{0:T(256)(128)(2,1)S(1)}, bf16[20]{0:T(256)(128)(2,1)}, u32[]{:S(2)}) copy-start(bf16[20]{0:T(256)(128)(2,1)} %param.25) | copy-start | bytes 124

commit v7 on v6

--- a/solution.py
+++ b/solution.py
@@ -572,7 +572,7 @@
     def columns(b):
         return pl.ds(pl.multiple_of(lax.rem(b, 2) * half, 128), half)
 
-    straight = shard * 2 // 5
+    straight = shard * 3 // 5
     cuts = (cut, cut, (shard - straight) // (n_ctx // 2))
 
     def piece(w, s, b):
@@ -682,7 +682,6 @@
         spread(OUT, 1)
         wline.forward(2)
         lines[DOWN].start(my_piece[DOWN])
-        straight_line.start(my_straight)
         arrived(others[1])
         arrived(others[2])
         tokens[0].from_diag()
@@ -692,6 +691,7 @@
         spread(OUT, 2)
         wline.forward(3)
         own_w.wait()
+        straight_line.start(my_straight)
         spread(UP, 1)
         gain_col = gain_column()
 

time: 203 us -> 201 us (level)
  no operation moved by 1% of the time
where the time goes in v7:
time: 201 us
  Pallas kernels  196 us (98%)
  local copies, waits for them, and re-layouts  2.94 us (1%)
    pallas_call x1, Pallas kernels, whole_call(): pl.pallas_call(functools.partial(whole_kernel, dims), out_shape=outs, in_...  187 us
    pallas_call x1, Pallas kernels, finish_call(): pl.pallas_call(functools.partial(finish_kernel, dims), out_shape=(jax.Sha...  8.16 us

profile of v7, /device:TPU:0, one launch (start us, length us, event | category | flops | bytes accessed | tf_op | source)
XLA Modules:
  0.0 201.2 jit_solution(4034811072333472523)
XLA Ops:
  0.6 0.7 convert_bitcast_fusion
  1.3 0.7 broadcast_in_dim.11
  2.0 0.7 broadcast_in_dim.12
  2.7 0.6 pad_add_fusion.pack_ref
  3.3 0.0 copy-start
  3.3 187.4 %shard_map.212 = (bf16[256,1280]{1,0:T(8,128)(2,1)}, bf16[256,1280]{1,0:T(8,128)(2,1)}, bf16[3,320,1280]{2,1,0:T(8,128)(2,1)}, bf16[8,2,240,384]{3,2,1,0:T(8,128)(2,1)}, f32[8,1280]{1,0:T(8,128)}) custom-call(bf16[256,1280]{1,0:T(8,128)(2,1)} %bitcast.10, bf16[256,1280]{1,0:T(8,128)(2,1)} %bitcast.11, bf16[320,1280]{1,0:T(8,128)(2,1)} %wq_ref.1, ...), custom_call_target="tpu_custom_call" | custom-call | tf_op jit(solution)/shard_map/pallas_call | solution.py:1349
  190.7 0.9 fusion.2
  191.6 0.0 copy-done
  191.6 0.6 divide_multiply_fusion
  192.2 0.7 dynamic-slice_reduce_fusion
  192.8 8.2 %shard_map.213 = (f32[320,1280]{1,0:T(8,128)}, f32[320,1280]{1,0:T(8,128)}, f32[320,1280]{1,0:T(8,128)}, f32[320,1280]{1,0:T(8,128)}, f32[320,1280]{1,0:T(8,128)...) custom-call(bf16[8,2,240,384]{3,2,1,0:T(8,128)(2,1)} %get-tuple-element.24.dwqkv_ref, ...), custom_call_target="tpu_custom_call" | custom-call | tf_op jit(solution)/shard_map/pallas_call | solution.py:1424
Async XLA Ops:
  3.3 188.3 %copy-start = (bf16[20]{0:T(256)(128)(2,1)S(1)}, bf16[20]{0:T(256)(128)(2,1)}, u32[]{:S(2)}) copy-start(bf16[20]{0:T(256)(128)(2,1)} %param.25) | copy-start | bytes 124
